TPU v7x, 512 devices: a whole 4x4x16 slice. The times are simulated.
512 devices in a mesh: space: 64 (over z, y), rep: 8 (over x, core).
Axes of the slice: x: 4, y: 4, z: 16, core: 2. Of those that a mesh axis runs over, the one named last changes fastest.
Arguments:
- feats: bfloat16 [512, 96, 512], P(('space', 'rep')), may hold values from -6 to 6
- cotangent: bfloat16 [512, 96, 512], P(('space', 'rep')), may hold values from -6 to 6
- occupancy: int32 [512, 512], P(('space', 'rep')), may hold values 0 or 1
- counts: int32 [512, 1], P(('space', 'rep')), may hold values from 1 to 1, as said below
- adjacency: int32 [512, 27], P(('space', 'rep')), may hold values from -1 to 511, as said below
- w_first: bfloat16 [96, 2592], replicated, may hold values from -0.125 to 0.125
- w_second: bfloat16 [96, 2592], replicated, may hold values from -0.125 to 0.125
Outputs:
- out_feats: bfloat16 [512, 96, 512], P(('space', 'rep'))
- grad_feats: bfloat16 [512, 96, 512], P(('space', 'rep'))
- grad_first: float32 [96, 2592], replicated
- grad_second: float32 [96, 2592], replicated
Inputs may be any that keep to these rules, and one draw needn't show every extreme that they name: `counts`: the live slots of a device are its slots 0 to count - 1; some device has 1 live slots. `adjacency`: each device owns a region of 2 x 2 x 2 block sites of a map two sites high; the owners' regions form a square grid in which space index s sits at column s % q and row s // q, q * q being the size of the space axis. Entry k of a live block's row is the live block at the site moved by (k // 9 - 1, k // 3 % 3 - 1, k % 3 - 1), or -1 where no live block is there; entry 13 is the block itself. Rows of dead slots are -1. A named block has the same rep index, and its owner is the device itself or one of the at most eight owners beside it in the grid.
All inputs are finite; a program needn't handle non-finite values. No bound on the sum of `occupancy` on one device may be relied on, other than what follows from the above.
Results may differ from a plain program's by a relative error of at most 0.0029.
Values may be sent and summed in bfloat16 or wider, within the bound.
No kernel may reach another device: no remote copies, remote signals or barrier semaphores. Data moves between devices by JAX's collectives and lax.ppermute only.
A program may use at most 64 MiB of HBM per device.

v0:
```python
import math

import jax
import jax.numpy as jnp
from jax import lax
from jax.sharding import PartitionSpec as P

BE = 8


OFFSETS = [(ax_a, ax_b, ax_c) for ax_a in (-1, 0, 1) for ax_b in (-1, 0, 1) for ax_c in (-1, 0, 1)]
DIRECTIONS = [(-1, -1), (0, -1), (1, -1), (-1, 0), (1, 0), (-1, 1), (0, 1), (1, 1)]


def from_behind(value, axis, steps):
    count = lax.axis_size(axis)
    initial, last = (max(0, -steps), min(count, count - steps))
    return lax.ppermute(value, axis, [(source, source + steps) for source in range(initial, last)])


def padded_field(gathered):
    planes = []
    for shift_x in (-1, 0, 1):
        row_list = []
        for shift_y in (-1, 0, 1):
            cell_list = []
            for shift_z in (-1, 0, 1):
                offset_id = (shift_x + 1) * 9 + (shift_y + 1) * 3 + (shift_z + 1)
                cell_list.append(gathered[offset_id])
            row_list.append(jnp.concatenate(cell_list, axis=3))
        planes.append(jnp.concatenate(row_list, axis=2))
    return jnp.concatenate(planes, axis=1)


def columns(padded, cube_edge):
    channels = padded.shape[0]
    stacked = []
    for shift_x, shift_y, shift_z in OFFSETS:
        window = padded[
            :,
            1 + shift_x : 1 + shift_x + cube_edge,
            1 + shift_y : 1 + shift_y + cube_edge,
            1 + shift_z : 1 + shift_z + cube_edge,
        ]
        stacked.append(window.reshape(channels, cube_edge**3))
    return jnp.concatenate(stacked, axis=0)


def flipped(weight):
    channels = weight.shape[0]
    turned = weight.reshape(channels, 27, channels)[:, ::-1, :]
    return jnp.transpose(turned, (2, 1, 0)).reshape(channels, 27 * channels)


def rim_piece(sources, index, shift_x, shift_y, shift_z, cube_edge):
    channels = sources.shape[1]
    starts = [index, jnp.int32(0)]
    extents = [1, channels]
    for shift_now in (shift_x, shift_y, shift_z):
        if shift_now < 0:
            starts.append(jnp.int32(cube_edge - 1))
            extents.append(1)
        elif shift_now > 0:
            starts.append(jnp.int32(0))
            extents.append(1)
        else:
            starts.append(jnp.int32(0))
            extents.append(cube_edge)
    return lax.dynamic_slice(sources, starts, extents)[0]


def body(feats, cotangent, occupancy, counts, adjacency, w_first, w_second):
    blocks, channels, volume = feats.shape
    cube_edge = BE
    space_count = lax.axis_size("space")
    rep_count = lax.axis_size("rep")
    grid_side = math.isqrt(space_count)
    own_index = lax.axis_index("space")
    slot_ids = jnp.arange(blocks, dtype=jnp.int32)
    live_slots = slot_ids < counts[0, 0]
    voxel_mask = ((occupancy != 0) & live_slots[:, None]).astype(jnp.float32)
    mask_half = voxel_mask.astype(jnp.bfloat16)
    mask_wide = voxel_mask[:, None, :]
    owner_index = jnp.where(adjacency >= 0, adjacency // (rep_count * blocks), -1)
    slot_index = jnp.where(adjacency >= 0, adjacency % blocks, 0)
    relative = owner_index - own_index
    source = jnp.full(adjacency.shape, 9 * blocks, jnp.int32)
    source = jnp.where(relative == 0, slot_index, source)
    for number, (step_x, step_y) in enumerate(DIRECTIONS):
        source = jnp.where(
            relative == step_x + grid_side * step_y, (number + 1) * blocks + slot_index, source
        )
    source = jnp.where(adjacency < 0, 9 * blocks, source)

    def gather_near(field_data):
        blocks_cube = field_data.reshape(blocks, channels, cube_edge, cube_edge, cube_edge)
        received = {}
        for step_x, step_y in DIRECTIONS:
            received[step_x, step_y] = from_behind(
                blocks_cube, "space", -(step_x + grid_side * step_y)
            )
        pieces_list = [blocks_cube]
        for step_x, step_y in DIRECTIONS:
            pieces_list.append(received[step_x, step_y])
        pieces_list.append(jnp.zeros((1, channels, cube_edge, cube_edge, cube_edge), jnp.bfloat16))
        return jnp.concatenate(pieces_list, axis=0)

    def slot_columns(sources, slot_id):
        pieces = []
        for offset_id, (shift_x, shift_y, shift_z) in enumerate(OFFSETS):
            pieces.append(
                rim_piece(sources, source[slot_id, offset_id], shift_x, shift_y, shift_z, cube_edge)
            )
        return columns(padded_field(pieces), cube_edge)

    def convolve(sources, weight):
        slot_id = 0

        def convolve_compute_block(slot_id=slot_id):
            return jnp.dot(
                weight, slot_columns(sources, slot_id), preferred_element_type=jnp.float32
            )

        result_block = convolve_compute_block()
        results = [result_block]
        return jnp.stack(results, axis=0)

    def weight_term(sources, gradient):
        slot_id = 0

        def weight_compute_block(slot_id=slot_id):
            return lax.dot_general(
                gradient[slot_id],
                slot_columns(sources, slot_id),
                (((1,), (1,)), ((), ())),
                preferred_element_type=jnp.float32,
            )

        result_sum = weight_compute_block()
        return result_sum

    masked = feats * mask_half[:, None, :]
    near_masked = gather_near(masked)
    pre_first = convolve(near_masked, w_first)
    hidden = (jax.nn.silu(pre_first) * mask_wide).astype(jnp.bfloat16)
    near_hidden = gather_near(hidden)
    pre_second = convolve(near_hidden, w_second)
    out_feats = (masked.astype(jnp.float32) + pre_second * mask_wide).astype(jnp.bfloat16)
    grad_two = cotangent * mask_half[:, None, :]
    near_two = gather_near(grad_two)
    back_two = convolve(near_two, flipped(w_second))
    sigmoid_first = jax.nn.sigmoid(pre_first)
    grad_one = (
        back_two * mask_wide * sigmoid_first * (1.0 + pre_first * (1.0 - sigmoid_first))
    ).astype(jnp.bfloat16)
    near_one = gather_near(grad_one)
    back_one = convolve(near_one, flipped(w_first))
    grad_feats = (mask_wide * (cotangent.astype(jnp.float32) + back_one)).astype(jnp.bfloat16)
    scaling = 1.0 / math.sqrt(blocks * space_count * rep_count * volume)
    local_first = weight_term(near_masked, grad_one) * scaling
    local_second = weight_term(near_hidden, grad_two) * scaling
    grad_first, grad_second = lax.psum((local_first, local_second), ("space", "rep"))
    return (out_feats, grad_feats, grad_first, grad_second)


def solution(mesh):
    in_specs = (
        P(("space", "rep"), None, None),
        P(("space", "rep"), None, None),
        P(("space", "rep"), None),
        P(("space", "rep"), None),
        P(("space", "rep"), None),
        P(),
        P(),
    )
    out_specs = (P(("space", "rep"), None, None), P(("space", "rep"), None, None), P(), P())
    return jax.shard_map(body, mesh=mesh, in_specs=in_specs, out_specs=out_specs, check_vma=False)
```

profile of v0, /device:TPU:1, one launch (start us, length us, event | category | flops | bytes accessed | tf_op | source)
XLA Modules:
  0.0 830.1 jit_solution(10082956417399038917)
XLA Ops:
  14.9 9.9 %collective-permute-start = (bf16[1,96,8,8,8]{1,4,3,2,0:T(8,128)(2,1)S(1)}, bf16[1,96,8,8,8]{1,4,3,2,0:T(8,128)(2,1)}, u32[]{:S(2)}, u32[]{:S(2)}) collective-permute-start(bf16[1,96,8,8,8]{1,4,3,2,0:T(8,128)(2,1)S(1)} %bitcast.521), channel_id=1, source_target_pairs={{0,72},{8,80},{16,88},{24,96},{32,104},{40,112},{48,120},{56,128},... | collective-permute-start | bytes 294920 | tf_op jit(solution)/shard_map/ppermute | solution.py:18
  80.8 7.6 collective-permute-start.1
  90.4 9.2 %collective-permute-start.2 = (bf16[1,96,8,8,8]{1,4,3,2,0:T(8,128)(2,1)S(1)}, bf16[1,96,8,8,8]{1,4,3,2,0:T(8,128)(2,1)S(1)}, u32[]{:S(2)}, u32[]{:S(2)}) collective-permute-start(bf16[1,96,8,8,8]{1,4,3,2,0:T(8,128)(2,1)S(1)} %bitcast.524), channel_id=1, source_target_pairs={{0,56},{8,64},{16,72},{24,80},{32,88},{40,96},{48,104},{56,112},{6... | collective-permute-start | bytes 294920 | tf_op jit(solution)/shard_map/ppermute | solution.py:18
  99.7 1.9 collective-permute-done.2
  102.9 1.9 collective-permute-done.3
  112.8 12.9 %collective-permute-start.16 = (bf16[1,96,8,8,8]{1,4,3,2,0:T(8,128)(2,1)S(1)}, bf16[1,96,8,8,8]{1,4,3,2,0:T(8,128)(2,1)S(1)}, u32[]{:S(2)}, u32[]{:S(2)}) collective-permute-start(bf16[1,96,8,8,8]{1,4,3,2,0:T(8,128)(2,1)S(1)} %bitcast.531), channel_id=1, source_target_pairs={{0,72},{8,80},{16,88},{24,96},{32,104},{40,112},{48,120},{56,128},... | collective-permute-start | bytes 294920 | tf_op jit(solution)/shard_map/ppermute | solution.py:18
  125.8 1.8 collective-permute-done.16
  127.7 9.0 %collective-permute-start.17 = (bf16[1,96,8,8,8]{1,4,3,2,0:T(8,128)(2,1)S(1)}, bf16[1,96,8,8,8]{1,4,3,2,0:T(8,128)(2,1)S(1)}, u32[]{:S(2)}, u32[]{:S(2)}) collective-permute-start(bf16[1,96,8,8,8]{1,4,3,2,0:T(8,128)(2,1)S(1)} %bitcast.532), channel_id=1, source_target_pairs={{0,64},{8,72},{16,80},{24,88},{32,96},{40,104},{48,112},{56,120},{... | collective-permute-start | bytes 294920 | tf_op jit(solution)/shard_map/ppermute | solution.py:18
  136.7 1.9 collective-permute-done.17
  138.6 7.6 collective-permute-start.18
  146.2 1.9 collective-permute-done.18
  148.1 3.3 collective-permute-start.19
  151.4 1.9 collective-permute-done.19
  170.7 5.6 concatenate.371
  176.3 2.7 multiply_convert_fusion
  179.0 6.1 concatenate.411
  185.1 2.8 fusion.9
  194.8 13.6 %collective-permute-start.24 = (bf16[1,96,8,8,8]{1,4,3,2,0:T(8,128)(2,1)S(1)}, bf16[1,96,8,8,8]{1,4,3,2,0:T(8,128)(2,1)S(1)}, u32[]{:S(2)}, u32[]{:S(2)}) collective-permute-start(bf16[1,96,8,8,8]{1,4,3,2,0:T(8,128)(2,1)S(1)} %bitcast.548), channel_id=1, source_target_pairs={{0,72},{8,80},{16,88},{24,96},{32,104},{40,112},{48,120},{56,128},... | collective-permute-start | bytes 294920 | tf_op jit(solution)/shard_map/ppermute | solution.py:18
  210.3 9.1 %collective-permute-start.25 = (bf16[1,96,8,8,8]{1,4,3,2,0:T(8,128)(2,1)S(1)}, bf16[1,96,8,8,8]{1,4,3,2,0:T(8,128)(2,1)S(1)}, u32[]{:S(2)}, u32[]{:S(2)}) collective-permute-start(bf16[1,96,8,8,8]{1,4,3,2,0:T(8,128)(2,1)S(1)} %bitcast.550), channel_id=1, source_target_pairs={{0,64},{8,72},{16,80},{24,88},{32,96},{40,104},{48,112},{56,120},{... | collective-permute-start | bytes 294920 | tf_op jit(solution)/shard_map/ppermute | solution.py:18
  220.0 1.9 collective-permute-done.25
  221.9 8.7 %collective-permute-start.26 = (bf16[1,96,8,8,8]{1,4,3,2,0:T(8,128)(2,1)S(1)}, bf16[1,96,8,8,8]{1,4,3,2,0:T(8,128)(2,1)S(1)}, u32[]{:S(2)}, u32[]{:S(2)}) collective-permute-start(bf16[1,96,8,8,8]{1,4,3,2,0:T(8,128)(2,1)S(1)} %bitcast.551), channel_id=1, source_target_pairs={{0,56},{8,64},{16,72},{24,80},{32,88},{40,96},{48,104},{56,112},{6... | collective-permute-start | bytes 294920 | tf_op jit(solution)/shard_map/ppermute | solution.py:18
  232.6 4.6 collective-permute-start.27
  246.9 18.6 %collective-permute-start.8 = (bf16[1,96,8,8,8]{1,4,3,2,0:T(8,128)(2,1)S(1)}, bf16[1,96,8,8,8]{1,4,3,2,0:T(8,128)(2,1)S(1)}, u32[]{:S(2)}, u32[]{:S(2)}) collective-permute-start(bf16[1,96,8,8,8]{1,4,3,2,0:T(8,128)(2,1)S(1)} %bitcast.540), channel_id=1, source_target_pairs={{0,72},{8,80},{16,88},{24,96},{32,104},{40,112},{48,120},{56,128},... | collective-permute-start | bytes 294920 | tf_op jit(solution)/shard_map/ppermute | solution.py:18
  267.7 8.8 %collective-permute-start.9 = (bf16[1,96,8,8,8]{1,4,3,2,0:T(8,128)(2,1)S(1)}, bf16[1,96,8,8,8]{1,4,3,2,0:T(8,128)(2,1)S(1)}, u32[]{:S(2)}, u32[]{:S(2)}) collective-permute-start(bf16[1,96,8,8,8]{1,4,3,2,0:T(8,128)(2,1)S(1)} %bitcast.541), channel_id=1, source_target_pairs={{0,64},{8,72},{16,80},{24,88},{32,96},{40,104},{48,112},{56,120},{... | collective-permute-start | bytes 294920 | tf_op jit(solution)/shard_map/ppermute | solution.py:18
  277.6 1.7 collective-permute-done.9
  279.4 8.1 collective-permute-start.10
  289.4 4.8 collective-permute-start.11
  310.7 5.3 concatenate.391
  321.2 6.1 concatenate.431
  329.3 1.6 fusion.7
  330.9 489.0 %all-reduce.3.cloned.1.call-done = (f32[96,2592]{1,0:T(8,128)}, f32[96,2592]{1,0:T(8,128)}) async-done(((f32[96,2592]{1,0:T(8,128)}, f32[96,2592]{1,0:T(8,128)}), (f32[96,2592]{1,0:T(8,128)}, f32[96,2592]{1,0:T(8,128)})) %all-reduce.3.cloned.1.call-update) | async-done | bytes 1990672 | tf_op jit(solution)/shard_map/psum | solution.py:162
  819.9 2.3 copy.142
  (202 shorter events, 91.3 us)
Async XLA Ops:
  7.2 812.8 %all-reduce.3.cloned.1.call-start = ((), (), s32[]{:S(2)}) async-start(), calls=%async_computation | async-start | bytes 4128768 | tf_op jit(solution)/shard_map/psum | solution.py:162
  9.7 103.1 %collective-permute-start.7 = (bf16[1,96,8,8,8]{1,4,3,2,0:T(8,128)(2,1)S(1)}, bf16[1,96,8,8,8]{1,4,3,2,0:T(8,128)(2,1)S(1)}, u32[]{:S(2)}, u32[]{:S(2)}) collective-permute-start(bf16[1,96,8,8,8]{1,4,3,2,0:T(8,128)(2,1)S(1)} %bitcast.517), channel_id=1, source_target_pairs={{72,0},{80,8},{88,16},{96,24},{104,32},{112,40},{120,48},{128,56},... | collective-permute-start | bytes 294920 | tf_op jit(solution)/shard_map/ppermute | solution.py:18
  11.0 99.6 %collective-permute-start.6 = (bf16[1,96,8,8,8]{1,4,3,2,0:T(8,128)(2,1)S(1)}, bf16[1,96,8,8,8]{1,4,3,2,0:T(8,128)(2,1)}, u32[]{:S(2)}, u32[]{:S(2)}) collective-permute-start(bf16[1,96,8,8,8]{1,4,3,2,0:T(8,128)(2,1)S(1)} %bitcast.518), channel_id=1, source_target_pairs={{64,0},{72,8},{80,16},{88,24},{96,32},{104,40},{112,48},{120,56},{... | collective-permute-start | bytes 294920 | tf_op jit(solution)/shard_map/ppermute | solution.py:18
  12.3 96.0 %collective-permute-start.5 = (bf16[1,96,8,8,8]{1,4,3,2,0:T(8,128)(2,1)S(1)}, bf16[1,96,8,8,8]{1,4,3,2,0:T(8,128)(2,1)}, u32[]{:S(2)}, u32[]{:S(2)}) collective-permute-start(bf16[1,96,8,8,8]{1,4,3,2,0:T(8,128)(2,1)S(1)} %bitcast.519), channel_id=1, source_target_pairs={{56,0},{64,8},{72,16},{80,24},{88,32},{96,40},{104,48},{112,56},{1... | collective-permute-start | bytes 294920 | tf_op jit(solution)/shard_map/ppermute | solution.py:18
  13.6 92.5 %collective-permute-start.4 = (bf16[1,96,8,8,8]{1,4,3,2,0:T(8,128)(2,1)S(1)}, bf16[1,96,8,8,8]{1,4,3,2,0:T(8,128)(2,1)}, u32[]{:S(2)}, u32[]{:S(2)}) collective-permute-start(bf16[1,96,8,8,8]{1,4,3,2,0:T(8,128)(2,1)S(1)} %bitcast.520), channel_id=1, source_target_pairs={{8,0},{16,8},{24,16},{32,24},{40,32},{48,40},{56,48},{64,56},{72,6... | collective-permute-start | bytes 294920 | tf_op jit(solution)/shard_map/ppermute | solution.py:18
  14.9 65.9 %collective-permute-start = (bf16[1,96,8,8,8]{1,4,3,2,0:T(8,128)(2,1)S(1)}, bf16[1,96,8,8,8]{1,4,3,2,0:T(8,128)(2,1)}, u32[]{:S(2)}, u32[]{:S(2)}) collective-permute-start(bf16[1,96,8,8,8]{1,4,3,2,0:T(8,128)(2,1)S(1)} %bitcast.521), channel_id=1, source_target_pairs={{0,72},{8,80},{16,88},{24,96},{32,104},{40,112},{48,120},{56,128},... | collective-permute-start | bytes 294920 | tf_op jit(solution)/shard_map/ppermute | solution.py:18
  80.8 9.6 %collective-permute-start.1 = (bf16[1,96,8,8,8]{1,4,3,2,0:T(8,128)(2,1)S(1)}, bf16[1,96,8,8,8]{1,4,3,2,0:T(8,128)(2,1)S(1)}, u32[]{:S(2)}, u32[]{:S(2)}) collective-permute-start(bf16[1,96,8,8,8]{1,4,3,2,0:T(8,128)(2,1)S(1)} %bitcast.523), channel_id=1, source_target_pairs={{0,64},{8,72},{16,80},{24,88},{32,96},{40,104},{48,112},{56,120},{... | collective-permute-start | bytes 294920 | tf_op jit(solution)/shard_map/ppermute | solution.py:18
  90.4 11.2 %collective-permute-start.2 = (bf16[1,96,8,8,8]{1,4,3,2,0:T(8,128)(2,1)S(1)}, bf16[1,96,8,8,8]{1,4,3,2,0:T(8,128)(2,1)S(1)}, u32[]{:S(2)}, u32[]{:S(2)}) collective-permute-start(bf16[1,96,8,8,8]{1,4,3,2,0:T(8,128)(2,1)S(1)} %bitcast.524), channel_id=1, source_target_pairs={{0,56},{8,64},{16,72},{24,80},{32,88},{40,96},{48,104},{56,112},{6... | collective-permute-start | bytes 294920 | tf_op jit(solution)/shard_map/ppermute | solution.py:18
  104.8 48.7 %collective-permute-start.23 = (bf16[1,96,8,8,8]{1,4,3,2,0:T(8,128)(2,1)S(1)}, bf16[1,96,8,8,8]{1,4,3,2,0:T(8,128)(2,1)S(1)}, u32[]{:S(2)}, u32[]{:S(2)}) collective-permute-start(bf16[1,96,8,8,8]{1,4,3,2,0:T(8,128)(2,1)S(1)} %bitcast.527), channel_id=1, source_target_pairs={{72,0},{80,8},{88,16},{96,24},{104,32},{112,40},{120,48},{128,56},... | collective-permute-start | bytes 294920 | tf_op jit(solution)/shard_map/ppermute | solution.py:18
  106.1 47.3 %collective-permute-start.22 = (bf16[1,96,8,8,8]{1,4,3,2,0:T(8,128)(2,1)S(1)}, bf16[1,96,8,8,8]{1,4,3,2,0:T(8,128)(2,1)S(1)}, u32[]{:S(2)}, u32[]{:S(2)}) collective-permute-start(bf16[1,96,8,8,8]{1,4,3,2,0:T(8,128)(2,1)S(1)} %bitcast.528), channel_id=1, source_target_pairs={{64,0},{72,8},{80,16},{88,24},{96,32},{104,40},{112,48},{120,56},{... | collective-permute-start | bytes 294920 | tf_op jit(solution)/shard_map/ppermute | solution.py:18
  108.4 45.0 %collective-permute-start.21 = (bf16[1,96,8,8,8]{1,4,3,2,0:T(8,128)(2,1)S(1)}, bf16[1,96,8,8,8]{1,4,3,2,0:T(8,128)(2,1)S(1)}, u32[]{:S(2)}, u32[]{:S(2)}) collective-permute-start(bf16[1,96,8,8,8]{1,4,3,2,0:T(8,128)(2,1)S(1)} %bitcast.529), channel_id=1, source_target_pairs={{56,0},{64,8},{72,16},{80,24},{88,32},{96,40},{104,48},{112,56},{1... | collective-permute-start | bytes 294920 | tf_op jit(solution)/shard_map/ppermute | solution.py:18
  110.6 42.8 %collective-permute-start.20 = (bf16[1,96,8,8,8]{1,4,3,2,0:T(8,128)(2,1)S(1)}, bf16[1,96,8,8,8]{1,4,3,2,0:T(8,128)(2,1)S(1)}, u32[]{:S(2)}, u32[]{:S(2)}) collective-permute-start(bf16[1,96,8,8,8]{1,4,3,2,0:T(8,128)(2,1)S(1)} %bitcast.530), channel_id=1, source_target_pairs={{8,0},{16,8},{24,16},{32,24},{40,32},{48,40},{56,48},{64,56},{72,6... | collective-permute-start | bytes 294920 | tf_op jit(solution)/shard_map/ppermute | solution.py:18
  112.8 14.9 %collective-permute-start.16 = (bf16[1,96,8,8,8]{1,4,3,2,0:T(8,128)(2,1)S(1)}, bf16[1,96,8,8,8]{1,4,3,2,0:T(8,128)(2,1)S(1)}, u32[]{:S(2)}, u32[]{:S(2)}) collective-permute-start(bf16[1,96,8,8,8]{1,4,3,2,0:T(8,128)(2,1)S(1)} %bitcast.531), channel_id=1, source_target_pairs={{0,72},{8,80},{16,88},{24,96},{32,104},{40,112},{48,120},{56,128},... | collective-permute-start | bytes 294920 | tf_op jit(solution)/shard_map/ppermute | solution.py:18
  127.7 10.9 %collective-permute-start.17 = (bf16[1,96,8,8,8]{1,4,3,2,0:T(8,128)(2,1)S(1)}, bf16[1,96,8,8,8]{1,4,3,2,0:T(8,128)(2,1)S(1)}, u32[]{:S(2)}, u32[]{:S(2)}) collective-permute-start(bf16[1,96,8,8,8]{1,4,3,2,0:T(8,128)(2,1)S(1)} %bitcast.532), channel_id=1, source_target_pairs={{0,64},{8,72},{16,80},{24,88},{32,96},{40,104},{48,112},{56,120},{... | collective-permute-start | bytes 294920 | tf_op jit(solution)/shard_map/ppermute | solution.py:18
  138.6 9.5 %collective-permute-start.18 = (bf16[1,96,8,8,8]{1,4,3,2,0:T(8,128)(2,1)S(1)}, bf16[1,96,8,8,8]{1,4,3,2,0:T(8,128)(2,1)S(1)}, u32[]{:S(2)}, u32[]{:S(2)}) collective-permute-start(bf16[1,96,8,8,8]{1,4,3,2,0:T(8,128)(2,1)S(1)} %bitcast.533), channel_id=1, source_target_pairs={{0,56},{8,64},{16,72},{24,80},{32,88},{40,96},{48,104},{56,112},{6... | collective-permute-start | bytes 294920 | tf_op jit(solution)/shard_map/ppermute | solution.py:18
  148.1 5.3 collective-permute-start.19
  189.6 57.3 %collective-permute-start.31 = (bf16[1,96,8,8,8]{1,4,3,2,0:T(8,128)(2,1)S(1)}, bf16[1,96,8,8,8]{1,4,3,2,0:T(8,128)(2,1)S(1)}, u32[]{:S(2)}, u32[]{:S(2)}) collective-permute-start(bf16[1,96,8,8,8]{1,4,3,2,0:T(8,128)(2,1)S(1)} %bitcast.544), channel_id=1, source_target_pairs={{72,0},{80,8},{88,16},{96,24},{104,32},{112,40},{120,48},{128,56},... | collective-permute-start | bytes 294920 | tf_op jit(solution)/shard_map/ppermute | solution.py:18
  190.9 54.1 %collective-permute-start.30 = (bf16[1,96,8,8,8]{1,4,3,2,0:T(8,128)(2,1)S(1)}, bf16[1,96,8,8,8]{1,4,3,2,0:T(8,128)(2,1)S(1)}, u32[]{:S(2)}, u32[]{:S(2)}) collective-permute-start(bf16[1,96,8,8,8]{1,4,3,2,0:T(8,128)(2,1)S(1)} %bitcast.545), channel_id=1, source_target_pairs={{64,0},{72,8},{80,16},{88,24},{96,32},{104,40},{112,48},{120,56},{... | collective-permute-start | bytes 294920 | tf_op jit(solution)/shard_map/ppermute | solution.py:18
  192.2 50.8 %collective-permute-start.29 = (bf16[1,96,8,8,8]{1,4,3,2,0:T(8,128)(2,1)S(1)}, bf16[1,96,8,8,8]{1,4,3,2,0:T(8,128)(2,1)S(1)}, u32[]{:S(2)}, u32[]{:S(2)}) collective-permute-start(bf16[1,96,8,8,8]{1,4,3,2,0:T(8,128)(2,1)S(1)} %bitcast.546), channel_id=1, source_target_pairs={{56,0},{64,8},{72,16},{80,24},{88,32},{96,40},{104,48},{112,56},{1... | collective-permute-start | bytes 294920 | tf_op jit(solution)/shard_map/ppermute | solution.py:18
  193.5 47.6 %collective-permute-start.28 = (bf16[1,96,8,8,8]{1,4,3,2,0:T(8,128)(2,1)S(1)}, bf16[1,96,8,8,8]{1,4,3,2,0:T(8,128)(2,1)S(1)}, u32[]{:S(2)}, u32[]{:S(2)}) collective-permute-start(bf16[1,96,8,8,8]{1,4,3,2,0:T(8,128)(2,1)S(1)} %bitcast.547), channel_id=1, source_target_pairs={{8,0},{16,8},{24,16},{32,24},{40,32},{48,40},{56,48},{64,56},{72,6... | collective-permute-start | bytes 294920 | tf_op jit(solution)/shard_map/ppermute | solution.py:18
  194.8 15.5 %collective-permute-start.24 = (bf16[1,96,8,8,8]{1,4,3,2,0:T(8,128)(2,1)S(1)}, bf16[1,96,8,8,8]{1,4,3,2,0:T(8,128)(2,1)S(1)}, u32[]{:S(2)}, u32[]{:S(2)}) collective-permute-start(bf16[1,96,8,8,8]{1,4,3,2,0:T(8,128)(2,1)S(1)} %bitcast.548), channel_id=1, source_target_pairs={{0,72},{8,80},{16,88},{24,96},{32,104},{40,112},{48,120},{56,128},... | collective-permute-start | bytes 294920 | tf_op jit(solution)/shard_map/ppermute | solution.py:18
  210.3 11.6 %collective-permute-start.25 = (bf16[1,96,8,8,8]{1,4,3,2,0:T(8,128)(2,1)S(1)}, bf16[1,96,8,8,8]{1,4,3,2,0:T(8,128)(2,1)S(1)}, u32[]{:S(2)}, u32[]{:S(2)}) collective-permute-start(bf16[1,96,8,8,8]{1,4,3,2,0:T(8,128)(2,1)S(1)} %bitcast.550), channel_id=1, source_target_pairs={{0,64},{8,72},{16,80},{24,88},{32,96},{40,104},{48,112},{56,120},{... | collective-permute-start | bytes 294920 | tf_op jit(solution)/shard_map/ppermute | solution.py:18
  221.9 10.7 %collective-permute-start.26 = (bf16[1,96,8,8,8]{1,4,3,2,0:T(8,128)(2,1)S(1)}, bf16[1,96,8,8,8]{1,4,3,2,0:T(8,128)(2,1)S(1)}, u32[]{:S(2)}, u32[]{:S(2)}) collective-permute-start(bf16[1,96,8,8,8]{1,4,3,2,0:T(8,128)(2,1)S(1)} %bitcast.551), channel_id=1, source_target_pairs={{0,56},{8,64},{16,72},{24,80},{32,88},{40,96},{48,104},{56,112},{6... | collective-permute-start | bytes 294920 | tf_op jit(solution)/shard_map/ppermute | solution.py:18
  232.6 6.5 collective-permute-start.27
  239.1 61.5 %collective-permute-start.15 = (bf16[1,96,8,8,8]{1,4,3,2,0:T(8,128)(2,1)S(1)}, bf16[1,96,8,8,8]{1,4,3,2,0:T(8,128)(2,1)S(1)}, u32[]{:S(2)}, u32[]{:S(2)}) collective-permute-start(bf16[1,96,8,8,8]{1,4,3,2,0:T(8,128)(2,1)S(1)} %bitcast.536), channel_id=1, source_target_pairs={{72,0},{80,8},{88,16},{96,24},{104,32},{112,40},{120,48},{128,56},... | collective-permute-start | bytes 294920 | tf_op jit(solution)/shard_map/ppermute | solution.py:18
  241.1 58.1 %collective-permute-start.14 = (bf16[1,96,8,8,8]{1,4,3,2,0:T(8,128)(2,1)S(1)}, bf16[1,96,8,8,8]{1,4,3,2,0:T(8,128)(2,1)S(1)}, u32[]{:S(2)}, u32[]{:S(2)}) collective-permute-start(bf16[1,96,8,8,8]{1,4,3,2,0:T(8,128)(2,1)S(1)} %bitcast.537), channel_id=1, source_target_pairs={{64,0},{72,8},{80,16},{88,24},{96,32},{104,40},{112,48},{120,56},{... | collective-permute-start | bytes 294920 | tf_op jit(solution)/shard_map/ppermute | solution.py:18
  243.0 54.8 %collective-permute-start.13 = (bf16[1,96,8,8,8]{1,4,3,2,0:T(8,128)(2,1)S(1)}, bf16[1,96,8,8,8]{1,4,3,2,0:T(8,128)(2,1)S(1)}, u32[]{:S(2)}, u32[]{:S(2)}) collective-permute-start(bf16[1,96,8,8,8]{1,4,3,2,0:T(8,128)(2,1)S(1)} %bitcast.538), channel_id=1, source_target_pairs={{56,0},{64,8},{72,16},{80,24},{88,32},{96,40},{104,48},{112,56},{1... | collective-permute-start | bytes 294920 | tf_op jit(solution)/shard_map/ppermute | solution.py:18
  245.0 52.0 %collective-permute-start.12 = (bf16[1,96,8,8,8]{1,4,3,2,0:T(8,128)(2,1)S(1)}, bf16[1,96,8,8,8]{1,4,3,2,0:T(8,128)(2,1)S(1)}, u32[]{:S(2)}, u32[]{:S(2)}) collective-permute-start(bf16[1,96,8,8,8]{1,4,3,2,0:T(8,128)(2,1)S(1)} %bitcast.539), channel_id=1, source_target_pairs={{8,0},{16,8},{24,16},{32,24},{40,32},{48,40},{56,48},{64,56},{72,6... | collective-permute-start | bytes 294920 | tf_op jit(solution)/shard_map/ppermute | solution.py:18
  246.9 20.8 %collective-permute-start.8 = (bf16[1,96,8,8,8]{1,4,3,2,0:T(8,128)(2,1)S(1)}, bf16[1,96,8,8,8]{1,4,3,2,0:T(8,128)(2,1)S(1)}, u32[]{:S(2)}, u32[]{:S(2)}) collective-permute-start(bf16[1,96,8,8,8]{1,4,3,2,0:T(8,128)(2,1)S(1)} %bitcast.540), channel_id=1, source_target_pairs={{0,72},{8,80},{16,88},{24,96},{32,104},{40,112},{48,120},{56,128},... | collective-permute-start | bytes 294920 | tf_op jit(solution)/shard_map/ppermute | solution.py:18
  267.7 11.6 %collective-permute-start.9 = (bf16[1,96,8,8,8]{1,4,3,2,0:T(8,128)(2,1)S(1)}, bf16[1,96,8,8,8]{1,4,3,2,0:T(8,128)(2,1)S(1)}, u32[]{:S(2)}, u32[]{:S(2)}) collective-permute-start(bf16[1,96,8,8,8]{1,4,3,2,0:T(8,128)(2,1)S(1)} %bitcast.541), channel_id=1, source_target_pairs={{0,64},{8,72},{16,80},{24,88},{32,96},{40,104},{48,112},{56,120},{... | collective-permute-start | bytes 294920 | tf_op jit(solution)/shard_map/ppermute | solution.py:18
  279.4 10.0 %collective-permute-start.10 = (bf16[1,96,8,8,8]{1,4,3,2,0:T(8,128)(2,1)S(1)}, bf16[1,96,8,8,8]{1,4,3,2,0:T(8,128)(2,1)S(1)}, u32[]{:S(2)}, u32[]{:S(2)}) collective-permute-start(bf16[1,96,8,8,8]{1,4,3,2,0:T(8,128)(2,1)S(1)} %bitcast.542), channel_id=1, source_target_pairs={{0,56},{8,64},{16,72},{24,80},{32,88},{40,96},{48,104},{56,112},{6... | collective-permute-start | bytes 294920 | tf_op jit(solution)/shard_map/ppermute | solution.py:18
  289.4 6.8 collective-permute-start.11
  (20 other events, 244.5 us)
Sparse Core Ops, SparseCore 0:
  317.8 502.1 all-reduce.2
where the time goes:
time: 834 us; the launch traced here: 830 us
  waiting for transfers between devices  511 us (61%)
  starting transfers between devices  158 us (19%)
  local copies, waits for them, and re-layouts  75.2 us (9%)
  between operations  66.4 us (8%)
  matrix products  11.8 us (1%)
    psum x1, waiting for transfers between devices, body(): lax.psum((local_first, local_second), ('space', 'rep'))  489 us
    ppermute x32, starting transfers between devices, from_behind(): lax.ppermute(value, axis, [(source, source + steps) for source in range(i...  158 us
    concatenate x4, local copies, waits for them, and re-layouts, columns(): return jnp.concatenate(stacked, axis=0)  23.2 us
    ppermute x32, waiting for transfers between devices, from_behind(): lax.ppermute(value, axis, [(source, source + steps) for source in range(i...  21.9 us
  transfers between devices with their start and end apart: 33, of which 15 were waited for; matrix products, arithmetic and copies ran while one was open for 4% of the time, Pallas kernels for 0%

commit v1 on v0

v1 whole, which is shorter than its diff:
```python
import functools
import math

import jax
import jax.numpy as jnp
import numpy as np
from jax import lax
from jax.experimental import pallas as pl
from jax.experimental.pallas import tpu as pltpu
from jax.sharding import Mesh, PartitionSpec as P

C = 96
BE = 8
GRID = 8
REPS = 8
ROWS = 208
PAD = 12
LANES = 1920
OUTER = 1536
INNER = 1152
BASE = PAD * PAD + PAD
TILES_R, TILES_L = 24, 21
DIRECTIONS = [(-1, -1), (0, -1), (1, -1), (-1, 0), (1, 0), (-1, 1), (0, 1), (1, 1)]
CORNERS = [(-1, -1), (1, -1), (-1, 1), (1, 1)]
OFFSETS = [(a, b, c) for a in (-1, 0, 1) for b in (-1, 0, 1) for c in (-1, 0, 1)]
F32, BF16 = jnp.float32, jnp.bfloat16


def pack_matrix():
    picks = np.zeros((512, 384), np.float32)
    for half, first in ((0, 6), (1, 0)):
        for x in range(8):
            for y in range(2):
                for z in range(8):
                    picks[x * 64 + (first + y) * 8 + z, half * 128 + x * 16 + y * 8 + z] = 1
    for number, (sx, sy) in enumerate(CORNERS):
        for x in range(2):
            for y in range(2):
                for z in range(8):
                    row = (x + (6 if sx < 0 else 0)) * 64 + (y + (6 if sy < 0 else 0)) * 8 + z
                    picks[row, 256 + 32 * number + x * 16 + y * 8 + z] = 1
    return picks


def place_table():
    table = np.full((16, LANES), -1, np.int32)
    table[0] = 27
    for p in range(PAD**3):
        at = (p // (PAD * PAD) - 2, p // PAD % PAD - 2, p % PAD - 2)
        site = [(-1 if a < 0 else 1 if a >= BE else 0) for a in at]
        x, y, z = (a % BE for a in at)
        table[0, p] = (site[0] + 1) * 9 + (site[1] + 1) * 3 + site[2] + 1
        table[1, p] = x * 64 + y * 8 + z
        for number, (sx, sy) in enumerate(DIRECTIONS):
            nx = x - 6 if sx < 0 else x
            ny = y - 6 if sy < 0 else y
            if sx != 0 and not 0 <= nx < 2 or sy != 0 and not 0 <= ny < 2:
                continue
            if sy == 0:
                place = 512 + nx * 64 + y * 8 + z
            elif sx == 0:
                place = 640 + x * 16 + ny * 8 + z
            else:
                place = 768 + 32 * CORNERS.index((sx, sy)) + nx * 16 + ny * 8 + z
            table[2 + number, p] = place
    return table


def inner_table():
    marks = np.zeros((8, OUTER), np.float32)
    squeeze = np.zeros((INNER, 512), np.float32)
    for x in range(8):
        for y in range(8):
            for z in range(8):
                t = x * PAD * PAD + y * PAD + z
                marks[0, t + BASE + 1] = 1
                marks[1, t] = 1
                squeeze[t, x * 64 + y * 8 + z] = 1
    return marks, squeeze


def pack_kernel(feats, cot, occ, picks, field, *sends):
    mask = (occ[...] != 0).astype(F32).astype(BF16)
    field[0:C, :] = feats[0] * mask
    field[C : 2 * C, :] = cot[0] * mask
    field[2 * C :, :] = jnp.broadcast_to(mask, (ROWS - 2 * C, 512))
    whole = field[...]
    rims = jnp.dot(whole, picks[...], preferred_element_type=F32).astype(BF16)
    left, right, down, up, corners = sends
    left[...] = whole[:, 384:512]
    right[...] = whole[:, 0:128]
    down[...] = rims[:, 0:128]
    up[...] = rims[:, 128:256]
    corners[...] = rims[:, 256:384]


def shifted_columns(source, columns, length):
    for number in range(9):
        start = (number // 3) * PAD * PAD + (number % 3) * PAD
        columns[number * C : (number + 1) * C, 0:length] = source[:, start : start + length]


def three_taps(weight, columns, length):
    parts = jnp.dot(weight[...], columns[:, 0:length], preferred_element_type=F32)
    return (
        parts[0:C]
        + pltpu.roll(parts[C : 2 * C], length - 1, 1)
        + pltpu.roll(parts[2 * C :], length - 2, 1)
    )


def weight_grad(gradient, columns, length, out, first_row):
    wide = gradient.astype(F32)
    stack = jnp.concatenate(
        [wide, pltpu.roll(wide, 1, 1), pltpu.roll(wide, 2, 1)], axis=0
    ).astype(BF16)
    sums = lax.dot_general(
        stack, columns[:, 0:length], (((1,), (1,)), ((), ())), preferred_element_type=F32
    ) * (1.0 / 512.0)
    for number in range(9):
        for dz in range(3):
            k = number * 3 + dz
            out[first_row : first_row + C, k * C : (k + 1) * C] = sums[
                dz * C : (dz + 1) * C, number * C : (number + 1) * C
            ]


def main_kernel(
    adj, own, field, xm, xp, ym, yp, c0, c1, c2, c3, table, marks, w_one, w_two,
    chunks, padded, hidden, grad_one,
    sources, col_m, col_g, grads,
):
    me = own[0]
    steps = [sx + GRID * sy for sx, sy in DIRECTIONS]
    numbers = []
    for k in range(27):
        block = adj[0, k]
        relative = block // REPS - me
        number = jnp.where(relative == 0, 1, -1)
        for d, step in enumerate(steps):
            number = jnp.where(relative == step, d + 2, number)
        numbers.append(jnp.where(block < 0, -1, number))

    def some(d):
        found = numbers[0] == d + 2
        for number in numbers[1:]:
            found = jnp.logical_or(found, number == d + 2)
        return found

    sources[:, 0:512] = field[...]

    @pl.when(some(3))
    def _():
        sources[:, 512:640] = xm[...]

    @pl.when(jnp.logical_not(some(3)))
    def _():
        sources[:, 512:640] = xp[...]

    @pl.when(some(1))
    def _():
        sources[:, 640:768] = ym[...]

    @pl.when(jnp.logical_not(some(1)))
    def _():
        sources[:, 640:768] = yp[...]

    sources[:, 768:896] = c0[...]
    for ref, d in ((c1, 2), (c2, 5), (c3, 7)):

        @pl.when(some(d))
        def _():
            sources[:, 768:896] = ref[...]

    site = table[0:1, :]
    which = jnp.full((1, LANES), -1, jnp.int32)
    for k in range(27):
        which = jnp.where(site == k, numbers[k], which)
    place = jnp.full((1, LANES), -1, jnp.int32)
    for d in range(9):
        place = jnp.where(which == d + 1, table[d + 1 : d + 2, :], place)

    width = 384
    for part in range(LANES // width):
        cut = slice(part * width, (part + 1) * width)
        rows = lax.broadcasted_iota(jnp.int32, (896, width), 0)
        hot = jnp.where(rows == place[:, cut], 1.0, 0.0).astype(BF16)
        padded[:, cut] = jnp.dot(sources[...], hot, preferred_element_type=F32).astype(BF16)

    shifted_columns(padded[0:C, :], col_m, OUTER)
    shifted_columns(padded[C : 2 * C, :], col_g, OUTER)
    mask = padded[2 * C : 2 * C + 1, BASE + 1 : BASE + 1 + OUTER].astype(F32)
    pre = three_taps(w_one, col_m, OUTER)
    sig = jax.nn.sigmoid(pre)
    hidden[...] = (pre * sig * mask).astype(BF16)
    back = three_taps(w_two, col_g, OUTER)
    grad = (back * mask * sig * (1.0 + pre * (1.0 - sig))).astype(BF16)
    grad_one[...] = grad
    grads[:, 27 * C :] = jnp.zeros((2 * C, TILES_L * 128 - 27 * C), F32)
    weight_grad(grad.astype(F32) * marks[0:1, :], col_m, OUTER, grads, 0)
    shifted_columns(hidden[...], col_g, INNER)
    start = 2 * (BASE + 1)
    grad_two = padded[C : 2 * C, start : start + INNER].astype(F32) * marks[1:2, 0:INNER]
    weight_grad(grad_two, col_g, INNER, grads, C)
    for row in range(TILES_R):
        for lane in range(TILES_L):
            chunks[row * TILES_L + lane] = grads[
                row * 8 : (row + 1) * 8, lane * 128 : (lane + 1) * 128
            ]
    chunks[TILES_R * TILES_L :] = jnp.zeros((8, 8, 128), F32)


def out_kernel(padded, hidden, grad_one, squeeze, w_two, w_one, out_feats, grad_feats, columns):
    start = 2 * (BASE + 1)
    mask = padded[2 * C : 2 * C + 1, start : start + INNER].astype(F32)
    for first, field, weight, out in (
        (0, hidden, w_two, out_feats),
        (C, grad_one, w_one, grad_feats),
    ):
        shifted_columns(field[...], columns, INNER)
        pre = three_taps(weight, columns, INNER)
        kept = padded[first : first + C, start : start + INNER].astype(F32)
        wide = (kept + pre * mask).astype(BF16)
        out[0] = jnp.dot(wide, squeeze[...], preferred_element_type=F32).astype(BF16)


def unpack_kernel(chunks, first, second):
    for row in range(TILES_R):
        out = first if row < 12 else second
        rows = slice(row % 12 * 8, row % 12 * 8 + 8)
        for lane in range(TILES_L):
            last = min((lane + 1) * 128, 27 * C)
            out[rows, lane * 128 : last] = chunks[row * TILES_L + lane][:, : last - lane * 128]


def forward_weight(weight):
    taps = weight.reshape(C, 9, 3, C)
    return jnp.transpose(taps, (2, 0, 1, 3)).reshape(3 * C, 9 * C)


def turned_weight(weight):
    taps = weight.reshape(C, 27, C)[:, ::-1, :].reshape(C, 9, 3, C)
    return jnp.transpose(taps, (2, 3, 1, 0)).reshape(3 * C, 9 * C)


VMEM = pl.BlockSpec(memory_space=pltpu.VMEM)
SMEM = pl.BlockSpec(memory_space=pltpu.SMEM)
PARAMS = pltpu.CompilerParams(vmem_limit_bytes=48 * 1024 * 1024)


def shape(dims, dtype):
    return jax.ShapeDtypeStruct(dims, dtype)


def body(feats, cotangent, occupancy, counts, adjacency, w_first, w_second):
    own = lax.axis_index("space")
    rim = shape((ROWS, 128), BF16)
    marks, squeeze = inner_table()
    with jax.named_scope("pack"):
        field, left, right, down, up, corners = pl.pallas_call(
            pack_kernel,
            out_shape=[shape((ROWS, 512), BF16)] + [rim] * 5,
            in_specs=[VMEM] * 4,
            out_specs=[VMEM] * 6,
            compiler_params=PARAMS,
        )(feats, cotangent, occupancy, jnp.asarray(pack_matrix(), BF16))
    sent = {(-1, 0): left, (1, 0): right, (0, -1): down, (0, 1): up}
    near = []
    with jax.named_scope("rims"):
        for sx, sy in DIRECTIONS:
            step = sx + GRID * sy
            pairs = []
            for owner in range(GRID * GRID):
                column, row = owner % GRID + sx, owner // GRID + sy
                if 0 <= column < GRID and 0 <= row < GRID:
                    pairs.append((owner + step, owner))
            near.append(lax.ppermute(sent.get((sx, sy), corners), "space", pairs))
    c0, ym, c1, xm, xp, c2, yp, c3 = near
    one_f, one_b = forward_weight(w_first), turned_weight(w_first)
    two_f, two_b = forward_weight(w_second), turned_weight(w_second)
    with jax.named_scope("middle"):
        chunks, padded, hidden, grad_one = pl.pallas_call(
            main_kernel,
            out_shape=[
                shape((512, 8, 128), F32),
                shape((ROWS, LANES), BF16),
                shape((C, OUTER), BF16),
                shape((C, OUTER), BF16),
            ],
            in_specs=[SMEM, SMEM] + [VMEM] * 13,
            out_specs=[VMEM] * 4,
            scratch_shapes=[
                pltpu.VMEM((ROWS, 896), BF16),
                pltpu.VMEM((9 * C, OUTER), BF16),
                pltpu.VMEM((9 * C, OUTER), BF16),
                pltpu.VMEM((2 * C, TILES_L * 128), F32),
            ],
            compiler_params=PARAMS,
        )(
            adjacency, own.reshape(1), field, xm, xp, ym, yp, c0, c1, c2, c3,
            jnp.asarray(place_table()), jnp.asarray(marks), one_f, two_b,
        )
    with jax.named_scope("sum"):
        total = lax.psum(chunks, ("space", "rep"))
    with jax.named_scope("outputs"):
        out_feats, grad_feats = pl.pallas_call(
            out_kernel,
            out_shape=[shape((1, C, 512), BF16)] * 2,
            in_specs=[VMEM] * 6,
            out_specs=[VMEM] * 2,
            scratch_shapes=[pltpu.VMEM((9 * C, INNER), BF16)],
            compiler_params=PARAMS,
        )(padded, hidden, grad_one, jnp.asarray(squeeze, BF16), two_f, one_b)
    with jax.named_scope("unpack"):
        grad_first, grad_second = pl.pallas_call(
            unpack_kernel,
            out_shape=[shape((C, 27 * C), F32)] * 2,
            in_specs=[VMEM],
            out_specs=[VMEM] * 2,
            compiler_params=PARAMS,
        )(total)
    return out_feats, grad_feats, grad_first, grad_second


def solution(mesh):
    both = ("space", "rep")
    blocks = P(both, None, None)
    rows = P(both, None)
    return jax.shard_map(
        body,
        mesh=mesh,
        in_specs=(blocks, blocks, rows, rows, rows, P(), P()),
        out_specs=(blocks, blocks, P(), P()),
        check_vma=False,
    )
```

time: 834 us -> 555 us (0.67)
  starting transfers between devices: 158 us -> 30.3 us
  between operations: 66.4 us -> 14.3 us
  local copies, waits for them, and re-layouts: 75.2 us -> 25.1 us
  waiting for transfers between devices: 511 us -> 470 us
  Pallas kernels: 0 us -> 14.2 us
  matrix products: 11.8 us -> 0 us
    ppermute x32 -> x8, starting transfers between devices: 158 us -> 30.3 us  [body(): near.append(lax.ppermute(sent.get((sx, sy), corners), 'space', pairs))]
    concatenate x8 -> x0, local copies, waits for them, and re-layouts: 23.9 us -> none  [the longest x4 23.2 us: columns(): return jnp.concatenate(stacked, axis=0)]
    ppermute x32 -> x8, waiting for transfers between devices: 21.9 us -> 0.02 us  [body(): near.append(lax.ppermute(sent.get((sx, sy), corners), 'space', pairs))]
    psum x1, waiting for transfers between devices: 489 us -> 470 us  [body(): total = lax.psum(chunks, ('space', 'rep'))]
    slice x18 -> x0, local copies, waits for them, and re-layouts: 16.6 us -> none  [the longest x16 15.2 us: columns(): padded[:, 1 + shift_x:1 + shift_x + cube_edge, 1 + shift_y:1 + shift_y +...]
    reshape x0 -> x8, local copies, waits for them, and re-layouts: none -> 14.8 us  [the longest x4 8.01 us: forward_weight(): return jnp.transpose(taps, (2, 0, 1, 3)).reshape(3 * C, 9 * C)]
    pallas_call x0 -> x4, Pallas kernels: none -> 14.2 us  [the longest x1 8.8 us: body(): pl.pallas_call(main_kernel, out_shape=[shape((512, 8, 128), F32), shape((...]
    squeeze x23 -> x0, local copies, waits for them, and re-layouts: 13.7 us -> none  [rim_piece(): return lax.dynamic_slice(sources, starts, extents)[0]]
  transfers between devices with their start and end apart: 33 -> 9, of which waited for: 15 -> 1; matrix products, arithmetic and copies ran while one was open for 4% -> 3% of each run, Pallas kernels for 0% -> 1%
where the time goes in v1:
time: 555 us; the launch traced here: 554 us
  waiting for transfers between devices  470 us (85%)
  starting transfers between devices  30.3 us (5%)
  local copies, waits for them, and re-layouts  25.1 us (5%)
  between operations  14.3 us (3%)
  Pallas kernels  14.2 us (3%)
    psum x1, waiting for transfers between devices, body(): total = lax.psum(chunks, ('space', 'rep'))  470 us
    ppermute x8, starting transfers between devices, body(): near.append(lax.ppermute(sent.get((sx, sy), corners), 'space', pairs))  30.3 us
  transfers between devices with their start and end apart: 9, of which 1 were waited for; matrix products, arithmetic and copies ran while one was open for 3% of the time, Pallas kernels for 1%

profile of v1, /device:TPU:1, one launch (start us, length us, event | category | flops | bytes accessed | tf_op | source)
XLA Modules:
  0.0 554.2 jit_solution(11245985788079560629)
XLA Ops:
  7.2 1.0 copy-done.2
  8.2 0.9 copy-done.6
  9.1 0.9 copy-done.7
  10.0 0.7 copy-done.9
  10.7 0.3 pack.1
  11.0 4.0 collective-permute-start
  15.0 1.3 collective-permute-start.1
  16.3 4.9 collective-permute-start.2
  21.2 1.3 collective-permute-start.7
  22.5 0.7 collective-permute-start.6
  23.2 1.3 collective-permute-start.3
  24.5 0.7 collective-permute-start.5
  25.2 16.1 %collective-permute-start.4 = (bf16[208,128]{1,0:T(8,128)(2,1)S(1)}, bf16[208,128]{1,0:T(8,128)(2,1)S(1)}, u32[]{:S(2)}, u32[]{:S(2)}) collective-permute-start(bf16[208,128]{1,0:T(8,128)(2,1)S(1)} %get-tuple-element.23), channel_id=1, source_target_pairs={{0,72},{8,80},{16,88},{24,96},{32,104},{40,112},{48,120},{64,136},... | collective-permute-start | bytes 159752 | tf_op jit(solution)/shard_map/rims/ppermute | solution.py:277
  41.3 1.4 copy.16
  42.7 0.3 copy.18
  43.1 0.8 copy-done.11
  43.9 1.4 copy.32
  45.3 1.9 reshape.53.w_two
  47.2 2.0 copy.30
  49.2 2.0 reshape.52.w_one
  51.3 8.8 %middle.1 = (f32[512,8,128]{2,1,0:T(8,128)}, bf16[208,1920]{1,0:T(8,128)(2,1)S(1)}, bf16[96,1536]{1,0:T(8,128)(2,1)S(1)}, bf16[96,1536]{1,0:T(8,128)(2,1)S(1)}) custom-call(s32[1,27]{1,0:T(1,128)S(1)} %copy-done.10, s32[1]{0:T(128)} %bitcast.own, bf16[208,512]{1,0:T(8,128)(2,1)S(1)} %get-tuple-element.18.field, ...), custom_call_target="tpu_custom_call" | custom-call | tf_op jit(solution)/shard_map/middle/pallas_call | solution.py:282
  60.1 0.7 copy-done.3
  60.8 1.1 copy-done.14
  62.0 1.4 copy.35
  63.4 2.0 reshape.55.w_one
  65.4 2.0 copy.33
  67.4 2.0 reshape.54.w_two
  69.5 1.0 copy-done.4
  70.4 3.7 outputs.1
  74.1 470.3 %all-reduce.2.cloned.1.call-done.chunks = f32[512,8,128]{2,1,0:T(8,128)} async-done(((f32[512,8,128]{2,1,0:T(8,128)}), f32[512,8,128]{2,1,0:T(8,128)}) %all-reduce.2.cloned.1.call-update) | async-done | bytes 2097168 | tf_op jit(solution)/shard_map/sum/psum | solution.py:304
  544.4 1.6 copy-done
  546.0 1.4 unpack.1
  (35 shorter events, 0.2 us)
Async XLA Ops:
  7.2 537.2 %all-reduce.2.cloned.1.call-start = ((), (), s32[]{:S(2)}) async-start(), calls=%async_computation | async-start | bytes 4194304 | tf_op jit(solution)/shard_map/sum/psum | solution.py:304
  7.2 1.0 copy-start.2
  8.2 0.9 copy-start.6
  9.1 0.9 copy-start.7
  10.0 0.7 copy-start.9
  10.7 32.0 %copy-start.15 = (bf16[96,2592]{1,0:T(8,128)(2,1)S(1)}, bf16[96,2592]{1,0:T(8,128)(2,1)}, u32[]{:S(2)}) copy-start(bf16[96,2592]{1,0:T(8,128)(2,1)} %param.16) | copy-start | bytes 1492996
  11.0 12.2 %collective-permute-start = (bf16[208,128]{1,0:T(8,128)(2,1)S(1)}, bf16[208,128]{1,0:T(8,128)(2,1)S(1)}, u32[]{:S(2)}, u32[]{:S(2)}) collective-permute-start(bf16[208,128]{1,0:T(8,128)(2,1)S(1)} %get-tuple-element.19), channel_id=1, source_target_pairs={{0,8},{8,16},{16,24},{24,32},{32,40},{40,48},{48,56},{64,72},{72,8... | collective-permute-start | bytes 159752 | tf_op jit(solution)/shard_map/rims/ppermute | solution.py:277
  15.0 9.5 %collective-permute-start.1 = (bf16[208,128]{1,0:T(8,128)(2,1)S(1)}, bf16[208,128]{1,0:T(8,128)(2,1)S(1)}, u32[]{:S(2)}, u32[]{:S(2)}) collective-permute-start(bf16[208,128]{1,0:T(8,128)(2,1)S(1)} %get-tuple-element.20), channel_id=1, source_target_pairs={{8,0},{16,8},{24,16},{32,24},{40,32},{48,40},{56,48},{72,64},{80,7... | collective-permute-start | bytes 159752 | tf_op jit(solution)/shard_map/rims/ppermute | solution.py:277
  16.3 8.9 %collective-permute-start.2 = (bf16[208,128]{1,0:T(8,128)(2,1)S(1)}, bf16[208,128]{1,0:T(8,128)(2,1)S(1)}, u32[]{:S(2)}, u32[]{:S(2)}) collective-permute-start(bf16[208,128]{1,0:T(8,128)(2,1)S(1)} %get-tuple-element.21), channel_id=1, source_target_pairs={{0,64},{8,72},{16,80},{24,88},{32,96},{40,104},{48,112},{56,120},{... | collective-permute-start | bytes 159752 | tf_op jit(solution)/shard_map/rims/ppermute | solution.py:277
  21.2 30.0 %collective-permute-start.7 = (bf16[208,128]{1,0:T(8,128)(2,1)S(1)}, bf16[208,128]{1,0:T(8,128)(2,1)S(1)}, u32[]{:S(2)}, u32[]{:S(2)}) collective-permute-start(bf16[208,128]{1,0:T(8,128)(2,1)S(1)} %get-tuple-element.23), channel_id=1, source_target_pairs={{72,0},{80,8},{88,16},{96,24},{104,32},{112,40},{120,48},{136,64},... | collective-permute-start | bytes 159752 | tf_op jit(solution)/shard_map/rims/ppermute | solution.py:277
  22.5 28.7 %collective-permute-start.6 = (bf16[208,128]{1,0:T(8,128)(2,1)S(1)}, bf16[208,128]{1,0:T(8,128)(2,1)S(1)}, u32[]{:S(2)}, u32[]{:S(2)}) collective-permute-start(bf16[208,128]{1,0:T(8,128)(2,1)S(1)} %get-tuple-element.23), channel_id=1, source_target_pairs={{64,8},{72,16},{80,24},{88,32},{96,40},{104,48},{112,56},{128,72},... | collective-permute-start | bytes 159752 | tf_op jit(solution)/shard_map/rims/ppermute | solution.py:277
  23.2 28.0 %collective-permute-start.3 = (bf16[208,128]{1,0:T(8,128)(2,1)S(1)}, bf16[208,128]{1,0:T(8,128)(2,1)S(1)}, u32[]{:S(2)}, u32[]{:S(2)}) collective-permute-start(bf16[208,128]{1,0:T(8,128)(2,1)S(1)} %get-tuple-element.22), channel_id=1, source_target_pairs={{64,0},{72,8},{80,16},{88,24},{96,32},{104,40},{112,48},{120,56},{... | collective-permute-start | bytes 159752 | tf_op jit(solution)/shard_map/rims/ppermute | solution.py:277
  24.5 26.8 %collective-permute-start.5 = (bf16[208,128]{1,0:T(8,128)(2,1)S(1)}, bf16[208,128]{1,0:T(8,128)(2,1)S(1)}, u32[]{:S(2)}, u32[]{:S(2)}) collective-permute-start(bf16[208,128]{1,0:T(8,128)(2,1)S(1)} %get-tuple-element.23), channel_id=1, source_target_pairs={{8,64},{16,72},{24,80},{32,88},{40,96},{48,104},{56,112},{72,128},... | collective-permute-start | bytes 159752 | tf_op jit(solution)/shard_map/rims/ppermute | solution.py:277
  25.2 26.1 %collective-permute-start.4 = (bf16[208,128]{1,0:T(8,128)(2,1)S(1)}, bf16[208,128]{1,0:T(8,128)(2,1)S(1)}, u32[]{:S(2)}, u32[]{:S(2)}) collective-permute-start(bf16[208,128]{1,0:T(8,128)(2,1)S(1)} %get-tuple-element.23), channel_id=1, source_target_pairs={{0,72},{8,80},{16,88},{24,96},{32,104},{40,112},{48,120},{64,136},... | collective-permute-start | bytes 159752 | tf_op jit(solution)/shard_map/rims/ppermute | solution.py:277
  42.7 4.5 copy-start.13
  43.0 0.8 copy-start.11
  49.2 2.0 copy-start.5
  49.2 2.1 copy-start.8
  49.2 2.1 copy-start.10
  60.1 0.7 copy-start.3
  60.8 1.1 copy-start.14
  63.4 2.0 copy-start.12
  67.4 2.0 copy-start.1
  69.5 1.0 copy-start.4
  544.4 1.6 copy-start
Sparse Core Ops, SparseCore 0:
  61.0 483.3 all-reduce.1

commit v2 on v1

v2 whole, which is shorter than its diff:
```python
import jax
import jax.numpy as jnp
import numpy as np
from jax import lax
from jax.experimental import pallas as pl
from jax.experimental.pallas import tpu as pltpu
from jax.sharding import Mesh, PartitionSpec as P

C = 96
BE = 8
GRID = 8
REPS = 8
ROWS = 208
PAD = 12
LANES = 1920
OUTER = 1536
INNER = 1152
BASE = PAD * PAD + PAD
TILES_L = 21
DIRECTIONS = [(-1, -1), (0, -1), (1, -1), (-1, 0), (1, 0), (-1, 1), (0, 1), (1, 1)]
OFFSETS = [(a, b, c) for a in (-1, 0, 1) for b in (-1, 0, 1) for c in (-1, 0, 1)]
F32, BF16 = jnp.float32, jnp.bfloat16


def rim_matrix():
    picks = np.zeros((768, 512), np.float32)
    for half, first in ((0, 6), (1, 0)):
        for y in range(2):
            for z in range(8):
                for x in range(8):
                    picks[x * 64 + (first + y) * 8 + z, half * 256 + x * 16 + y * 8 + z] = 1
                for x in range(2):
                    rim = x * 64 + (first + y) * 8 + z
                    picks[512 + rim, half * 256 + 128 + x * 16 + y * 8 + z] = 1
                    picks[640 + rim, half * 256 + 160 + x * 16 + y * 8 + z] = 1
    return picks


def place_table():
    table = np.full((16, LANES), -1, np.int32)
    table[0] = 27
    for p in range(PAD**3):
        at = (p // (PAD * PAD) - 2, p // PAD % PAD - 2, p % PAD - 2)
        site = [(-1 if a < 0 else 1 if a >= BE else 0) for a in at]
        x, y, z = (a % BE for a in at)
        table[0, p] = (site[0] + 1) * 9 + (site[1] + 1) * 3 + site[2] + 1
        table[1, p] = x * 64 + y * 8 + z
        for number, (sx, sy) in enumerate(DIRECTIONS):
            nx = x - 6 if sx < 0 else x
            ny = y - 6 if sy < 0 else y
            if sx != 0 and not 0 <= nx < 2 or sy != 0 and not 0 <= ny < 2:
                continue
            if sy == 0:
                place = 512 + nx * 64 + y * 8 + z
            elif sx == 0:
                place = 640 + x * 16 + ny * 8 + z
            else:
                place = (768 if sx < 0 else 800) + nx * 16 + ny * 8 + z
            table[2 + number, p] = place
    return table


def inner_table():
    marks = np.zeros((8, OUTER), np.float32)
    squeeze = np.zeros((INNER, 512), np.float32)
    for x in range(8):
        for y in range(8):
            for z in range(8):
                t = x * PAD * PAD + y * PAD + z
                marks[0, t + BASE + 1] = 1
                marks[1, t] = 1
                squeeze[t, x * 64 + y * 8 + z] = 1
    return marks, squeeze


def pack_kernel(feats_in, cot_in, occ_in, field, left, right, feats, cot, occ, sems):
    copies = [
        pltpu.make_async_copy(source, target, sems.at[number])
        for number, (source, target) in enumerate(((occ_in, occ), (feats_in, feats), (cot_in, cot)))
    ]
    for copy in copies:
        copy.start()
    copies[0].wait()
    mask = (occ[...] != 0).astype(F32).astype(BF16)
    field[2 * C :, :] = jnp.broadcast_to(mask, (ROWS - 2 * C, 512))
    copies[1].wait()
    field[0:C, :] = feats[0] * mask
    copies[2].wait()
    field[C : 2 * C, :] = cot[0] * mask
    left[...] = field[:, 384:512]
    right[...] = field[:, 0:128]


def rim_kernel(field, xm, xp, picks, down, up):
    sources = jnp.concatenate([field[...], xm[...], xp[...]], axis=1)
    rims = jnp.dot(sources, picks[...], preferred_element_type=F32).astype(BF16)
    down[...] = rims[:, 0:256]
    up[...] = rims[:, 256:512]


def weight_kernel(first, second, first_forward, first_turned, second_forward, second_turned):
    for weight, forward, turned in (
        (first, first_forward, first_turned),
        (second, second_forward, second_turned),
    ):
        whole = weight[...]
        across = whole.astype(F32).T.astype(BF16)
        for number in range(9):
            for dz in range(3):
                k = number * 3 + dz
                rows = slice(dz * C, (dz + 1) * C)
                columns = slice(number * C, (number + 1) * C)
                forward[rows, columns] = whole[:, k * C : (k + 1) * C]
                turned[rows, columns] = across[(26 - k) * C : (27 - k) * C, :]


def shifted_columns(source, columns, length):
    for number in range(9):
        start = (number // 3) * PAD * PAD + (number % 3) * PAD
        columns[number * C : (number + 1) * C, 0:length] = source[:, start : start + length]


def three_taps(weight, columns, length):
    parts = jnp.dot(weight[...], columns[:, 0:length], preferred_element_type=F32)
    return (
        parts[0:C]
        + pltpu.roll(parts[C : 2 * C], length - 1, 1)
        + pltpu.roll(parts[2 * C :], length - 2, 1)
    )


def weight_grad(gradient, columns, length, out, first_row):
    wide = gradient.astype(F32)
    stack = jnp.concatenate(
        [wide, pltpu.roll(wide, 1, 1), pltpu.roll(wide, 2, 1)], axis=0
    ).astype(BF16)
    sums = lax.dot_general(
        stack, columns[:, 0:length], (((1,), (1,)), ((), ())), preferred_element_type=F32
    ) * (1.0 / 512.0)
    for number in range(9):
        for dz in range(3):
            k = number * 3 + dz
            out[first_row : first_row + C, k * C : (k + 1) * C] = sums[
                dz * C : (dz + 1) * C, number * C : (number + 1) * C
            ]


def main_kernel(
    adj, own, field, xm, xp, ym, yp, table, marks, w_one, w_two,
    keep, send, padded, hidden, grad_one,
    sources, col_m, col_g, grads,
):
    me = own[0]
    steps = [sx + GRID * sy for sx, sy in DIRECTIONS]
    numbers = []
    for k in range(27):
        block = adj[0, k]
        relative = block // REPS - me
        number = jnp.where(relative == 0, 1, -1)
        for d, step in enumerate(steps):
            number = jnp.where(relative == step, d + 2, number)
        numbers.append(jnp.where(block < 0, -1, number))

    def some(*directions):
        found = numbers[0] == directions[0] + 2
        for number in numbers:
            for d in directions:
                found = jnp.logical_or(found, number == d + 2)
        return found

    sources[:, 0:512] = field[...]
    at_left, at_low = some(3), some(0, 1, 2)

    @pl.when(at_left)
    def _():
        sources[:, 512:640] = xm[...]

    @pl.when(jnp.logical_not(at_left))
    def _():
        sources[:, 512:640] = xp[...]

    @pl.when(at_low)
    def _():
        sources[:, 640:896] = ym[...]

    @pl.when(jnp.logical_not(at_low))
    def _():
        sources[:, 640:896] = yp[...]

    site = table[0:1, :]
    which = jnp.full((1, LANES), -1, jnp.int32)
    for k in range(27):
        which = jnp.where(site == k, numbers[k], which)
    place = jnp.full((1, LANES), -1, jnp.int32)
    for d in range(9):
        place = jnp.where(which == d + 1, table[d + 1 : d + 2, :], place)

    width = 384
    for part in range(LANES // width):
        cut = slice(part * width, (part + 1) * width)
        rows = lax.broadcasted_iota(jnp.int32, (896, width), 0)
        hot = jnp.where(rows == place[:, cut], 1.0, 0.0).astype(BF16)
        padded[:, cut] = jnp.dot(sources[...], hot, preferred_element_type=F32).astype(BF16)

    shifted_columns(padded[0:C, :], col_m, OUTER)
    shifted_columns(padded[C : 2 * C, :], col_g, OUTER)
    mask = padded[2 * C : 2 * C + 1, BASE + 1 : BASE + 1 + OUTER].astype(F32)
    pre = three_taps(w_one, col_m, OUTER)
    sig = jax.nn.sigmoid(pre)
    hidden[...] = (pre * sig * mask).astype(BF16)
    back = three_taps(w_two, col_g, OUTER)
    grad = (back * mask * sig * (1.0 + pre * (1.0 - sig))).astype(BF16)
    grad_one[...] = grad
    grads[:, 27 * C :] = jnp.zeros((2 * C, TILES_L * 128 - 27 * C), F32)
    weight_grad(grad.astype(F32) * marks[0:1, :], col_m, OUTER, grads, 0)
    shifted_columns(hidden[...], col_g, INNER)
    start = 2 * (BASE + 1)
    grad_two = padded[C : 2 * C, start : start + INNER].astype(F32) * marks[1:2, 0:INNER]
    weight_grad(grad_two, col_g, INNER, grads, C)

    def split(halves):
        for tile in range(256):
            half, place = halves[tile // 128], tile % 128
            if tile < 12 * TILES_L:
                row, lane = tile // TILES_L * 16, tile % TILES_L * 128
                half[place] = grads[row : row + 16, lane : lane + 128]
            else:
                half[place] = jnp.zeros((16, 128), F32)

    @pl.when(own[1] == 0)
    def _():
        split((keep, send))

    @pl.when(own[1] != 0)
    def _():
        split((send, keep))


def out_kernel(padded, hidden, grad_one, squeeze, w_two, w_one, out_feats, grad_feats, columns):
    start = 2 * (BASE + 1)
    mask = padded[2 * C : 2 * C + 1, start : start + INNER].astype(F32)
    for first, field, weight, out in (
        (0, hidden, w_two, out_feats),
        (C, grad_one, w_one, grad_feats),
    ):
        shifted_columns(field[...], columns, INNER)
        pre = three_taps(weight, columns, INNER)
        kept = padded[first : first + C, start : start + INNER].astype(F32)
        wide = (kept + pre * mask).astype(BF16)
        out[0] = jnp.dot(wide, squeeze[...], preferred_element_type=F32).astype(BF16)


def unpack_kernel(own, mine, other, first, second):
    def join(halves):
        for tile in range(12 * TILES_L):
            row, lane = tile // TILES_L * 16, tile % TILES_L * 128
            out = first if row < C else second
            last = min(lane + 128, 27 * C)
            part = halves[tile // 128][tile % 128].astype(F32)
            out[row % C : row % C + 16, lane:last] = part[:, : last - lane]

    @pl.when(own[1] == 0)
    def _():
        join((mine, other))

    @pl.when(own[1] != 0)
    def _():
        join((other, mine))


VMEM = pl.BlockSpec(memory_space=pltpu.VMEM)
SMEM = pl.BlockSpec(memory_space=pltpu.SMEM)
PARAMS = pltpu.CompilerParams(vmem_limit_bytes=48 * 1024 * 1024)


def shape(dims, dtype):
    return jax.ShapeDtypeStruct(dims, dtype)


def call(kernel, outs, specs, scratch=()):
    return pl.pallas_call(
        kernel,
        out_shape=[shape(*out) for out in outs],
        in_specs=specs,
        out_specs=[VMEM] * len(outs),
        scratch_shapes=scratch,
        compiler_params=PARAMS,
    )


def from_owner(value, sx, sy):
    pairs = []
    for owner in range(GRID * GRID):
        column, row = owner % GRID + sx, owner // GRID + sy
        if 0 <= column < GRID and 0 <= row < GRID:
            pairs.append((row * GRID + column, owner))
    return lax.ppermute(value, ("z", "y"), pairs)


def sum_shares(value, axes, count):
    parts = lax.all_to_all(value, axes, 0, 0, tiled=True)
    parts = parts.reshape((count, value.shape[0] // count) + value.shape[1:])
    return jnp.sum(parts.astype(F32), axis=0)


def all_shares(value, axes, count):
    copies = jnp.broadcast_to(value[None], (count,) + value.shape)
    return lax.all_to_all(copies, axes, 0, 0).reshape((count * value.shape[0],) + value.shape[1:])


def body(feats, cotangent, occupancy, counts, adjacency, w_first, w_second):
    own = jnp.stack([lax.axis_index(("z", "y")), lax.axis_index("core")]).astype(jnp.int32)
    marks, squeeze = inner_table()
    wide, rim, turned = ((ROWS, 512), BF16), ((ROWS, 128), BF16), ((3 * C, 9 * C), BF16)
    with jax.named_scope("pack"):
        field, left, right = call(
            pack_kernel,
            [wide, rim, rim],
            [pl.BlockSpec(memory_space=pl.ANY)] * 3,
            [
                pltpu.VMEM((1, C, 512), BF16),
                pltpu.VMEM((1, C, 512), BF16),
                pltpu.VMEM((1, 512), jnp.int32),
                pltpu.SemaphoreType.DMA((3,)),
            ],
        )(feats, cotangent, occupancy)
    with jax.named_scope("weights"):
        one_f, one_b, two_f, two_b = call(weight_kernel, [turned] * 4, [VMEM] * 2)(w_first, w_second)
    with jax.named_scope("rims_x"):
        xm, xp = from_owner(left, -1, 0), from_owner(right, 1, 0)
    with jax.named_scope("rim_rows"):
        down, up = call(rim_kernel, [((ROWS, 256), BF16)] * 2, [VMEM] * 4)(
            field, xm, xp, jnp.asarray(rim_matrix(), BF16)
        )
    with jax.named_scope("rims_y"):
        ym, yp = from_owner(down, 0, -1), from_owner(up, 0, 1)
    half = ((128, 16, 128), F32)
    with jax.named_scope("middle"):
        keep, send, padded, hidden, grad_one = call(
            main_kernel,
            [half, half, ((ROWS, LANES), BF16), ((C, OUTER), BF16), ((C, OUTER), BF16)],
            [SMEM, SMEM] + [VMEM] * 9,
            [
                pltpu.VMEM((ROWS, 896), BF16),
                pltpu.VMEM((9 * C, OUTER), BF16),
                pltpu.VMEM((9 * C, OUTER), BF16),
                pltpu.VMEM((2 * C, TILES_L * 128), F32),
            ],
        )(
            adjacency, own, field, xm, xp, ym, yp,
            jnp.asarray(place_table()), jnp.asarray(marks), one_f, two_b,
        )
    with jax.named_scope("sum"):
        swap = [(0, 1), (1, 0)]
        pair = (keep + lax.ppermute(send, "core", swap)).astype(BF16)
        plane = sum_shares(pair, ("y", "x"), 16)
        total = sum_shares(plane.reshape(16, 8, 128), "z", 16)
        total = all_shares(total.astype(BF16), "z", 16)
        mine = all_shares(total.reshape(8, 16, 128), ("y", "x"), 16)
        other = lax.ppermute(mine, "core", swap)
    with jax.named_scope("outputs"):
        out_feats, grad_feats = call(
            out_kernel,
            [((1, C, 512), BF16)] * 2,
            [VMEM] * 6,
            [pltpu.VMEM((9 * C, INNER), BF16)],
        )(padded, hidden, grad_one, jnp.asarray(squeeze, BF16), two_f, one_b)
    with jax.named_scope("unpack"):
        grad_first, grad_second = call(
            unpack_kernel, [((C, 27 * C), F32)] * 2, [SMEM] + [VMEM] * 2
        )(own, mine, other)
    return out_feats, grad_feats, grad_first, grad_second


def solution(mesh):
    fine = Mesh(mesh.devices.reshape(16, 4, 4, 2), ("z", "y", "x", "core"))
    both = ("z", "y", "x", "core")
    blocks = P(both, None, None)
    rows = P(both, None)
    return jax.shard_map(
        body,
        mesh=fine,
        in_specs=(blocks, blocks, rows, rows, rows, P(), P()),
        out_specs=(blocks, blocks, P(), P()),
        check_vma=False,
    )
```

time: 555 us -> 123 us (0.22)
  waiting for transfers between devices: 470 us -> 9.18 us
  blocking collectives: 0 us -> 69.2 us
  local copies, waits for them, and re-layouts: 25.1 us -> 4.73 us
  between operations: 14.3 us -> 0.82 us
  starting transfers between devices: 30.3 us -> 23.5 us
    psum x1 -> x0, waiting for transfers between devices: 470 us -> none  [body(): total = lax.psum(chunks, ('space', 'rep'))]
    all_to_all x0 -> x4, blocking collectives: none -> 69.2 us  [the longest x2 42.2 us: sum_shares(): parts = lax.all_to_all(value, axes, 0, 0, tiled=True)]
    reshape x8 -> x0, local copies, waits for them, and re-layouts: 14.8 us -> none  [the longest x4 8.01 us: forward_weight(): return jnp.transpose(taps, (2, 0, 1, 3)).reshape(3 * C, 9 * C)]
    ppermute x8 -> x6, waiting for transfers between devices: 0.02 us -> 9.18 us  [the longest x4 6.91 us: from_owner(): return lax.ppermute(value, ('z', 'y'), pairs)]
    ppermute x8 -> x6, starting transfers between devices: 30.3 us -> 23.5 us  [the longest x4 11.5 us: from_owner(): return lax.ppermute(value, ('z', 'y'), pairs)]
    unnamed x34 -> x24, local copies, waits for them, and re-layouts: 10.3 us -> 4.63 us
    pallas_call x4 -> x6, Pallas kernels: 14.2 us -> 14.8 us  [the longest x1 7.1 us: body(): call(main_kernel, [half, half, ((ROWS, LANES), BF16), ((C, OUTER), BF16),...]
  transfers between devices with their start and end apart: 9 -> 6, of which waited for: 1 -> 4; matrix products, arithmetic and copies ran while one was open for 3% -> 0% of each run, Pallas kernels for 1% -> 4%
where the time goes in v2:
time: 123 us; the launch traced here: 122 us
  blocking collectives  69.2 us (56%)
  starting transfers between devices  23.5 us (19%)
  Pallas kernels  14.8 us (12%)
  waiting for transfers between devices  9.18 us (7%)
  local copies, waits for them, and re-layouts  4.73 us (4%)
    all_to_all x2, blocking collectives, sum_shares(): parts = lax.all_to_all(value, axes, 0, 0, tiled=True)  42.2 us
    all_to_all x2, blocking collectives, all_shares(): lax.all_to_all(copies, axes, 0, 0)  27 us
    ppermute x4, starting transfers between devices, from_owner(): return lax.ppermute(value, ('z', 'y'), pairs)  11.5 us
    pallas_call x1, Pallas kernels, body(): call(main_kernel, [half, half, ((ROWS, LANES), BF16), ((C, OUTER), BF16),...  7.1 us
    ppermute x4, waiting for transfers between devices, from_owner(): return lax.ppermute(value, ('z', 'y'), pairs)  6.91 us
    ppermute x1, starting transfers between devices, body(): other = lax.ppermute(mine, 'core', swap)  6.81 us
    ppermute x1, starting transfers between devices, body(): pair = (keep + lax.ppermute(send, 'core', swap)).astype(BF16)  5.13 us
    unnamed x24, local copies, waits for them, and re-layouts  4.63 us
  transfers between devices with their start and end apart: 6, of which 4 were waited for; matrix products, arithmetic and copies ran while one was open for 0% of the time, Pallas kernels for 4%

profile of v2, /device:TPU:1, one launch (start us, length us, event | category | flops | bytes accessed | tf_op | source)
XLA Modules:
  0.0 122.5 jit_solution(15422770260311430498)
XLA Ops:
  0.6 0.0 copy-start.1
  0.7 1.0 copy-done.7
  1.6 0.9 copy-done.8
  2.5 0.7 copy-done.10
  3.2 0.3 pack.1
  3.5 4.0 %collective-permute-start = (bf16[208,128]{1,0:T(8,128)(2,1)S(1)}, bf16[208,128]{1,0:T(8,128)(2,1)S(1)}, u32[]{:S(2)}, u32[]{:S(2)}) collective-permute-start(bf16[208,128]{1,0:T(8,128)(2,1)S(1)} %get-tuple-element.23), channel_id=1, source_target_pairs={{0,8},{8,16},{16,24},{24,32},{32,40},{40,48},{48,56},{64,72},{72,8... | collective-permute-start | bytes 159752 | tf_op jit(solution)/shard_map/rims_x/ppermute | solution.py:297
  7.5 1.3 %collective-permute-start.1 = (bf16[208,128]{1,0:T(8,128)(2,1)S(1)}, bf16[208,128]{1,0:T(8,128)(2,1)S(1)}, u32[]{:S(2)}, u32[]{:S(2)}) collective-permute-start(bf16[208,128]{1,0:T(8,128)(2,1)S(1)} %get-tuple-element.24), channel_id=1, source_target_pairs={{8,0},{16,8},{24,16},{32,24},{40,32},{48,40},{56,48},{72,64},{80,7... | collective-permute-start | bytes 159752 | tf_op jit(solution)/shard_map/rims_x/ppermute | solution.py:297
  8.8 0.0 copy-start.2
  8.9 1.0 copy-done.2
  9.9 1.0 copy-done.3
  10.9 1.4 %weights.1 = (bf16[288,864]{1,0:T(8,128)(2,1)S(1)}, bf16[288,864]{1,0:T(8,128)(2,1)S(1)}, bf16[288,864]{1,0:T(8,128)(2,1)S(1)}, bf16[288,864]{1,0:T(8,128)(2,1)S(1)}) custom-call(bf16[96,2592]{1,0:T(8,128)(2,1)S(1)} %copy-done.2, bf16[96,2592]{1,0:T(8,128)(2,1)S(1)} %copy-done.3), custom_call_target="tpu_custom_call" | custom-call | tf_op jit(solution)/shard_map/weights/pallas_call | solution.py:328
  12.3 0.1 collective-permute-done.1.xp
  12.4 0.3 rim_rows.1
  12.8 4.9 %collective-permute-start.2 = (bf16[208,256]{1,0:T(8,128)(2,1)S(1)}, bf16[208,256]{1,0:T(8,128)(2,1)S(1)}, u32[]{:S(2)}, u32[]{:S(2)}) collective-permute-start(bf16[208,256]{1,0:T(8,128)(2,1)S(1)} %get-tuple-element.25), channel_id=1, source_target_pairs={{0,64},{8,72},{16,80},{24,88},{32,96},{40,104},{48,112},{56,120},{... | collective-permute-start | bytes 319496 | tf_op jit(solution)/shard_map/rims_y/ppermute | solution.py:297
  17.7 1.3 %collective-permute-start.3 = (bf16[208,256]{1,0:T(8,128)(2,1)S(1)}, bf16[208,256]{1,0:T(8,128)(2,1)S(1)}, u32[]{:S(2)}, u32[]{:S(2)}) collective-permute-start(bf16[208,256]{1,0:T(8,128)(2,1)S(1)} %get-tuple-element.26), channel_id=1, source_target_pairs={{64,0},{72,8},{80,16},{88,24},{96,32},{104,40},{112,48},{120,56},{... | collective-permute-start | bytes 319496 | tf_op jit(solution)/shard_map/rims_y/ppermute | solution.py:297
  19.0 0.1 pad_add_fusion.own
  19.0 0.3 collective-permute-done.2.ym
  19.4 6.5 %collective-permute-done.3.yp = bf16[208,256]{1,0:T(8,128)(2,1)S(1)} collective-permute-done((bf16[208,256]{1,0:T(8,128)(2,1)S(1)}, bf16[208,256]{1,0:T(8,128)(2,1)S(1)}, u32[]{:S(2)}, u32[]{:S(2)}) %collective-permute-start.3) | collective-permute-done | bytes 106528 | tf_op jit(solution)/shard_map/rims_y/ppermute | solution.py:297
  25.9 7.1 %middle.1 = (f32[128,16,128]{2,1,0:T(8,128)S(1)}, f32[128,16,128]{2,1,0:T(8,128)S(1)}, bf16[208,1920]{1,0:T(8,128)(2,1)S(1)}, bf16[96,1536]{1,0:T(8,128)(2,1)S(1)}, bf16[96,1536]{1,0:T(8,128)(2,1)S(1)}) custom-call(s32[1,27]{1,0:T(1,128)S(1)} %copy-done.11, s32[2]{0:T(128)S(1)} %pad_add_fusion.own, bf16[208,512]{1,0:T(8,128)(2,1)S(1)} %get-tuple-element.22.field, ...), custom_call_target="tpu_custom_call" | custom-call | tf_op jit(solution)/shard_map/middle/pallas_call | solution.py:339
  33.0 0.0 copy-start.4
  33.0 5.1 %collective-permute-start.4 = (f32[128,16,128]{2,1,0:T(8,128)S(1)}, f32[128,16,128]{2,1,0:T(8,128)S(1)}, u32[]{:S(2)}, u32[]{:S(2)}) collective-permute-start(f32[128,16,128]{2,1,0:T(8,128)S(1)} %get-tuple-element.37), channel_id=1, source_target_pairs={{0,1},{1,0},{2,3},{3,2},{4,5},{5,4},{6,7},{7,6},{8,9},{9,8},{10,11... | collective-permute-start | bytes 3145736 | tf_op jit(solution)/shard_map/sum/ppermute | solution.py:355
  38.1 2.3 %collective-permute-done.4 = f32[128,16,128]{2,1,0:T(8,128)S(1)} collective-permute-done((f32[128,16,128]{2,1,0:T(8,128)S(1)}, f32[128,16,128]{2,1,0:T(8,128)S(1)}, u32[]{:S(2)}, u32[]{:S(2)}) %collective-permute-start.4) | collective-permute-done | bytes 1048608 | tf_op jit(solution)/shard_map/sum/ppermute | solution.py:355
  40.4 0.1 add_convert_fusion
  40.5 20.0 %all_to_all.20 = bf16[128,16,128]{2,1,0:T(8,128)(2,1)S(1)} all-to-all(bf16[128,16,128]{2,1,0:T(8,128)(2,1)S(1)} %add_convert_fusion), channel_id=1, replica_groups=mesh['z'=16,'y'=4,'x'=4,'core'=2] {'y','x'}, dimensions={0} | all-to-all | bytes 1048576 | tf_op jit(solution)/shard_map/sum/all_to_all | solution.py:301
  60.5 0.1 convert_reduce_fusion
  60.6 22.2 %all_to_all.21 = f32[16,8,128]{2,1,0:T(8,128)S(1)} all-to-all(f32[16,8,128]{2,1,0:T(8,128)S(1)} %bitcast.10), channel_id=1, replica_groups=mesh['z'=16,'y'=4,'x'=4,'core'=2] {'z'}, dimensions={0} | all-to-all | bytes 131072 | tf_op jit(solution)/shard_map/sum/all_to_all | solution.py:301
  82.8 14.4 %all_to_all.22 = bf16[16,1,8,128]{3,2,1,0:T(8,128)(2,1)S(1)} all-to-all(bf16[16,1,8,128]{3,2,1,0:T(8,128)(2,1)S(1)} %broadcast_in_dim.6), channel_id=1, replica_groups=mesh['z'=16,'y'=4,'x'=4,'core'=2] {'z'}, dimensions={0} | all-to-all | bytes 65536 | tf_op jit(solution)/shard_map/sum/all_to_all | solution.py:308
  97.3 0.1 broadcast_in_dim.15
  97.4 12.5 %all_to_all.23 = bf16[16,8,16,128]{3,2,1,0:T(8,128)(2,1)S(1)} all-to-all(bf16[16,8,16,128]{3,2,1,0:T(8,128)(2,1)S(1)} %broadcast_in_dim.15), channel_id=1, replica_groups=mesh['z'=16,'y'=4,'x'=4,'core'=2] {'y','x'}, dimensions={0} | all-to-all | bytes 1048576 | tf_op jit(solution)/shard_map/sum/all_to_all | solution.py:308
  109.9 6.8 %collective-permute-start.5 = (bf16[128,16,128]{2,1,0:T(8,128)(2,1)S(1)}, bf16[128,16,128]{2,1,0:T(8,128)(2,1)S(1)}, u32[]{:S(2)}, u32[]{:S(2)}) collective-permute-start(bf16[128,16,128]{2,1,0:T(8,128)(2,1)S(1)} %bitcast.7), channel_id=1, source_target_pairs={{0,1},{1,0},{2,3},{3,2},{4,5},{5,4},{6,7},{7,6},{8,9},{9,8},{10,11... | collective-permute-start | bytes 1572872 | tf_op jit(solution)/shard_map/sum/ppermute | solution.py:360
  116.8 3.7 %outputs.1 = (bf16[1,96,512]{2,1,0:T(8,128)(2,1)}, bf16[1,96,512]{2,1,0:T(8,128)(2,1)}) custom-call(bf16[208,1920]{1,0:T(8,128)(2,1)S(1)} %get-tuple-element.29.padded, bf16[96,1536]{1,0:T(8,128)(2,1)S(1)} %get-tuple-element.30.hidden, bf16[96,1536]{1,0:T(8,128)(2,1)S(1)} %copy-done.5, bf16[1152,512]{1,0:T(8,128)(2,1)S(1)} %copy-done, ...), custom_call_target="tpu_custom_call" | custom-call | tf_op jit(solution)/shard_map/outputs/pallas_call | solution.py:362
  120.5 2.0 %unpack.1 = (f32[96,2592]{1,0:T(8,128)}, f32[96,2592]{1,0:T(8,128)}) custom-call(s32[2]{0:T(128)S(1)} %pad_add_fusion.own, bf16[128,16,128]{2,1,0:T(8,128)(2,1)S(1)} %bitcast.8, bf16[128,16,128]{2,1,0:T(8,128)(2,1)S(1)} %collective-permute-done.5.other), custom_call_target="tpu_custom_call" | custom-call | tf_op jit(solution)/shard_map/unpack/pallas_call | solution.py:369
  (20 shorter events, 0.1 us)
Async XLA Ops:
  0.6 11.8 %copy-start.1 = (bf16[768,512]{1,0:T(8,128)(2,1)S(1)}, bf16[768,512]{1,0:T(8,128)(2,1)}, u32[]{:S(2)}) copy-start(bf16[768,512]{1,0:T(8,128)(2,1)} %constant.27.clone.picks) | copy-start | bytes 2359300
  0.6 1.0 copy-start.7
  1.6 0.9 copy-start.8
  2.5 0.7 copy-start.10
  3.5 8.8 %collective-permute-start = (bf16[208,128]{1,0:T(8,128)(2,1)S(1)}, bf16[208,128]{1,0:T(8,128)(2,1)S(1)}, u32[]{:S(2)}, u32[]{:S(2)}) collective-permute-start(bf16[208,128]{1,0:T(8,128)(2,1)S(1)} %get-tuple-element.23), channel_id=1, source_target_pairs={{0,8},{8,16},{16,24},{24,32},{32,40},{40,48},{48,56},{64,72},{72,8... | collective-permute-start | bytes 159752 | tf_op jit(solution)/shard_map/rims_x/ppermute | solution.py:297
  7.5 4.9 %collective-permute-start.1 = (bf16[208,128]{1,0:T(8,128)(2,1)S(1)}, bf16[208,128]{1,0:T(8,128)(2,1)S(1)}, u32[]{:S(2)}, u32[]{:S(2)}) collective-permute-start(bf16[208,128]{1,0:T(8,128)(2,1)S(1)} %get-tuple-element.24), channel_id=1, source_target_pairs={{8,0},{16,8},{24,16},{32,24},{40,32},{48,40},{56,48},{72,64},{80,7... | collective-permute-start | bytes 159752 | tf_op jit(solution)/shard_map/rims_x/ppermute | solution.py:297
  8.8 1.0 copy-start.2
  9.9 1.0 copy-start.3
  10.9 14.9 %copy-start.6 = (s32[16,1920]{1,0:T(8,128)S(1)}, s32[16,1920]{1,0:T(8,128)}, u32[]{:S(2)}) copy-start(s32[16,1920]{1,0:T(8,128)} %constant.28.clone.table) | copy-start | bytes 368644
  10.9 14.9 %copy-start.9 = (f32[8,1536]{1,0:T(8,128)S(1)}, f32[8,1536]{1,0:T(8,128)}, u32[]{:S(2)}) copy-start(f32[8,1536]{1,0:T(8,128)} %constant.29.clone.marks) | copy-start | bytes 147460
  10.9 14.9 %copy-start.11 = (s32[1,27]{1,0:T(1,128)S(1)}, s32[1,27]{1,0:T(1,128)}, u32[]{:S(2)}) copy-start(s32[1,27]{1,0:T(1,128)} %adj.1) | copy-start | bytes 328
  12.8 6.6 %collective-permute-start.2 = (bf16[208,256]{1,0:T(8,128)(2,1)S(1)}, bf16[208,256]{1,0:T(8,128)(2,1)S(1)}, u32[]{:S(2)}, u32[]{:S(2)}) collective-permute-start(bf16[208,256]{1,0:T(8,128)(2,1)S(1)} %get-tuple-element.25), channel_id=1, source_target_pairs={{0,64},{8,72},{16,80},{24,88},{32,96},{40,104},{48,112},{56,120},{... | collective-permute-start | bytes 319496 | tf_op jit(solution)/shard_map/rims_y/ppermute | solution.py:297
  17.7 8.2 %collective-permute-start.3 = (bf16[208,256]{1,0:T(8,128)(2,1)S(1)}, bf16[208,256]{1,0:T(8,128)(2,1)S(1)}, u32[]{:S(2)}, u32[]{:S(2)}) collective-permute-start(bf16[208,256]{1,0:T(8,128)(2,1)S(1)} %get-tuple-element.26), channel_id=1, source_target_pairs={{64,0},{72,8},{80,16},{88,24},{96,32},{104,40},{112,48},{120,56},{... | collective-permute-start | bytes 319496 | tf_op jit(solution)/shard_map/rims_y/ppermute | solution.py:297
  33.0 7.6 %copy-start.4 = (bf16[96,1536]{1,0:T(8,128)(2,1)}, bf16[96,1536]{1,0:T(8,128)(2,1)S(1)}, u32[]{:S(2)}) copy-start(bf16[96,1536]{1,0:T(8,128)(2,1)S(1)} %get-tuple-element.31.grad_one) | copy-start | bytes 884740
  33.0 7.4 %collective-permute-start.4 = (f32[128,16,128]{2,1,0:T(8,128)S(1)}, f32[128,16,128]{2,1,0:T(8,128)S(1)}, u32[]{:S(2)}, u32[]{:S(2)}) collective-permute-start(f32[128,16,128]{2,1,0:T(8,128)S(1)} %get-tuple-element.37), channel_id=1, source_target_pairs={{0,1},{1,0},{2,3},{3,2},{4,5},{5,4},{6,7},{7,6},{8,9},{9,8},{10,11... | collective-permute-start | bytes 3145736 | tf_op jit(solution)/shard_map/sum/ppermute | solution.py:355
  60.5 56.2 %copy-start = (bf16[1152,512]{1,0:T(8,128)(2,1)S(1)}, bf16[1152,512]{1,0:T(8,128)(2,1)}, u32[]{:S(2)}) copy-start(bf16[1152,512]{1,0:T(8,128)(2,1)} %constant.30.clone.squeeze) | copy-start | bytes 3538948
  82.8 33.9 %copy-start.5 = (bf16[96,1536]{1,0:T(8,128)(2,1)S(1)}, bf16[96,1536]{1,0:T(8,128)(2,1)}, u32[]{:S(2)}) copy-start(bf16[96,1536]{1,0:T(8,128)(2,1)} %copy-done.4) | copy-start | bytes 884740
  109.9 10.6 %collective-permute-start.5 = (bf16[128,16,128]{2,1,0:T(8,128)(2,1)S(1)}, bf16[128,16,128]{2,1,0:T(8,128)(2,1)S(1)}, u32[]{:S(2)}, u32[]{:S(2)}) collective-permute-start(bf16[128,16,128]{2,1,0:T(8,128)(2,1)S(1)} %bitcast.7), channel_id=1, source_target_pairs={{0,1},{1,0},{2,3},{3,2},{4,5},{5,4},{6,7},{7,6},{8,9},{9,8},{10,11... | collective-permute-start | bytes 1572872 | tf_op jit(solution)/shard_map/sum/ppermute | solution.py:360

commit v3 on v2

v3 whole, which is shorter than its diff:
```python
import jax
import jax.numpy as jnp
import numpy as np
from jax import lax
from jax.experimental import pallas as pl
from jax.experimental.pallas import tpu as pltpu
from jax.sharding import Mesh, PartitionSpec as P

C = 96
BE = 8
GRID = 8
REPS = 8
ROWS = 208
PAD = 12
LANES = 1920
OUTER = 1536
INNER = 1152
BASE = PAD * PAD + PAD
TILES_L = 21
DIRECTIONS = [(-1, -1), (0, -1), (1, -1), (-1, 0), (1, 0), (-1, 1), (0, 1), (1, 1)]
OFFSETS = [(a, b, c) for a in (-1, 0, 1) for b in (-1, 0, 1) for c in (-1, 0, 1)]
F32, BF16 = jnp.float32, jnp.bfloat16


def place_table():
    table = np.full((16, LANES), -1, np.int32)
    table[0] = 27
    for p in range(PAD**3):
        at = (p // (PAD * PAD) - 2, p // PAD % PAD - 2, p % PAD - 2)
        site = [(-1 if a < 0 else 1 if a >= BE else 0) for a in at]
        x, y, z = (a % BE for a in at)
        table[0, p] = (site[0] + 1) * 9 + (site[1] + 1) * 3 + site[2] + 1
        table[1, p] = x * 64 + y * 8 + z
        for number, (sx, sy) in enumerate(DIRECTIONS):
            nx = x - 6 if sx < 0 else x
            ny = y - 6 if sy < 0 else y
            if sx != 0 and not 0 <= nx < 2 or sy != 0 and not 0 <= ny < 2:
                continue
            if sx == 0:
                place = 512 + x * 16 + ny * 8 + z
            elif sy == 0:
                place = 640 + nx * 64 + y * 8 + z
            else:
                place = (768 if sy < 0 else 800) + nx * 16 + ny * 8 + z
            table[2 + number, p] = place
    return table


def ints(dims, axis):
    return lax.broadcasted_iota(jnp.int32, dims, axis)


def pack_kernel(feats_in, cot_in, occ_in, field, down, up, feats, cot, occ, sems):
    copies = [
        pltpu.make_async_copy(source, target, sems.at[number])
        for number, (source, target) in enumerate(((occ_in, occ), (feats_in, feats), (cot_in, cot)))
    ]
    for copy in copies:
        copy.start()
    lane = ints((512, 256), 1)
    rim = lane % 128
    wanted = rim // 16 * 64 + rim // 8 % 2 * 8 + rim % 8 + jnp.where(lane < 128, 48, 0)
    picks = jnp.where(ints((512, 256), 0) == wanted, 1.0, 0.0).astype(BF16)
    copies[0].wait()
    mask = (occ[...] != 0).astype(F32).astype(BF16)
    field[2 * C :, :] = jnp.broadcast_to(mask, (ROWS - 2 * C, 512))
    copies[1].wait()
    field[0:C, :] = feats[0] * mask
    copies[2].wait()
    field[C : 2 * C, :] = cot[0] * mask
    rims = jnp.dot(field[...], picks, preferred_element_type=F32).astype(BF16)
    down[...] = rims[:, 0:128]
    up[...] = rims[:, 128:256]


def slab_kernel(field, ym, yp, left, right):
    blank = jnp.zeros((ROWS, 64), BF16)
    left[:, 0:128] = field[:, 384:512]
    left[:, 128:256] = jnp.concatenate([ym[:, 96:128], yp[:, 96:128], blank], axis=1)
    right[:, 0:128] = field[:, 0:128]
    right[:, 128:256] = jnp.concatenate([ym[:, 0:32], yp[:, 0:32], blank], axis=1)


def weight_kernel(
    first_in, second_in, first_forward, first_turned, second_forward, second_turned,
    first, second, sems,
):
    copies = [
        pltpu.make_async_copy(first_in, first, sems.at[0]),
        pltpu.make_async_copy(second_in, second, sems.at[1]),
    ]
    for copy in copies:
        copy.start()
    for copy, weight, forward, turned in (
        (copies[0], first, first_forward, first_turned),
        (copies[1], second, second_forward, second_turned),
    ):
        copy.wait()
        whole = weight[...]
        across = whole.astype(F32).T.astype(BF16)
        for number in range(9):
            for dz in range(3):
                k = number * 3 + dz
                rows = slice(dz * C, (dz + 1) * C)
                columns = slice(number * C, (number + 1) * C)
                forward[rows, columns] = whole[:, k * C : (k + 1) * C]
                turned[rows, columns] = across[(26 - k) * C : (27 - k) * C, :]


def shifted_columns(source, columns, length):
    for number in range(9):
        start = (number // 3) * PAD * PAD + (number % 3) * PAD
        columns[number * C : (number + 1) * C, 0:length] = source[:, start : start + length]


def three_taps(weight, columns, length):
    parts = jnp.dot(weight[...], columns[:, 0:length], preferred_element_type=F32)
    return (
        parts[0:C]
        + pltpu.roll(parts[C : 2 * C], length - 1, 1)
        + pltpu.roll(parts[2 * C :], length - 2, 1)
    )


def weight_grad(gradient, columns, length, grads, tiles):
    stack = jnp.concatenate(
        [gradient, pltpu.roll(gradient, 1, 1), pltpu.roll(gradient, 2, 1)], axis=0
    ).astype(BF16)
    sums = lax.dot_general(
        stack, columns[:, 0:length], (((1,), (1,)), ((), ())), preferred_element_type=F32
    ) * (1.0 / 512.0)
    for number in range(9):
        for dz in range(3):
            k = number * 3 + dz
            grads[:, k * C : (k + 1) * C] = sums[
                dz * C : (dz + 1) * C, number * C : (number + 1) * C
            ]
    grads[:, 27 * C :] = jnp.zeros((C, TILES_L * 128 - 27 * C), F32)
    for tile in range(6 * TILES_L):
        row, lane = tile // TILES_L * 16, tile % TILES_L * 128
        tiles[tile] = grads[row : row + 16, lane : lane + 128]
    tiles[6 * TILES_L :] = jnp.zeros((128 - 6 * TILES_L, 16, 128), F32)


def first_grad(padded, grad_one, table, columns, grads, tiles):
    own = table[0:1, BASE + 1 : BASE + 1 + OUTER] == 13
    weight_grad(jnp.where(own, grad_one[...].astype(F32), 0.0), columns, OUTER, grads, tiles)


def second_grad(padded, grad_one, table, columns, grads, tiles):
    start = 2 * (BASE + 1)
    own = table[0:1, start : start + INNER] == 13
    grad_two = padded[C : 2 * C, start : start + INNER].astype(F32)
    weight_grad(jnp.where(own, grad_two, 0.0), columns, INNER, grads, tiles)


def relative_owners(adj, own):
    owners = [adj[0, k] for k in range(27)]
    return [jnp.where(block < 0, 99, block // REPS - own[0]) for block in owners]


def among(relative, steps):
    found = relative[0] == steps[0]
    for value in relative:
        for step in steps:
            found = jnp.logical_or(found, value == step)
    return found


def place_kernel(adj, own, field, ym, yp, table, base, hot_x, sources):
    relative = relative_owners(adj, own)
    from_low = among(relative, [-GRID])
    sources[:, 0:512] = field[...]

    @pl.when(from_low)
    def _():
        sources[:, 512:640] = ym[...]

    @pl.when(jnp.logical_not(from_low))
    def _():
        sources[:, 512:640] = yp[...]

    site = table[0:1, :]
    which = jnp.full((1, LANES), 99, jnp.int32)
    for k in range(27):
        which = jnp.where(site == k, relative[k], which)
    place = jnp.where(which == 0, table[1:2, :], -1)
    for number, (sx, sy) in enumerate(DIRECTIONS):
        place = jnp.where(which == sx + GRID * sy, table[number + 2 : number + 3, :], place)
    width = 384
    for part in range(LANES // width):
        cut = slice(part * width, (part + 1) * width)
        hot = jnp.where(ints((896, width), 0) == place[:, cut], 1.0, 0.0).astype(BF16)
        hot_x[:, cut] = hot[640:896]
        base[:, cut] = jnp.dot(
            sources[...], hot[0:640], preferred_element_type=F32
        ).astype(BF16)


def main_kernel(
    adj, own, xm, xp, base, hot_x, table, w_one, w_two,
    send, padded, hidden, grad_one, col_m, col_h,
    slab, col_g, grads,
):
    from_left = among(relative_owners(adj, own), [-1 - GRID, -1, -1 + GRID])

    @pl.when(from_left)
    def _():
        slab[...] = xm[...]

    @pl.when(jnp.logical_not(from_left))
    def _():
        slab[...] = xp[...]

    width = 384
    for part in range(LANES // width):
        cut = slice(part * width, (part + 1) * width)
        near = jnp.dot(slab[...], hot_x[:, cut], preferred_element_type=F32)
        padded[:, cut] = (base[:, cut].astype(F32) + near).astype(BF16)
    shifted_columns(padded[0:C, :], col_m, OUTER)
    shifted_columns(padded[C : 2 * C, :], col_g, OUTER)
    mask = padded[2 * C : 2 * C + 1, BASE + 1 : BASE + 1 + OUTER].astype(F32)
    pre = three_taps(w_one, col_m, OUTER)
    sig = jax.nn.sigmoid(pre)
    hidden[...] = (pre * sig * mask).astype(BF16)
    back = three_taps(w_two, col_g, OUTER)
    grad_one[...] = (back * mask * sig * (1.0 + pre * (1.0 - sig))).astype(BF16)
    shifted_columns(hidden[...], col_h, INNER)

    @pl.when(own[1] == 0)
    def _():
        second_grad(padded, grad_one, table, col_h, grads, send)

    @pl.when(own[1] != 0)
    def _():
        first_grad(padded, grad_one, table, col_m, grads, send)


def keep_kernel(own, padded, grad_one, table, col_m, col_h, keep, grads):
    @pl.when(own[1] == 0)
    def _():
        first_grad(padded, grad_one, table, col_m, grads, keep)

    @pl.when(own[1] != 0)
    def _():
        second_grad(padded, grad_one, table, col_h, grads, keep)


def out_kernel(after, padded, hidden, grad_one, w_two, w_one, out_feats, grad_feats, done, columns):
    done[...] = jnp.zeros((8, 128), F32)
    voxel = ints((INNER, 512), 1)
    inner = voxel // 64 * (PAD * PAD) + voxel // 8 % 8 * PAD + voxel % 8
    squeeze = jnp.where(ints((INNER, 512), 0) == inner, 1.0, 0.0).astype(BF16)
    start = 2 * (BASE + 1)
    mask = padded[2 * C : 2 * C + 1, start : start + INNER].astype(F32)
    for first, field, weight, out in (
        (0, hidden, w_two, out_feats),
        (C, grad_one, w_one, grad_feats),
    ):
        shifted_columns(field[...], columns, INNER)
        pre = three_taps(weight, columns, INNER)
        kept = padded[first : first + C, start : start + INNER].astype(F32)
        wide = (kept + pre * mask).astype(BF16)
        out[0] = jnp.dot(wide, squeeze, preferred_element_type=F32).astype(BF16)


def share_kernel(count, parts, *refs):
    total = parts[0].astype(F32)
    for number in range(1, count):
        total = total + parts[number].astype(F32)
    copies = refs[-1]
    for number in range(copies.shape[0]):
        copies[number] = total.astype(BF16)


def write_half(half, out, rows, sems):
    copies = []
    for row in range(6):
        for lane in range(TILES_L):
            last = min((lane + 1) * 128, 27 * C)
            part = half[row * TILES_L + lane].astype(F32)
            rows[row * 16 : row * 16 + 16, lane * 128 : last] = part[:, : last - lane * 128]
        at = pl.ds(row * 16, 16)
        copies.append(pltpu.make_async_copy(rows.at[at], out.at[at], sems.at[row]))
        copies[-1].start()
    for copy in copies:
        copy.wait()


def mine_kernel(own, half, first, second, rows, sems):
    @pl.when(own[1] == 0)
    def _():
        write_half(half, first, rows, sems)

    @pl.when(own[1] != 0)
    def _():
        write_half(half, second, rows, sems)


def other_kernel(own, half, first_in, second_in, first, second, rows, sems):
    @pl.when(own[1] == 0)
    def _():
        write_half(half, second, rows, sems)

    @pl.when(own[1] != 0)
    def _():
        write_half(half, first, rows, sems)


VMEM = pl.BlockSpec(memory_space=pltpu.VMEM)
SMEM = pl.BlockSpec(memory_space=pltpu.SMEM)
HBM = pl.BlockSpec(memory_space=pltpu.HBM)
ANY = pl.BlockSpec(memory_space=pl.ANY)
DMA = pltpu.SemaphoreType.DMA
MIB = 1024 * 1024


def call(kernel, outs, specs, scratch=(), place=VMEM, limit=40 * MIB, **options):
    return pl.pallas_call(
        kernel,
        out_shape=[jax.ShapeDtypeStruct(*out) for out in outs],
        in_specs=specs,
        out_specs=[place] * len(outs),
        scratch_shapes=scratch,
        compiler_params=pltpu.CompilerParams(vmem_limit_bytes=limit),
        **options,
    )


def from_owner(value, sx, sy):
    pairs = []
    for owner in range(GRID * GRID):
        column, row = owner % GRID + sx, owner // GRID + sy
        if 0 <= column < GRID and 0 <= row < GRID:
            pairs.append((row * GRID + column, owner))
    return lax.ppermute(value, ("zh", "zl", "y"), pairs)


def swap_halves(value):
    return lax.ppermute(value, "core", [(0, 1), (1, 0)])


def body(feats, cotangent, occupancy, counts, adjacency, w_first, w_second):
    own = jnp.stack([lax.axis_index(("zh", "zl", "y")), lax.axis_index("core")]).astype(jnp.int32)
    table = jnp.asarray(place_table())
    rim, slab, turned = ((ROWS, 128), BF16), ((ROWS, 256), BF16), ((3 * C, 9 * C), BF16)
    vmem = pltpu.VMEM
    with jax.named_scope("pack"):
        field, down, up = call(
            pack_kernel,
            [((ROWS, 512), BF16), rim, rim],
            [HBM] * 3,
            [vmem((1, C, 512), BF16)] * 2 + [vmem((1, 512), jnp.int32), DMA((3,))],
        )(feats, cotangent, occupancy)
    with jax.named_scope("weights"):
        one_f, one_b, two_f, two_b = call(
            weight_kernel, [turned] * 4, [HBM] * 2, [vmem((C, 27 * C), BF16)] * 2 + [DMA((2,))],
        )(w_first, w_second)
    with jax.named_scope("rims_y"):
        ym, yp = from_owner(down, 0, -1), from_owner(up, 0, 1)
    with jax.named_scope("slabs"):
        left, right = call(slab_kernel, [slab, slab], [VMEM] * 3)(field, ym, yp)
    with jax.named_scope("rims_x"):
        xm, xp = from_owner(left, -1, 0), from_owner(right, 1, 0)
    with jax.named_scope("place"):
        base, hot_x = call(
            place_kernel,
            [((ROWS, LANES), BF16), ((256, LANES), BF16)],
            [SMEM] * 2 + [VMEM] * 4,
            [vmem((ROWS, 640), BF16)],
        )(adjacency, own, field, ym, yp, table)
    half, grads = ((128, 16, 128), F32), vmem((C, TILES_L * 128), F32)
    with jax.named_scope("middle"):
        send, padded, hidden, grad_one, col_m, col_h = call(
            main_kernel,
            [
                half, ((ROWS, LANES), BF16), ((C, OUTER), BF16), ((C, OUTER), BF16),
                ((9 * C, OUTER), BF16), ((9 * C, INNER), BF16),
            ],
            [SMEM] * 2 + [VMEM] * 7,
            [vmem((ROWS, 256), BF16), vmem((9 * C, OUTER), BF16), grads],
        )(adjacency, own, xm, xp, base, hot_x, table, one_f, two_b)
    with jax.named_scope("keep"):
        (keep,) = call(keep_kernel, [half], [SMEM] + [VMEM] * 5, [grads])(
            own, padded, grad_one, table, col_m, col_h
        )
    with jax.named_scope("pair"):
        pair = keep + swap_halves(send)
    with jax.named_scope("outputs"):
        out_feats, grad_feats, done = call(
            out_kernel,
            [((1, C, 512), BF16)] * 2 + [((8, 128), F32)],
            [ANY] + [VMEM] * 5,
            [vmem((9 * C, INNER), BF16)],
        )(pair, padded, hidden, grad_one, two_f, one_b)
    near, far = ("zl", "y", "x"), "zh"
    with jax.named_scope("sum"):
        parts = lax.all_to_all(pair, near, 0, 0, tiled=True).reshape(32, 4, 16, 128)
        (copies,) = call(
            lambda *refs: share_kernel(32, *refs), [((8, 4, 16, 128), BF16)], [VMEM] * 2
        )(parts, done)
        parts = lax.all_to_all(copies, far, 0, 0)
        (copies,) = call(
            lambda *refs: share_kernel(8, *refs), [((32, 4, 16, 128), BF16)], [VMEM]
        )(parts)
        mine = lax.all_to_all(copies, near, 0, 0).reshape(128, 16, 128)
        other = swap_halves(mine)
    grad, rows = ((C, 27 * C), F32), [vmem((C, 27 * C), F32), DMA((6,))]
    with jax.named_scope("mine"):
        begun = call(mine_kernel, [grad] * 2, [SMEM, VMEM], rows, place=ANY)(own, mine)
    with jax.named_scope("other"):
        grad_first, grad_second = call(
            other_kernel, [grad] * 2, [SMEM, VMEM, ANY, ANY], rows, place=ANY,
            input_output_aliases={2: 0, 3: 1},
        )(own, other, *begun)
    return out_feats, grad_feats, grad_first, grad_second


def solution(mesh):
    fine = Mesh(mesh.devices.reshape(8, 2, 4, 4, 2), ("zh", "zl", "y", "x", "core"))
    both = ("zh", "zl", "y", "x", "core")
    blocks = P(both, None, None)
    rows = P(both, None)
    return jax.shard_map(
        body,
        mesh=fine,
        in_specs=(blocks, blocks, rows, rows, rows, P(), P()),
        out_specs=(blocks, blocks, P(), P()),
        check_vma=False,
    )
```

time: 123 us -> 117 us (0.951)
  blocking collectives: 69.2 us -> 40.9 us
  starting transfers between devices: 23.5 us -> 31 us
  Pallas kernels: 14.8 us -> 21.1 us
  waiting for transfers between devices: 9.18 us -> 13.8 us
  local copies, waits for them, and re-layouts: 4.73 us -> 6.99 us
    all_to_all x4 -> x2, blocking collectives: 69.2 us -> 40.9 us  [the longest x1 26.2 us: body(): parts = lax.all_to_all(copies, far, 0, 0)]
    all_to_all x0 -> x1, waiting for transfers between devices: none -> 11.3 us  [body(): parts = lax.all_to_all(pair, near, 0, 0, tiled=True).reshape(32, 4, 16, 128)]
    all_to_all x0 -> x1, starting transfers between devices: none -> 8.4 us  [body(): parts = lax.all_to_all(pair, near, 0, 0, tiled=True).reshape(32, 4, 16, 128)]
    ppermute x6, waiting for transfers between devices: 9.18 us -> 2.48 us  [the longest x4 2.48 us: from_owner(): return lax.ppermute(value, ('zh', 'zl', 'y'), pairs)]
    pallas_call x6 -> x11, Pallas kernels: 14.8 us -> 21.1 us  [the longest x1 6.56 us: body(): call(main_kernel, [half, ((ROWS, LANES), BF16), ((C, OUTER), BF16), ((C,...]
    unnamed x24 -> x16, local copies, waits for them, and re-layouts: 4.63 us -> 6.99 us
  transfers between devices with their start and end apart: 6 -> 7, of which waited for: 4 -> 3; matrix products, arithmetic and copies ran while one was open for 0% -> 0% of each run, Pallas kernels for 4% -> 10%
where the time goes in v3:
time: 117 us; the launch traced here: 116 us
  blocking collectives  40.9 us (35%)
  starting transfers between devices  31 us (26%)
  Pallas kernels  21.1 us (18%)
  waiting for transfers between devices  13.8 us (12%)
  local copies, waits for them, and re-layouts  6.99 us (6%)
  other arithmetic  1.21 us (1%)
    all_to_all x1, blocking collectives, body(): parts = lax.all_to_all(copies, far, 0, 0)  26.2 us
    all_to_all x1, blocking collectives, body(): mine = lax.all_to_all(copies, near, 0, 0).reshape(128, 16, 128)  14.7 us
    ppermute x4, starting transfers between devices, from_owner(): return lax.ppermute(value, ('zh', 'zl', 'y'), pairs)  11.5 us
    all_to_all x1, waiting for transfers between devices, body(): parts = lax.all_to_all(pair, near, 0, 0, tiled=True).reshape(32, 4, 16, 128)  11.3 us
    ppermute x2, starting transfers between devices, swap_halves(): return lax.ppermute(value, 'core', [(0, 1), (1, 0)])  11.1 us
    all_to_all x1, starting transfers between devices, body(): parts = lax.all_to_all(pair, near, 0, 0, tiled=True).reshape(32, 4, 16, 128)  8.4 us
    unnamed x16, local copies, waits for them, and re-layouts  6.99 us
    pallas_call x1, Pallas kernels, body(): call(main_kernel, [half, ((ROWS, LANES), BF16), ((C, OUTER), BF16), ((C,...  6.56 us
  transfers between devices with their start and end apart: 7, of which 3 were waited for; matrix products, arithmetic and copies ran while one was open for 0% of the time, Pallas kernels for 10%

profile of v3, /device:TPU:1, one launch (start us, length us, event | category | flops | bytes accessed | tf_op | source)
XLA Modules:
  0.0 115.9 jit_solution(10588789455723733613)
XLA Ops:
  0.6 0.9 copy-done.4
  1.5 0.9 copy-done.5
  2.4 0.7 copy-done.6
  3.1 0.6 pack.1
  3.7 5.7 %collective-permute-start = (bf16[208,128]{1,0:T(8,128)(2,1)S(1)}, bf16[208,128]{1,0:T(8,128)(2,1)S(1)}, u32[]{:S(2)}, u32[]{:S(2)}) collective-permute-start(bf16[208,128]{1,0:T(8,128)(2,1)S(1)} %get-tuple-element.29), channel_id=1, source_target_pairs={{0,64},{8,72},{16,80},{24,88},{32,96},{40,104},{48,112},{56,120},{... | collective-permute-start | bytes 159752 | tf_op jit(solution)/shard_map/rims_y/ppermute | solution.py:336
  9.4 1.3 %collective-permute-start.1 = (bf16[208,128]{1,0:T(8,128)(2,1)S(1)}, bf16[208,128]{1,0:T(8,128)(2,1)S(1)}, u32[]{:S(2)}, u32[]{:S(2)}) collective-permute-start(bf16[208,128]{1,0:T(8,128)(2,1)S(1)} %get-tuple-element.30), channel_id=1, source_target_pairs={{64,0},{72,8},{80,16},{88,24},{96,32},{104,40},{112,48},{120,56},{... | collective-permute-start | bytes 159752 | tf_op jit(solution)/shard_map/rims_y/ppermute | solution.py:336
  10.7 1.0 copy-done.2
  11.8 1.0 copy-done.3
  12.8 2.2 %weights.1 = (bf16[288,864]{1,0:T(8,128)(2,1)S(1)}, bf16[288,864]{1,0:T(8,128)(2,1)S(1)}, bf16[288,864]{1,0:T(8,128)(2,1)S(1)}, bf16[288,864]{1,0:T(8,128)(2,1)S(1)}) custom-call(bf16[96,2592]{1,0:T(8,128)(2,1)S(1)} %copy-done.2, bf16[96,2592]{1,0:T(8,128)(2,1)S(1)} %copy-done.3), custom_call_target="tpu_custom_call" | custom-call | tf_op jit(solution)/shard_map/weights/pallas_call | solution.py:356
  15.0 2.0 %collective-permute-done.1.yp = bf16[208,128]{1,0:T(8,128)(2,1)S(1)} collective-permute-done((bf16[208,128]{1,0:T(8,128)(2,1)S(1)}, bf16[208,128]{1,0:T(8,128)(2,1)S(1)}, u32[]{:S(2)}, u32[]{:S(2)}) %collective-permute-start.1) | collective-permute-done | bytes 53280 | tf_op jit(solution)/shard_map/rims_y/ppermute | solution.py:336
  17.0 0.1 slabs.1
  17.2 3.2 %collective-permute-start.2 = (bf16[208,256]{1,0:T(8,128)(2,1)S(1)}, bf16[208,256]{1,0:T(8,128)(2,1)S(1)}, u32[]{:S(2)}, u32[]{:S(2)}) collective-permute-start(bf16[208,256]{1,0:T(8,128)(2,1)S(1)} %get-tuple-element.31), channel_id=1, source_target_pairs={{0,8},{8,16},{16,24},{24,32},{32,40},{40,48},{48,56},{64,72},{72,8... | collective-permute-start | bytes 319496 | tf_op jit(solution)/shard_map/rims_x/ppermute | solution.py:336
  20.4 1.3 %collective-permute-start.3 = (bf16[208,256]{1,0:T(8,128)(2,1)S(1)}, bf16[208,256]{1,0:T(8,128)(2,1)S(1)}, u32[]{:S(2)}, u32[]{:S(2)}) collective-permute-start(bf16[208,256]{1,0:T(8,128)(2,1)S(1)} %get-tuple-element.32), channel_id=1, source_target_pairs={{8,0},{16,8},{24,16},{32,24},{40,32},{48,40},{56,48},{72,64},{80,7... | collective-permute-start | bytes 319496 | tf_op jit(solution)/shard_map/rims_x/ppermute | solution.py:336
  21.7 0.1 pad_add_fusion.own
  21.8 0.9 copy-done
  22.7 0.7 copy-done.7
  23.3 2.1 %place.1 = (bf16[208,1920]{1,0:T(8,128)(2,1)S(1)}, bf16[256,1920]{1,0:T(8,128)(2,1)S(1)}) custom-call(s32[1,27]{1,0:T(1,128)S(1)} %copy-done.7, s32[2]{0:T(128)S(1)} %pad_add_fusion.own, bf16[208,512]{1,0:T(8,128)(2,1)S(1)} %get-tuple-element.28.field, bf16[208,128]{1,0:T(8,128)(2,1)S(1)} %collective-permute-done.ym, ...), custom_call_target="tpu_custom_call" | custom-call | tf_op jit(solution)/shard_map/place/pallas_call | solution.py:366
  25.4 0.4 collective-permute-done.3.xp
  25.8 0.9 copy-done.1
  26.7 6.6 %middle.1 = (f32[128,16,128]{2,1,0:T(8,128)S(1)}, bf16[208,1920]{1,0:T(8,128)(2,1)S(1)}, bf16[96,1536]{1,0:T(8,128)(2,1)S(1)}, bf16[96,1536]{1,0:T(8,128)(2,1)S(...) custom-call(s32[1,27]{1,0:T(1,128)S(1)} %copy-done.7, s32[2]{0:T(128)S(1)} %pad_add_fusion.own, ...), custom_call_target="tpu_custom_call" | custom-call | tf_op jit(solution)/shard_map/middle/pallas_call | solution.py:374
  33.3 5.3 %collective-permute-start.4 = (f32[128,16,128]{2,1,0:T(8,128)S(1)}, f32[128,16,128]{2,1,0:T(8,128)S(1)}, u32[]{:S(2)}, u32[]{:S(2)}) collective-permute-start(f32[128,16,128]{2,1,0:T(8,128)S(1)} %get-tuple-element.41), channel_id=1, source_target_pairs={{0,1},{1,0},{2,3},{3,2},{4,5},{5,4},{6,7},{7,6},{8,9},{9,8},{10,11... | collective-permute-start | bytes 3145736 | tf_op jit(solution)/shard_map/pair/ppermute | solution.py:340
  38.6 2.5 %keep.1 = f32[128,16,128]{2,1,0:T(8,128)S(1)} custom-call(s32[2]{0:T(128)S(1)} %pad_add_fusion.own, bf16[208,1920]{1,0:T(8,128)(2,1)S(1)} %get-tuple-element.37.padded, bf16[96,1536]{1,0:T(8,128)(2,1)S(1)} %get-tuple-element.38.grad_one, s32[16,1920]{1,0:T(8,128)S(1)} %copy-done.1, bf16[864,1536]{1,0:T(8,128)(2,1)S(1)} %get-tuple-element.39.col_m, ...), custom_call_target="tpu_custom_call" | custom-call | tf_op jit(solution)/shard_map/keep/pallas_call | solution.py:384
  41.2 1.1 add.11.after
  42.3 8.4 %all-to-all-start = ((f32[128,16,128]{2,1,0:T(8,128)}), f32[128,16,128]{2,1,0:T(8,128)S(1)}, u32[]{:S(2)}, u32[]{:S(2)}) async-start(f32[128,16,128]{2,1,0:T(8,128)} %add.11.after), calls=%async_computation | async-start | bytes 2097152 | tf_op jit(solution)/shard_map/sum/all_to_all | solution.py:398
  50.7 3.8 %outputs.1 = (bf16[1,96,512]{2,1,0:T(8,128)(2,1)}, bf16[1,96,512]{2,1,0:T(8,128)(2,1)}, f32[8,128]{1,0:T(8,128)S(1)}) custom-call(f32[128,16,128]{2,1,0:T(8,128)} %add.11.after, bf16[208,1920]{1,0:T(8,128)(2,1)S(1)} %get-tuple-element.37.padded, bf16[96,1536]{1,0:T(8,128)(2,1)S(1)} %get-tuple-element.42.hidden, ...), custom_call_target="tpu_custom_call" | custom-call | tf_op jit(solution)/shard_map/outputs/pallas_call | solution.py:390
  54.5 11.3 %all-to-all-done = f32[128,16,128]{2,1,0:T(8,128)S(1)} async-done(((f32[128,16,128]{2,1,0:T(8,128)}), f32[128,16,128]{2,1,0:T(8,128)S(1)}, u32[]{:S(2)}, u32[]{:S(2)}) %all-to-all-start) | async-done | bytes 1048608 | tf_op jit(solution)/shard_map/sum/all_to_all | solution.py:398
  65.8 0.1 sum.2
  65.9 26.2 %all_to_all.15.refs_0_ = bf16[8,4,16,128]{3,2,1,0:T(8,128)(2,1)S(1)} all-to-all(bf16[8,4,16,128]{3,2,1,0:T(8,128)(2,1)S(1)} %sum.2), channel_id=1, replica_groups=mesh['zh'=8,'zl'=2,'y'=4,'x'=4,'core'=2] {'zh'}, dimensions={0} | all-to-all | bytes 262144 | tf_op jit(solution)/shard_map/sum/all_to_all | solution.py:402
  92.1 14.7 %all_to_all.16 = bf16[32,4,16,128]{3,2,1,0:T(8,128)(2,1)S(1)} all-to-all(bf16[32,4,16,128]{3,2,1,0:T(8,128)(2,1)S(1)} %sum.3), channel_id=1, replica_groups=mesh['zh'=8,'zl'=2,'y'=4,'x'=4,'core'=2] {'zl','y','x'}, dimensions={0} | all-to-all | bytes 1048576 | tf_op jit(solution)/shard_map/sum/all_to_all | solution.py:406
  106.8 5.7 %collective-permute-start.5 = (bf16[128,16,128]{2,1,0:T(8,128)(2,1)S(1)}, bf16[128,16,128]{2,1,0:T(8,128)(2,1)S(1)}, u32[]{:S(2)}, u32[]{:S(2)}) collective-permute-start(bf16[128,16,128]{2,1,0:T(8,128)(2,1)S(1)} %bitcast.5), channel_id=1, source_target_pairs={{0,1},{1,0},{2,3},{3,2},{4,5},{5,4},{6,7},{7,6},{8,9},{9,8},{10,11... | collective-permute-start | bytes 1572872 | tf_op jit(solution)/shard_map/sum/ppermute | solution.py:340
  112.6 1.6 %mine.1 = (f32[96,2592]{1,0:T(8,128)}, f32[96,2592]{1,0:T(8,128)}) custom-call(s32[2]{0:T(128)S(1)} %pad_add_fusion.own, bf16[128,16,128]{2,1,0:T(8,128)(2,1)S(1)} %bitcast.6), custom_call_target="tpu_custom_call" | custom-call | tf_op jit(solution)/shard_map/mine/pallas_call | solution.py:410
  114.2 1.6 %other.1 = (f32[96,2592]{1,0:T(8,128)}, f32[96,2592]{1,0:T(8,128)}) custom-call(s32[2]{0:T(128)S(1)} %pad_add_fusion.own, bf16[128,16,128]{2,1,0:T(8,128)(2,1)S(1)} %collective-permute-done.5.half, f32[96,2592]{1,0:T(8,128)} %get-tuple-element.48.first_in, f32[96,2592]{1,0:T(8,128)} %get-tuple-element.49.second_in), custom_call_target="tpu_custom_call", output_to_operand_aliasing={{0}: (2, {}), {1}: (3, {})} | custom-call | tf_op jit(solution)/shard_map/other/pallas_call | solution.py:412
  (13 shorter events, 0.1 us)
Async XLA Ops:
  0.6 0.9 copy-start.4
  1.5 0.9 copy-start.5
  2.4 0.7 copy-start.6
  3.7 11.3 %collective-permute-start = (bf16[208,128]{1,0:T(8,128)(2,1)S(1)}, bf16[208,128]{1,0:T(8,128)(2,1)S(1)}, u32[]{:S(2)}, u32[]{:S(2)}) collective-permute-start(bf16[208,128]{1,0:T(8,128)(2,1)S(1)} %get-tuple-element.29), channel_id=1, source_target_pairs={{0,64},{8,72},{16,80},{24,88},{32,96},{40,104},{48,112},{56,120},{... | collective-permute-start | bytes 159752 | tf_op jit(solution)/shard_map/rims_y/ppermute | solution.py:336
  9.4 7.6 %collective-permute-start.1 = (bf16[208,128]{1,0:T(8,128)(2,1)S(1)}, bf16[208,128]{1,0:T(8,128)(2,1)S(1)}, u32[]{:S(2)}, u32[]{:S(2)}) collective-permute-start(bf16[208,128]{1,0:T(8,128)(2,1)S(1)} %get-tuple-element.30), channel_id=1, source_target_pairs={{64,0},{72,8},{80,16},{88,24},{96,32},{104,40},{112,48},{120,56},{... | collective-permute-start | bytes 159752 | tf_op jit(solution)/shard_map/rims_y/ppermute | solution.py:336
  10.7 1.0 copy-start.2
  11.8 1.0 copy-start.3
  17.2 8.2 %collective-permute-start.2 = (bf16[208,256]{1,0:T(8,128)(2,1)S(1)}, bf16[208,256]{1,0:T(8,128)(2,1)S(1)}, u32[]{:S(2)}, u32[]{:S(2)}) collective-permute-start(bf16[208,256]{1,0:T(8,128)(2,1)S(1)} %get-tuple-element.31), channel_id=1, source_target_pairs={{0,8},{8,16},{16,24},{24,32},{32,40},{40,48},{48,56},{64,72},{72,8... | collective-permute-start | bytes 319496 | tf_op jit(solution)/shard_map/rims_x/ppermute | solution.py:336
  20.4 5.4 %collective-permute-start.3 = (bf16[208,256]{1,0:T(8,128)(2,1)S(1)}, bf16[208,256]{1,0:T(8,128)(2,1)S(1)}, u32[]{:S(2)}, u32[]{:S(2)}) collective-permute-start(bf16[208,256]{1,0:T(8,128)(2,1)S(1)} %get-tuple-element.32), channel_id=1, source_target_pairs={{8,0},{16,8},{24,16},{32,24},{40,32},{48,40},{56,48},{72,64},{80,7... | collective-permute-start | bytes 319496 | tf_op jit(solution)/shard_map/rims_x/ppermute | solution.py:336
  21.8 0.9 copy-start
  22.7 0.7 copy-start.7
  25.8 0.9 copy-start.1
  33.3 7.9 %collective-permute-start.4 = (f32[128,16,128]{2,1,0:T(8,128)S(1)}, f32[128,16,128]{2,1,0:T(8,128)S(1)}, u32[]{:S(2)}, u32[]{:S(2)}) collective-permute-start(f32[128,16,128]{2,1,0:T(8,128)S(1)} %get-tuple-element.41), channel_id=1, source_target_pairs={{0,1},{1,0},{2,3},{3,2},{4,5},{5,4},{6,7},{7,6},{8,9},{9,8},{10,11... | collective-permute-start | bytes 3145736 | tf_op jit(solution)/shard_map/pair/ppermute | solution.py:340
  42.3 23.5 %all-to-all-start = ((f32[128,16,128]{2,1,0:T(8,128)}), f32[128,16,128]{2,1,0:T(8,128)S(1)}, u32[]{:S(2)}, u32[]{:S(2)}) async-start(f32[128,16,128]{2,1,0:T(8,128)} %add.11.after), calls=%async_computation | async-start | bytes 2097152 | tf_op jit(solution)/shard_map/sum/all_to_all | solution.py:398
  106.8 7.3 %collective-permute-start.5 = (bf16[128,16,128]{2,1,0:T(8,128)(2,1)S(1)}, bf16[128,16,128]{2,1,0:T(8,128)(2,1)S(1)}, u32[]{:S(2)}, u32[]{:S(2)}) collective-permute-start(bf16[128,16,128]{2,1,0:T(8,128)(2,1)S(1)} %bitcast.5), channel_id=1, source_target_pairs={{0,1},{1,0},{2,3},{3,2},{4,5},{5,4},{6,7},{7,6},{8,9},{9,8},{10,11... | collective-permute-start | bytes 1572872 | tf_op jit(solution)/shard_map/sum/ppermute | solution.py:340

commit v4 on v3

v4 whole, which is shorter than its diff:
```python
import jax
import jax.numpy as jnp
import numpy as np
from jax import lax
from jax.experimental import pallas as pl
from jax.experimental.pallas import tpu as pltpu
from jax.sharding import Mesh, PartitionSpec as P

C = 96
BE = 8
GRID = 8
REPS = 8
ROWS = 208
PAD = 12
LANES = 1920
OUTER = 1536
INNER = 1152
BASE = PAD * PAD + PAD
TILES_L = 21
DIRECTIONS = [(-1, -1), (0, -1), (1, -1), (-1, 0), (1, 0), (-1, 1), (0, 1), (1, 1)]
OFFSETS = [(a, b, c) for a in (-1, 0, 1) for b in (-1, 0, 1) for c in (-1, 0, 1)]
F32, BF16 = jnp.float32, jnp.bfloat16


def ints(dims, axis):
    return lax.broadcasted_iota(jnp.int32, dims, axis)


def own_voxels(first, length):
    p = ints((1, length), 1) + first
    x, y, z = p // (PAD * PAD), p // PAD % PAD, p % PAD
    inside = [jnp.logical_and(at >= 2, at < 10) for at in (x, y, z)]
    return jnp.logical_and(jnp.logical_and(inside[0], inside[1]), inside[2])


def start_inputs(feats_in, cot_in, occ_in, feats, cot, occ, sems):
    copies = [
        pltpu.make_async_copy(source, target, sems.at[number])
        for number, (source, target) in enumerate(((occ_in, occ), (feats_in, feats), (cot_in, cot)))
    ]
    for copy in copies:
        copy.start()
    return copies


def mask_inputs(copies, feats, cot, occ, field):
    copies[0].wait()
    mask = (occ[...] != 0).astype(F32).astype(BF16)
    field[2 * C :, 0:512] = jnp.broadcast_to(mask, (ROWS - 2 * C, 512))
    copies[1].wait()
    field[0:C, 0:512] = feats[0] * mask
    copies[2].wait()
    field[C : 2 * C, 0:512] = cot[0] * mask


def pack_kernel(feats_in, cot_in, occ_in, down, up, *refs):
    quarters, (field, feats, cot, occ, sems) = refs[:4], refs[4:]
    copies = start_inputs(feats_in, cot_in, occ_in, feats, cot, occ, sems)
    lane = ints((512, 256), 1)
    rim = lane % 128
    wanted = rim // 16 * 64 + rim // 8 % 2 * 8 + rim % 8 + jnp.where(lane < 128, 48, 0)
    picks = jnp.where(ints((512, 256), 0) == wanted, 1.0, 0.0).astype(BF16)
    mask_inputs(copies, feats, cot, occ, field)
    rims = jnp.dot(field[...], picks, preferred_element_type=F32).astype(BF16)
    down[...] = rims[:, 0:128]
    up[...] = rims[:, 128:256]
    for number in range(4):
        quarters[number][...] = field[:, number * 128 : (number + 1) * 128]


def slab_kernel(first, last, ym, yp, left, right):
    blank = jnp.zeros((ROWS, 64), BF16)
    left[:, 0:128] = last[...]
    left[:, 128:256] = jnp.concatenate([ym[:, 96:128], yp[:, 96:128], blank], axis=1)
    right[:, 0:128] = first[...]
    right[:, 128:256] = jnp.concatenate([ym[:, 0:32], yp[:, 0:32], blank], axis=1)


def turn_weights(copies, weights, outs):
    for copy, weight, forward, turned in zip(copies, weights, outs[0::2], outs[1::2]):
        copy.wait()
        whole = weight[...]
        across = whole.astype(F32).T.astype(BF16)
        for number in range(9):
            for dz in range(3):
                k = number * 3 + dz
                rows = slice(dz * C, (dz + 1) * C)
                columns = slice(number * C, (number + 1) * C)
                forward[rows, columns] = whole[:, k * C : (k + 1) * C]
                turned[rows, columns] = across[(26 - k) * C : (27 - k) * C, :]


def shifted_columns(source, columns, length):
    for number in range(9):
        start = (number // 3) * PAD * PAD + (number % 3) * PAD
        columns[number * C : (number + 1) * C, 0:length] = source[:, start : start + length]


def three_taps(weight, columns, length):
    parts = jnp.dot(weight[...], columns[:, 0:length], preferred_element_type=F32)
    return (
        parts[0:C]
        + pltpu.roll(parts[C : 2 * C], length - 1, 1)
        + pltpu.roll(parts[2 * C :], length - 2, 1)
    )


def weight_grad(gradient, columns, grads, tiles):
    stack = jnp.concatenate(
        [gradient, pltpu.roll(gradient, 1, 1), pltpu.roll(gradient, 2, 1)], axis=0
    ).astype(BF16)
    sums = lax.dot_general(
        stack, columns, (((1,), (1,)), ((), ())), preferred_element_type=F32
    ) * (1.0 / 512.0)
    for number in range(9):
        for dz in range(3):
            k = number * 3 + dz
            grads[:, k * C : (k + 1) * C] = sums[
                dz * C : (dz + 1) * C, number * C : (number + 1) * C
            ]
    grads[:, 27 * C :] = jnp.zeros((C, TILES_L * 128 - 27 * C), F32)
    for tile in range(6 * TILES_L):
        row, lane = tile // TILES_L * 16, tile % TILES_L * 128
        tiles[tile] = grads[row : row + 16, lane : lane + 128]
    tiles[6 * TILES_L :] = jnp.zeros((128 - 6 * TILES_L, 16, 128), F32)


def relative_owners(adj, own):
    owners = [adj[0, k] for k in range(27)]
    return [jnp.where(block < 0, 99, block // REPS - own[0]) for block in owners]


def among(relative, steps):
    found = relative[0] == steps[0]
    for value in relative:
        for step in steps:
            found = jnp.logical_or(found, value == step)
    return found


def prepare_kernel(
    adj, own, first_in, second_in,
    first_forward, first_turned, second_forward, second_turned, places, low, side,
    first, second, weight_sems,
):
    weight_copies = [
        pltpu.make_async_copy(first_in, first, weight_sems.at[0]),
        pltpu.make_async_copy(second_in, second, weight_sems.at[1]),
    ]
    for copy in weight_copies:
        copy.start()
    relative = relative_owners(adj, own)
    from_left = among(relative, [-1 - GRID, -1, -1 + GRID])
    side[...] = jnp.full(side.shape, jnp.where(from_left, 1.0, 0.0), F32).astype(BF16)
    from_low = among(relative, [-GRID])
    low[...] = jnp.full(low.shape, jnp.where(from_low, 1.0, 0.0), F32).astype(BF16)
    p = ints((1, LANES), 1)
    at = [p // (PAD * PAD) - 2, p // PAD % PAD - 2, p % PAD - 2]
    out = [jnp.where(v < 0, 0, jnp.where(v >= BE, 2, 1)) for v in at]
    site = jnp.where(p < PAD**3, out[0] * 9 + out[1] * 3 + out[2], 27)
    x, y, z = (jnp.where(v < 0, v + BE, jnp.where(v >= BE, v - BE, v)) for v in at)
    which = jnp.full((1, LANES), 99, jnp.int32)
    for k in range(27):
        which = jnp.where(site == k, relative[k], which)
    place = jnp.where(which == 0, x * 64 + y * 8 + z, -1)
    for sx, sy in DIRECTIONS:
        nx, ny = (x - 6 if sx < 0 else x), (y - 6 if sy < 0 else y)
        if sx == 0:
            there = 512 + x * 16 + ny * 8 + z
        elif sy == 0:
            there = 640 + nx * 64 + y * 8 + z
        else:
            there = (768 if sy < 0 else 800) + nx * 16 + ny * 8 + z
        place = jnp.where(which == sx + GRID * sy, there, place)
    places[...] = jnp.broadcast_to(place, places.shape)
    turn_weights(
        weight_copies, (first, second), (first_forward, first_turned, second_forward, second_turned)
    )


def either(flag, one, other):
    return one * flag + other * (1.0 - flag.astype(F32)).astype(BF16)


def place_kernel(q0, q1, q2, q3, ym, yp, places, low, base, hot_x, sources):
    for number, quarter in enumerate((q0, q1, q2, q3)):
        sources[:, number * 128 : (number + 1) * 128] = quarter[...]
    sources[:, 512:640] = either(low[0:1, :], ym[...], yp[...])
    width = 384
    for part in range(LANES // width):
        cut = slice(part * width, (part + 1) * width)
        hot = jnp.where(ints((896, width), 0) == places[0:1, cut], 1.0, 0.0).astype(BF16)
        hot_x[:, cut] = hot[640:896]
        base[:, cut] = jnp.dot(
            sources[...], hot[0:640], preferred_element_type=F32
        ).astype(BF16)


def main_kernel(
    own, xm, xp, base, hot_x, side, w_one, w_two,
    send, padded, hidden, grad_one, inner, columns,
    col_g, grads,
):
    slab = either(side[0:1, :], xm[...], xp[...])
    width = 384
    for part in range(LANES // width):
        cut = slice(part * width, (part + 1) * width)
        near = jnp.dot(slab, hot_x[:, cut], preferred_element_type=F32)
        padded[:, cut] = (base[:, cut].astype(F32) + near).astype(BF16)
    shifted_columns(padded[0:C, :], columns.at[0], OUTER)
    shifted_columns(padded[C : 2 * C, :], col_g, OUTER)
    mask = padded[2 * C : 2 * C + 1, BASE + 1 : BASE + 1 + OUTER].astype(F32)
    pre = three_taps(w_one, columns.at[0], OUTER)
    sig = jax.nn.sigmoid(pre)
    hidden[...] = (pre * sig * mask).astype(BF16)
    back = three_taps(w_two, col_g, OUTER)
    grad = (back * mask * sig * (1.0 + pre * (1.0 - sig))).astype(BF16)
    grad_one[...] = grad
    shifted_columns(hidden[...], columns.at[1], INNER)
    columns[1, :, INNER:OUTER] = jnp.zeros((9 * C, OUTER - INNER), BF16)
    kept = jnp.where(own_voxels(BASE + 1, OUTER), 1.0, 0.0)
    inner[0] = (grad.astype(F32) * kept).astype(BF16)
    start = 2 * (BASE + 1)
    kept = jnp.where(own_voxels(start, INNER), 1.0, 0.0)
    grad_two = padded[C : 2 * C, start : start + INNER].astype(F32)
    inner[1, :, 0:INNER] = (grad_two * kept).astype(BF16)
    inner[1, :, INNER:OUTER] = jnp.zeros((C, OUTER - INNER), BF16)
    weight_grad(inner[1 - own[1]].astype(F32), columns[1 - own[1]], grads, send)


def keep_kernel(own, inner, columns, keep, grads):
    weight_grad(inner[own[1]].astype(F32), columns[own[1]], grads, keep)


def out_kernel(after, padded, hidden, grad_one, w_two, w_one, out_feats, grad_feats, done, columns):
    done[...] = jnp.zeros((8, 128), F32)
    voxel = ints((INNER, 512), 1)
    inner = voxel // 64 * (PAD * PAD) + voxel // 8 % 8 * PAD + voxel % 8
    squeeze = jnp.where(ints((INNER, 512), 0) == inner, 1.0, 0.0).astype(BF16)
    start = 2 * (BASE + 1)
    mask = padded[2 * C : 2 * C + 1, start : start + INNER].astype(F32)
    for first, field, weight, out in (
        (0, hidden, w_two, out_feats),
        (C, grad_one, w_one, grad_feats),
    ):
        shifted_columns(field[...], columns, INNER)
        pre = three_taps(weight, columns, INNER)
        kept = padded[first : first + C, start : start + INNER].astype(F32)
        wide = (kept + pre * mask).astype(BF16)
        out[0] = jnp.dot(wide, squeeze, preferred_element_type=F32).astype(BF16)


def share_kernel(count, parts, *refs):
    total = parts[0].astype(F32)
    for number in range(1, count):
        total = total + parts[number].astype(F32)
    copies = refs[-1]
    for number in range(copies.shape[0]):
        copies[number] = total.astype(BF16)


def write_half(half, out, rows, sems):
    copies = []
    for row in range(6):
        for lane in range(TILES_L):
            last = min((lane + 1) * 128, 27 * C)
            part = half[row * TILES_L + lane].astype(F32)
            rows[row * 16 : row * 16 + 16, lane * 128 : last] = part[:, : last - lane * 128]
        at = pl.ds(row * 16, 16)
        copies.append(pltpu.make_async_copy(rows.at[at], out.at[at], sems.at[row]))
        copies[-1].start()
    for copy in copies:
        copy.wait()


def mine_kernel(own, half, first, second, rows, sems):
    @pl.when(own[1] == 0)
    def _():
        write_half(half, first, rows, sems)

    @pl.when(own[1] != 0)
    def _():
        write_half(half, second, rows, sems)


def other_kernel(own, half, first_in, second_in, first, second, rows, sems):
    @pl.when(own[1] == 0)
    def _():
        write_half(half, second, rows, sems)

    @pl.when(own[1] != 0)
    def _():
        write_half(half, first, rows, sems)


VMEM = pl.BlockSpec(memory_space=pltpu.VMEM)
SMEM = pl.BlockSpec(memory_space=pltpu.SMEM)
HBM = pl.BlockSpec(memory_space=pltpu.HBM)
ANY = pl.BlockSpec(memory_space=pl.ANY)
DMA = pltpu.SemaphoreType.DMA
MIB = 1024 * 1024
PACK, PREPARE = int(53.58 * MIB), int(51.4 * MIB)


def call(kernel, outs, specs, scratch=(), place=VMEM, limit=40 * MIB, **options):
    return pl.pallas_call(
        kernel,
        out_shape=[jax.ShapeDtypeStruct(*out) for out in outs],
        in_specs=specs,
        out_specs=[place] * len(outs),
        scratch_shapes=scratch,
        compiler_params=pltpu.CompilerParams(vmem_limit_bytes=limit),
        **options,
    )


def from_owner(value, sx, sy):
    pairs = []
    for owner in range(GRID * GRID):
        column, row = owner % GRID + sx, owner // GRID + sy
        if 0 <= column < GRID and 0 <= row < GRID:
            pairs.append((row * GRID + column, owner))
    return lax.ppermute(value, ("zh", "zl", "y"), pairs)


def swap_halves(value):
    return lax.ppermute(value, "core", [(0, 1), (1, 0)])


def body(feats, cotangent, occupancy, counts, adjacency, w_first, w_second):
    own = jnp.stack([lax.axis_index(("zh", "zl", "y")), lax.axis_index("core")]).astype(jnp.int32)
    rim, slab, turned = ((ROWS, 128), BF16), ((ROWS, 256), BF16), ((3 * C, 9 * C), BF16)
    vmem = pltpu.VMEM
    inputs = [
        vmem((1, C, 512), BF16), vmem((1, C, 512), BF16), vmem((1, 512), jnp.int32), DMA((3,))
    ]
    with jax.named_scope("pack"):
        down, up, *quarters = call(
            pack_kernel, [rim] * 6, [HBM] * 3, [vmem((ROWS, 512), BF16)] + inputs, limit=PACK
        )(feats, cotangent, occupancy)
    with jax.named_scope("prepare"):
        one_f, one_b, two_f, two_b, places, low, side = call(
            prepare_kernel,
            [turned] * 4
            + [((8, LANES), jnp.int32), ((16, 128), BF16), ((16, 256), BF16)],
            [SMEM] * 2 + [HBM] * 2,
            [vmem((C, 27 * C), BF16)] * 2 + [DMA((2,))],
            limit=PREPARE,
        )(adjacency, own, w_first, w_second)
    with jax.named_scope("rims_y"):
        ym, yp = from_owner(down, 0, -1), from_owner(up, 0, 1)
    with jax.named_scope("slabs"):
        left, right = call(slab_kernel, [slab, slab], [VMEM] * 4)(quarters[0], quarters[3], ym, yp)
    with jax.named_scope("rims_x"):
        xm, xp = from_owner(left, -1, 0), from_owner(right, 1, 0)
    with jax.named_scope("place"):
        base, hot_x = call(
            place_kernel,
            [((ROWS, LANES), BF16), ((256, LANES), BF16)],
            [VMEM] * 8,
            [vmem((ROWS, 640), BF16)],
        )(*quarters, ym, yp, places, low)
    half, grads = ((128, 16, 128), F32), vmem((C, TILES_L * 128), F32)
    outer = ((C, OUTER), BF16)
    with jax.named_scope("middle"):
        send, padded, hidden, grad_one, inner, columns = call(
            main_kernel,
            [
                half, ((ROWS, LANES), BF16), outer, outer,
                ((2, C, OUTER), BF16), ((2, 9 * C, OUTER), BF16),
            ],
            [SMEM] + [VMEM] * 7,
            [vmem((9 * C, OUTER), BF16), grads],
        )(own, xm, xp, base, hot_x, side, one_f, two_b)
    with jax.named_scope("keep"):
        (keep,) = call(keep_kernel, [half], [SMEM] + [VMEM] * 2, [grads])(own, inner, columns)
    with jax.named_scope("pair"):
        pair = keep + swap_halves(send)
    near, far = ("zl", "y", "x"), "zh"
    with jax.named_scope("sum"):
        parts = lax.all_to_all(pair, near, 0, 0, tiled=True).reshape(32, 4, 16, 128)
        (copies,) = call(
            lambda *refs: share_kernel(32, *refs), [((8, 4, 16, 128), BF16)], [VMEM]
        )(parts)
        parts = lax.all_to_all(copies, far, 0, 0)
    with jax.named_scope("outputs"):
        out_feats, grad_feats, done = call(
            out_kernel,
            [((1, C, 512), BF16)] * 2 + [((8, 128), F32)],
            [ANY] + [VMEM] * 5,
            [vmem((9 * C, INNER), BF16)],
        )(copies, padded, hidden, grad_one, two_f, one_b)
    with jax.named_scope("shares"):
        (copies,) = call(
            lambda *refs: share_kernel(8, *refs), [((32, 4, 16, 128), BF16)], [VMEM] * 2
        )(parts, done)
        mine = lax.all_to_all(copies, near, 0, 0).reshape(128, 16, 128)
        other = swap_halves(mine)
    grad, rows = ((C, 27 * C), F32), [vmem((C, 27 * C), F32), DMA((6,))]
    with jax.named_scope("mine"):
        begun = call(mine_kernel, [grad] * 2, [SMEM, VMEM], rows, place=ANY)(own, mine)
    with jax.named_scope("other"):
        grad_first, grad_second = call(
            other_kernel, [grad] * 2, [SMEM, VMEM, ANY, ANY], rows, place=ANY,
            input_output_aliases={2: 0, 3: 1},
        )(own, other, *begun)
    return out_feats, grad_feats, grad_first, grad_second


def solution(mesh):
    fine = Mesh(mesh.devices.reshape(8, 2, 4, 4, 2), ("zh", "zl", "y", "x", "core"))
    both = ("zh", "zl", "y", "x", "core")
    blocks = P(both, None, None)
    rows = P(both, None)
    return jax.shard_map(
        body,
        mesh=fine,
        in_specs=(blocks, blocks, rows, rows, rows, P(), P()),
        out_specs=(blocks, blocks, P(), P()),
        check_vma=False,
    )
```

time: 117 us -> 112 us (0.957)
  local copies, waits for them, and re-layouts: 6.99 us -> 1.33 us
  waiting for transfers between devices: 13.8 us -> 16.7 us
  blocking collectives: 40.9 us -> 38.2 us
  starting transfers between devices: 31 us -> 33.1 us
    unnamed x16 -> x4, local copies, waits for them, and re-layouts: 6.99 us -> 1.33 us
    ppermute x4, waiting for transfers between devices: 2.48 us -> 6.32 us  [from_owner(): return lax.ppermute(value, ('zh', 'zl', 'y'), pairs)]
    all_to_all x1, starting transfers between devices: 8.4 us -> 11.1 us  [body(): parts = lax.all_to_all(copies, far, 0, 0)]
    all_to_all x1, blocking collectives: 26.2 us -> 23.7 us  [body(): parts = lax.all_to_all(pair, near, 0, 0, tiled=True).reshape(32, 4, 16, 128)]
  transfers between devices with their start and end apart: 7 -> 7, of which waited for: 3 -> 3; matrix products, arithmetic and copies ran while one was open for 0% -> 0% of each run, Pallas kernels for 10% -> 11%
where the time goes in v4:
time: 112 us; the launch traced here: 111 us
  blocking collectives  38.2 us (34%)
  starting transfers between devices  33.1 us (30%)
  Pallas kernels  21 us (19%)
  waiting for transfers between devices  16.7 us (15%)
  local copies, waits for them, and re-layouts  1.33 us (1%)
    all_to_all x1, blocking collectives, body(): parts = lax.all_to_all(pair, near, 0, 0, tiled=True).reshape(32, 4, 16, 128)  23.7 us
    all_to_all x1, blocking collectives, body(): mine = lax.all_to_all(copies, near, 0, 0).reshape(128, 16, 128)  14.5 us
    ppermute x4, starting transfers between devices, from_owner(): return lax.ppermute(value, ('zh', 'zl', 'y'), pairs)  11.5 us
    all_to_all x1, starting transfers between devices, body(): parts = lax.all_to_all(copies, far, 0, 0)  11.1 us
    ppermute x2, starting transfers between devices, swap_halves(): return lax.ppermute(value, 'core', [(0, 1), (1, 0)])  10.4 us
    all_to_all x1, waiting for transfers between devices, body(): parts = lax.all_to_all(copies, far, 0, 0)  10.1 us
    ppermute x4, waiting for transfers between devices, from_owner(): return lax.ppermute(value, ('zh', 'zl', 'y'), pairs)  6.32 us
    pallas_call x1, Pallas kernels, body(): call(main_kernel, [half, ((ROWS, LANES), BF16), outer, outer, ((2, C, OUT...  5.56 us
  transfers between devices with their start and end apart: 7, of which 3 were waited for; matrix products, arithmetic and copies ran while one was open for 0% of the time, Pallas kernels for 11%

profile of v4, /device:TPU:1, one launch (start us, length us, event | category | flops | bytes accessed | tf_op | source)
XLA Modules:
  0.0 111.5 jit_solution(7152918999676375598)
XLA Ops:
  0.6 0.0 copy-start
  0.6 0.7 copy-done
  1.3 1.2 %pack.1 = (bf16[208,128]{1,0:T(8,128)(2,1)S(1)}, bf16[208,128]{1,0:T(8,128)(2,1)S(1)}, bf16[208,128]{1,0:T(8,128)(2,1)S(1)}, bf16[208,128]{1,0:T(8,128)(2,1)S(1)...) custom-call(bf16[1,96,512]{2,1,0:T(8,128)(2,1)} %feats_in.1, bf16[1,96,512]{2,1,0:T(8,128)(2,1)} %cot_in.1, ...), custom_call_target="tpu_custom_call" | custom-call | tf_op jit(solution)/shard_map/pack/pallas_call | solution.py:338
  2.5 5.7 %collective-permute-start = (bf16[208,128]{1,0:T(8,128)(2,1)S(1)}, bf16[208,128]{1,0:T(8,128)(2,1)S(1)}, u32[]{:S(2)}, u32[]{:S(2)}) collective-permute-start(bf16[208,128]{1,0:T(8,128)(2,1)S(1)} %get-tuple-element.36), channel_id=1, source_target_pairs={{0,64},{8,72},{16,80},{24,88},{32,96},{40,104},{48,112},{56,120},{... | collective-permute-start | bytes 159752 | tf_op jit(solution)/shard_map/rims_y/ppermute | solution.py:323
  8.2 1.3 %collective-permute-start.1 = (bf16[208,128]{1,0:T(8,128)(2,1)S(1)}, bf16[208,128]{1,0:T(8,128)(2,1)S(1)}, u32[]{:S(2)}, u32[]{:S(2)}) collective-permute-start(bf16[208,128]{1,0:T(8,128)(2,1)S(1)} %get-tuple-element.37), channel_id=1, source_target_pairs={{64,0},{72,8},{80,16},{88,24},{96,32},{104,40},{112,48},{120,56},{... | collective-permute-start | bytes 159752 | tf_op jit(solution)/shard_map/rims_y/ppermute | solution.py:323
  9.6 0.0 collective-permute-done.ym
  9.6 6.3 %collective-permute-done.1.yp = bf16[208,128]{1,0:T(8,128)(2,1)S(1)} collective-permute-done((bf16[208,128]{1,0:T(8,128)(2,1)S(1)}, bf16[208,128]{1,0:T(8,128)(2,1)S(1)}, u32[]{:S(2)}, u32[]{:S(2)}) %collective-permute-start.1) | collective-permute-done | bytes 53280 | tf_op jit(solution)/shard_map/rims_y/ppermute | solution.py:323
  15.9 0.1 slabs.1
  16.0 3.2 %collective-permute-start.2 = (bf16[208,256]{1,0:T(8,128)(2,1)S(1)}, bf16[208,256]{1,0:T(8,128)(2,1)S(1)}, u32[]{:S(2)}, u32[]{:S(2)}) collective-permute-start(bf16[208,256]{1,0:T(8,128)(2,1)S(1)} %get-tuple-element.38), channel_id=1, source_target_pairs={{0,8},{8,16},{16,24},{24,32},{32,40},{40,48},{48,56},{64,72},{72,8... | collective-permute-start | bytes 319496 | tf_op jit(solution)/shard_map/rims_x/ppermute | solution.py:323
  19.2 1.3 %collective-permute-start.3 = (bf16[208,256]{1,0:T(8,128)(2,1)S(1)}, bf16[208,256]{1,0:T(8,128)(2,1)S(1)}, u32[]{:S(2)}, u32[]{:S(2)}) collective-permute-start(bf16[208,256]{1,0:T(8,128)(2,1)S(1)} %get-tuple-element.39), channel_id=1, source_target_pairs={{8,0},{16,8},{24,16},{32,24},{40,32},{48,40},{56,48},{72,64},{80,7... | collective-permute-start | bytes 319496 | tf_op jit(solution)/shard_map/rims_x/ppermute | solution.py:323
  20.5 0.1 pad_add_fusion.own
  20.6 0.7 copy-done.1
  21.2 3.1 %prepare.1 = (bf16[288,864]{1,0:T(8,128)(2,1)S(1)}, bf16[288,864]{1,0:T(8,128)(2,1)S(1)}, bf16[288,864]{1,0:T(8,128)(2,1)S(1)}, bf16[288,864]{1,0:T(8,128)(2,1)S...) custom-call(s32[1,27]{1,0:T(1,128)S(1)} %copy-done.1, ...), custom_call_target="tpu_custom_call" | custom-call | tf_op jit(solution)/shard_map/prepare/pallas_call | solution.py:342
  24.3 1.3 %place.1 = (bf16[208,1920]{1,0:T(8,128)(2,1)S(1)}, bf16[256,1920]{1,0:T(8,128)(2,1)S(1)}) custom-call(bf16[208,128]{1,0:T(8,128)(2,1)S(1)} %get-tuple-element.34.first.q0, bf16[208,128]{1,0:T(8,128)(2,1)S(1)} %get-tuple-element.40.q1, bf16[208,128]{1,0:T(8,128)(2,1)S(1)} %get-tuple-element.41.q2, bf16[208,128]{1,0:T(8,128)(2,1)S(1)} %get-tuple-element.35.last.q3, ...), custom_call_target="tpu_custom_call" | custom-call | tf_op jit(solution)/shard_map/place/pallas_call | solution.py:357
  25.6 0.0 collective-permute-done.2.xm
  25.7 0.0 collective-permute-done.3.xp
  25.7 5.6 %middle.1 = (f32[128,16,128]{2,1,0:T(8,128)S(1)}, bf16[208,1920]{1,0:T(8,128)(2,1)S(1)}, bf16[96,1536]{1,0:T(8,128)(2,1)S(1)}, bf16[96,1536]{1,0:T(8,128)(2,1)S(...) custom-call(s32[2]{0:T(128)S(1)} %pad_add_fusion.own, ...), custom_call_target="tpu_custom_call" | custom-call | tf_op jit(solution)/shard_map/middle/pallas_call | solution.py:366
  31.2 4.7 %collective-permute-start.4 = (f32[128,16,128]{2,1,0:T(8,128)S(1)}, f32[128,16,128]{2,1,0:T(8,128)S(1)}, u32[]{:S(2)}, u32[]{:S(2)}) collective-permute-start(f32[128,16,128]{2,1,0:T(8,128)S(1)} %get-tuple-element.51), channel_id=1, source_target_pairs={{0,1},{1,0},{2,3},{3,2},{4,5},{5,4},{6,7},{7,6},{8,9},{9,8},{10,11... | collective-permute-start | bytes 3145736 | tf_op jit(solution)/shard_map/pair/ppermute | solution.py:327
  35.9 2.0 %keep.1 = f32[128,16,128]{2,1,0:T(8,128)S(1)} custom-call(s32[2]{0:T(128)S(1)} %pad_add_fusion.own, bf16[2,96,1536]{2,1,0:T(8,128)(2,1)S(1)} %get-tuple-element.49.inner, bf16[2,864,1536]{2,1,0:T(8,128)(2,1)S(1)} %get-tuple-element.50.columns), custom_call_target="tpu_custom_call" | custom-call | tf_op jit(solution)/shard_map/keep/pallas_call | solution.py:376
  37.9 0.3 collective-permute-done.4
  38.2 0.1 add.11
  38.4 23.7 %all_to_all.15 = f32[128,16,128]{2,1,0:T(8,128)S(1)} all-to-all(f32[128,16,128]{2,1,0:T(8,128)S(1)} %add.11), channel_id=1, replica_groups=mesh['zh'=8,'zl'=2,'y'=4,'x'=4,'core'=2] {'zl','y','x'}, dimensions={0} | all-to-all | bytes 2097152 | tf_op jit(solution)/shard_map/sum/all_to_all | solution.py:381
  62.1 0.7 sum.1.after
  62.8 11.1 %all-to-all-start.1 = ((bf16[8,4,16,128]{3,2,1,0:T(8,128)(2,1)}), bf16[8,4,16,128]{3,2,1,0:T(8,128)(2,1)S(1)}, u32[]{:S(2)}, u32[]{:S(2)}) async-start(bf16[8,4,16,128]{3,2,1,0:T(8,128)(2,1)} %sum.1.after), calls=%async_computation.1 | async-start | bytes 262144 | tf_op jit(solution)/shard_map/sum/all_to_all | solution.py:385
  73.9 3.8 %outputs.1 = (bf16[1,96,512]{2,1,0:T(8,128)(2,1)}, bf16[1,96,512]{2,1,0:T(8,128)(2,1)}, f32[8,128]{1,0:T(8,128)S(1)}) custom-call(bf16[8,4,16,128]{3,2,1,0:T(8,128)(2,1)} %sum.1.after, bf16[208,1920]{1,0:T(8,128)(2,1)S(1)} %get-tuple-element.52.padded, bf16[96,1536]{1,0:T(8,128)(2,1)S(1)} %get-tuple-element.53.hidden, ...), custom_call_target="tpu_custom_call" | custom-call | tf_op jit(solution)/shard_map/outputs/pallas_call | solution.py:387
  77.7 10.1 %all-to-all-done.1.refs_0_ = bf16[8,4,16,128]{3,2,1,0:T(8,128)(2,1)S(1)} async-done(((bf16[8,4,16,128]{3,2,1,0:T(8,128)(2,1)}), bf16[8,4,16,128]{3,2,1,0:T(8,128)(2,1)S(1)}, u32[]{:S(2)}, u32[]{:S(2)}) %all-to-all-start.1) | async-done | bytes 131104 | tf_op jit(solution)/shard_map/sum/all_to_all | solution.py:385
  87.8 0.1 shares.1
  87.9 14.5 %all_to_all.16 = bf16[32,4,16,128]{3,2,1,0:T(8,128)(2,1)S(1)} all-to-all(bf16[32,4,16,128]{3,2,1,0:T(8,128)(2,1)S(1)} %shares.1), channel_id=1, replica_groups=mesh['zh'=8,'zl'=2,'y'=4,'x'=4,'core'=2] {'zl','y','x'}, dimensions={0} | all-to-all | bytes 1048576 | tf_op jit(solution)/shard_map/shares/all_to_all | solution.py:397
  102.4 5.7 %collective-permute-start.5 = (bf16[128,16,128]{2,1,0:T(8,128)(2,1)S(1)}, bf16[128,16,128]{2,1,0:T(8,128)(2,1)S(1)}, u32[]{:S(2)}, u32[]{:S(2)}) collective-permute-start(bf16[128,16,128]{2,1,0:T(8,128)(2,1)S(1)} %bitcast.5), channel_id=1, source_target_pairs={{0,1},{1,0},{2,3},{3,2},{4,5},{5,4},{6,7},{7,6},{8,9},{9,8},{10,11... | collective-permute-start | bytes 1572872 | tf_op jit(solution)/shard_map/shares/ppermute | solution.py:327
  108.2 1.6 %mine.1 = (f32[96,2592]{1,0:T(8,128)}, f32[96,2592]{1,0:T(8,128)}) custom-call(s32[2]{0:T(128)S(1)} %pad_add_fusion.own, bf16[128,16,128]{2,1,0:T(8,128)(2,1)S(1)} %bitcast.6), custom_call_target="tpu_custom_call" | custom-call | tf_op jit(solution)/shard_map/mine/pallas_call | solution.py:401
  109.7 0.0 collective-permute-done.5.half
  109.8 1.6 %other.1 = (f32[96,2592]{1,0:T(8,128)}, f32[96,2592]{1,0:T(8,128)}) custom-call(s32[2]{0:T(128)S(1)} %pad_add_fusion.own, bf16[128,16,128]{2,1,0:T(8,128)(2,1)S(1)} %collective-permute-done.5.half, f32[96,2592]{1,0:T(8,128)} %get-tuple-element.60.first_in, f32[96,2592]{1,0:T(8,128)} %get-tuple-element.61.second_in), custom_call_target="tpu_custom_call", output_to_operand_aliasing={{0}: (2, {}), {1}: (3, {})} | custom-call | tf_op jit(solution)/shard_map/other/pallas_call | solution.py:403
  (1 shorter events, 0.0 us)
Async XLA Ops:
  0.6 0.7 copy-start
  2.5 7.0 %collective-permute-start = (bf16[208,128]{1,0:T(8,128)(2,1)S(1)}, bf16[208,128]{1,0:T(8,128)(2,1)S(1)}, u32[]{:S(2)}, u32[]{:S(2)}) collective-permute-start(bf16[208,128]{1,0:T(8,128)(2,1)S(1)} %get-tuple-element.36), channel_id=1, source_target_pairs={{0,64},{8,72},{16,80},{24,88},{32,96},{40,104},{48,112},{56,120},{... | collective-permute-start | bytes 159752 | tf_op jit(solution)/shard_map/rims_y/ppermute | solution.py:323
  8.2 7.6 %collective-permute-start.1 = (bf16[208,128]{1,0:T(8,128)(2,1)S(1)}, bf16[208,128]{1,0:T(8,128)(2,1)S(1)}, u32[]{:S(2)}, u32[]{:S(2)}) collective-permute-start(bf16[208,128]{1,0:T(8,128)(2,1)S(1)} %get-tuple-element.37), channel_id=1, source_target_pairs={{64,0},{72,8},{80,16},{88,24},{96,32},{104,40},{112,48},{120,56},{... | collective-permute-start | bytes 159752 | tf_op jit(solution)/shard_map/rims_y/ppermute | solution.py:323
  16.0 9.7 %collective-permute-start.2 = (bf16[208,256]{1,0:T(8,128)(2,1)S(1)}, bf16[208,256]{1,0:T(8,128)(2,1)S(1)}, u32[]{:S(2)}, u32[]{:S(2)}) collective-permute-start(bf16[208,256]{1,0:T(8,128)(2,1)S(1)} %get-tuple-element.38), channel_id=1, source_target_pairs={{0,8},{8,16},{16,24},{24,32},{32,40},{40,48},{48,56},{64,72},{72,8... | collective-permute-start | bytes 319496 | tf_op jit(solution)/shard_map/rims_x/ppermute | solution.py:323
  19.2 6.5 %collective-permute-start.3 = (bf16[208,256]{1,0:T(8,128)(2,1)S(1)}, bf16[208,256]{1,0:T(8,128)(2,1)S(1)}, u32[]{:S(2)}, u32[]{:S(2)}) collective-permute-start(bf16[208,256]{1,0:T(8,128)(2,1)S(1)} %get-tuple-element.39), channel_id=1, source_target_pairs={{8,0},{16,8},{24,16},{32,24},{40,32},{48,40},{56,48},{72,64},{80,7... | collective-permute-start | bytes 319496 | tf_op jit(solution)/shard_map/rims_x/ppermute | solution.py:323
  20.6 0.7 copy-start.1
  31.2 7.0 %collective-permute-start.4 = (f32[128,16,128]{2,1,0:T(8,128)S(1)}, f32[128,16,128]{2,1,0:T(8,128)S(1)}, u32[]{:S(2)}, u32[]{:S(2)}) collective-permute-start(f32[128,16,128]{2,1,0:T(8,128)S(1)} %get-tuple-element.51), channel_id=1, source_target_pairs={{0,1},{1,0},{2,3},{3,2},{4,5},{5,4},{6,7},{7,6},{8,9},{9,8},{10,11... | collective-permute-start | bytes 3145736 | tf_op jit(solution)/shard_map/pair/ppermute | solution.py:327
  62.8 25.0 %all-to-all-start.1 = ((bf16[8,4,16,128]{3,2,1,0:T(8,128)(2,1)}), bf16[8,4,16,128]{3,2,1,0:T(8,128)(2,1)S(1)}, u32[]{:S(2)}, u32[]{:S(2)}) async-start(bf16[8,4,16,128]{3,2,1,0:T(8,128)(2,1)} %sum.1.after), calls=%async_computation.1 | async-start | bytes 262144 | tf_op jit(solution)/shard_map/sum/all_to_all | solution.py:385
  102.4 7.3 %collective-permute-start.5 = (bf16[128,16,128]{2,1,0:T(8,128)(2,1)S(1)}, bf16[128,16,128]{2,1,0:T(8,128)(2,1)S(1)}, u32[]{:S(2)}, u32[]{:S(2)}) collective-permute-start(bf16[128,16,128]{2,1,0:T(8,128)(2,1)S(1)} %bitcast.5), channel_id=1, source_target_pairs={{0,1},{1,0},{2,3},{3,2},{4,5},{5,4},{6,7},{7,6},{8,9},{9,8},{10,11... | collective-permute-start | bytes 1572872 | tf_op jit(solution)/shard_map/shares/ppermute | solution.py:327

commit v5 on v4

--- a/solution.py
+++ b/solution.py
@@ -68,7 +68,7 @@
         quarters[number][...] = field[:, number * 128 : (number + 1) * 128]
 
 
-def slab_kernel(first, last, ym, yp, left, right):
+def slab_kernel(after, first, last, ym, yp, left, right):
     blank = jnp.zeros((ROWS, 64), BF16)
     left[:, 0:128] = last[...]
     left[:, 128:256] = jnp.concatenate([ym[:, 96:128], yp[:, 96:128], blank], axis=1)
@@ -76,18 +76,41 @@
     right[:, 128:256] = jnp.concatenate([ym[:, 0:32], yp[:, 0:32], blank], axis=1)
 
 
-def turn_weights(copies, weights, outs):
-    for copy, weight, forward, turned in zip(copies, weights, outs[0::2], outs[1::2]):
-        copy.wait()
-        whole = weight[...]
-        across = whole.astype(F32).T.astype(BF16)
-        for number in range(9):
-            for dz in range(3):
-                k = number * 3 + dz
-                rows = slice(dz * C, (dz + 1) * C)
-                columns = slice(number * C, (number + 1) * C)
-                forward[rows, columns] = whole[:, k * C : (k + 1) * C]
-                turned[rows, columns] = across[(26 - k) * C : (27 - k) * C, :]
+def tap_blocks():
+    for number in range(9):
+        for dz in range(3):
+            k = number * 3 + dz
+            yield k, slice(dz * C, (dz + 1) * C), slice(number * C, (number + 1) * C)
+
+
+def forward_weight(weight, out):
+    whole = weight[...]
+    for k, rows, columns in tap_blocks():
+        out[rows, columns] = whole[:, k * C : (k + 1) * C]
+
+
+def turned_weight(weight, out):
+    across = weight[...].astype(F32).T.astype(BF16)
+    for k, rows, columns in tap_blocks():
+        out[rows, columns] = across[(26 - k) * C : (27 - k) * C, :]
+
+
+def start_weights(first_in, second_in, first, second, sems):
+    copies = [
+        pltpu.make_async_copy(first_in, first, sems.at[0]),
+        pltpu.make_async_copy(second_in, second, sems.at[1]),
+    ]
+    for copy in copies:
+        copy.start()
+    return copies
+
+
+def late_weight_kernel(after, first_in, second_in, second_forward, first_turned, first, second, sems):
+    copies = start_weights(first_in, second_in, first, second, sems)
+    copies[1].wait()
+    forward_weight(second, second_forward)
+    copies[0].wait()
+    turned_weight(first, first_turned)
 
 
 def shifted_columns(source, columns, length):
@@ -139,16 +162,10 @@
 
 
 def prepare_kernel(
-    adj, own, first_in, second_in,
-    first_forward, first_turned, second_forward, second_turned, places, low, side,
-    first, second, weight_sems,
+    adj, own, first_in, second_in, first_forward, second_turned, places, low, side,
+    first, second, sems,
 ):
-    weight_copies = [
-        pltpu.make_async_copy(first_in, first, weight_sems.at[0]),
-        pltpu.make_async_copy(second_in, second, weight_sems.at[1]),
-    ]
-    for copy in weight_copies:
-        copy.start()
+    copies = start_weights(first_in, second_in, first, second, sems)
     relative = relative_owners(adj, own)
     from_left = among(relative, [-1 - GRID, -1, -1 + GRID])
     side[...] = jnp.full(side.shape, jnp.where(from_left, 1.0, 0.0), F32).astype(BF16)
@@ -173,9 +190,10 @@
             there = (768 if sy < 0 else 800) + nx * 16 + ny * 8 + z
         place = jnp.where(which == sx + GRID * sy, there, place)
     places[...] = jnp.broadcast_to(place, places.shape)
-    turn_weights(
-        weight_copies, (first, second), (first_forward, first_turned, second_forward, second_turned)
-    )
+    copies[0].wait()
+    forward_weight(first, first_forward)
+    copies[1].wait()
+    turned_weight(second, second_turned)
 
 
 def either(flag, one, other):
@@ -299,7 +317,7 @@
 ANY = pl.BlockSpec(memory_space=pl.ANY)
 DMA = pltpu.SemaphoreType.DMA
 MIB = 1024 * 1024
-PACK, PREPARE = int(53.58 * MIB), int(51.4 * MIB)
+PACK, PREPARE, LATE = int(53.58 * MIB), int(52.4 * MIB), int(52.5 * MIB)
 
 
 def call(kernel, outs, specs, scratch=(), place=VMEM, limit=40 * MIB, **options):
@@ -334,23 +352,26 @@
     inputs = [
         vmem((1, C, 512), BF16), vmem((1, C, 512), BF16), vmem((1, 512), jnp.int32), DMA((3,))
     ]
+    weights = [vmem((C, 27 * C), BF16)] * 2 + [DMA((2,))]
     with jax.named_scope("pack"):
         down, up, *quarters = call(
             pack_kernel, [rim] * 6, [HBM] * 3, [vmem((ROWS, 512), BF16)] + inputs, limit=PACK
         )(feats, cotangent, occupancy)
     with jax.named_scope("prepare"):
-        one_f, one_b, two_f, two_b, places, low, side = call(
+        one_f, two_b, places, low, side = call(
             prepare_kernel,
-            [turned] * 4
+            [turned] * 2
             + [((8, LANES), jnp.int32), ((16, 128), BF16), ((16, 256), BF16)],
             [SMEM] * 2 + [HBM] * 2,
-            [vmem((C, 27 * C), BF16)] * 2 + [DMA((2,))],
+            weights,
             limit=PREPARE,
         )(adjacency, own, w_first, w_second)
     with jax.named_scope("rims_y"):
         ym, yp = from_owner(down, 0, -1), from_owner(up, 0, 1)
     with jax.named_scope("slabs"):
-        left, right = call(slab_kernel, [slab, slab], [VMEM] * 4)(quarters[0], quarters[3], ym, yp)
+        left, right = call(slab_kernel, [slab, slab], [VMEM] * 5)(
+            side, quarters[0], quarters[3], ym, yp
+        )
     with jax.named_scope("rims_x"):
         xm, xp = from_owner(left, -1, 0), from_owner(right, 1, 0)
     with jax.named_scope("place"):
@@ -383,6 +404,10 @@
             lambda *refs: share_kernel(32, *refs), [((8, 4, 16, 128), BF16)], [VMEM]
         )(parts)
         parts = lax.all_to_all(copies, far, 0, 0)
+    with jax.named_scope("late_weights"):
+        two_f, one_b = call(
+            late_weight_kernel, [turned] * 2, [ANY] + [HBM] * 2, weights, limit=LATE
+        )(copies, w_first, w_second)
     with jax.named_scope("outputs"):
         out_feats, grad_feats, done = call(
             out_kernel,

time: 112 us -> 112 us (level)
  waiting for transfers between devices: 16.7 us -> 14.3 us
  Pallas kernels: 21 us -> 22.3 us
  starting transfers between devices: 33.1 us -> 34.4 us
    all_to_all x1, waiting for transfers between devices: 10.1 us -> 8.1 us  [body(): parts = lax.all_to_all(copies, far, 0, 0)]
    pallas_call x2 -> x3, Pallas kernels: 3.18 us -> 4.59 us  [the longest x1 2.44 us: body(): call(prepare_kernel, [turned] * 2 + [((8, LANES), jnp.int32), ((16, 128),...]
  transfers between devices with their start and end apart: 7 -> 7, of which waited for: 3 -> 4; matrix products, arithmetic and copies ran while one was open for 0% -> 0% of each run, Pallas kernels for 11% -> 12%
where the time goes in v5:
time: 112 us; the launch traced here: 111 us
  blocking collectives  37.9 us (34%)
  starting transfers between devices  34.4 us (31%)
  Pallas kernels  22.3 us (20%)
  waiting for transfers between devices  14.3 us (13%)
  local copies, waits for them, and re-layouts  1.33 us (1%)
    all_to_all x1, blocking collectives, body(): parts = lax.all_to_all(pair, near, 0, 0, tiled=True).reshape(32, 4, 16, 128)  23.3 us
    all_to_all x1, blocking collectives, body(): mine = lax.all_to_all(copies, near, 0, 0).reshape(128, 16, 128)  14.5 us
    ppermute x4, starting transfers between devices, from_owner(): return lax.ppermute(value, ('zh', 'zl', 'y'), pairs)  11.5 us
    ppermute x2, starting transfers between devices, swap_halves(): return lax.ppermute(value, 'core', [(0, 1), (1, 0)])  11.5 us
    all_to_all x1, starting transfers between devices, body(): parts = lax.all_to_all(copies, far, 0, 0)  11.4 us
    all_to_all x1, waiting for transfers between devices, body(): parts = lax.all_to_all(copies, far, 0, 0)  8.1 us
    ppermute x4, waiting for transfers between devices, from_owner(): return lax.ppermute(value, ('zh', 'zl', 'y'), pairs)  5.93 us
    pallas_call x1, Pallas kernels, body(): call(main_kernel, [half, ((ROWS, LANES), BF16), outer, outer, ((2, C, OUT...  5.54 us
  transfers between devices with their start and end apart: 7, of which 4 were waited for; matrix products, arithmetic and copies ran while one was open for 0% of the time, Pallas kernels for 12%

profile of v5, /device:TPU:1, one launch (start us, length us, event | category | flops | bytes accessed | tf_op | source)
XLA Modules:
  0.0 111.4 jit_solution(6574544785453815487)
XLA Ops:
  0.6 0.7 copy-done
  1.3 1.2 %pack.1 = (bf16[208,128]{1,0:T(8,128)(2,1)S(1)}, bf16[208,128]{1,0:T(8,128)(2,1)S(1)}, bf16[208,128]{1,0:T(8,128)(2,1)S(1)}, bf16[208,128]{1,0:T(8,128)(2,1)S(1)...) custom-call(bf16[1,96,512]{2,1,0:T(8,128)(2,1)} %feats_in.1, bf16[1,96,512]{2,1,0:T(8,128)(2,1)} %cot_in.1, ...), custom_call_target="tpu_custom_call" | custom-call | tf_op jit(solution)/shard_map/pack/pallas_call | solution.py:357
  2.5 5.7 %collective-permute-start = (bf16[208,128]{1,0:T(8,128)(2,1)S(1)}, bf16[208,128]{1,0:T(8,128)(2,1)S(1)}, u32[]{:S(2)}, u32[]{:S(2)}) collective-permute-start(bf16[208,128]{1,0:T(8,128)(2,1)S(1)} %get-tuple-element.37), channel_id=1, source_target_pairs={{0,64},{8,72},{16,80},{24,88},{32,96},{40,104},{48,112},{56,120},{... | collective-permute-start | bytes 159752 | tf_op jit(solution)/shard_map/rims_y/ppermute | solution.py:341
  8.2 1.3 %collective-permute-start.1 = (bf16[208,128]{1,0:T(8,128)(2,1)S(1)}, bf16[208,128]{1,0:T(8,128)(2,1)S(1)}, u32[]{:S(2)}, u32[]{:S(2)}) collective-permute-start(bf16[208,128]{1,0:T(8,128)(2,1)S(1)} %get-tuple-element.38), channel_id=1, source_target_pairs={{64,0},{72,8},{80,16},{88,24},{96,32},{104,40},{112,48},{120,56},{... | collective-permute-start | bytes 159752 | tf_op jit(solution)/shard_map/rims_y/ppermute | solution.py:341
  9.5 0.1 pad_add_fusion.own
  9.6 0.7 copy-done.1
  10.3 2.4 %prepare.1 = (bf16[288,864]{1,0:T(8,128)(2,1)S(1)}, bf16[288,864]{1,0:T(8,128)(2,1)S(1)}, s32[8,1920]{1,0:T(8,128)S(1)}, bf16[16,128]{1,0:T(8,128)(2,1)S(1)}, bf16[16,256]{1,0:T(8,128)(2,1)S(1)}) custom-call(s32[1,27]{1,0:T(1,128)S(1)} %copy-done.1, s32[2]{0:T(128)S(1)} %pad_add_fusion.own, bf16[96,2592]{1,0:T(8,128)(2,1)} %first_in.3, ...), custom_call_target="tpu_custom_call" | custom-call | tf_op jit(solution)/shard_map/prepare/pallas_call | solution.py:361
  12.7 0.0 collective-permute-done.ym
  12.7 3.1 %collective-permute-done.1.yp = bf16[208,128]{1,0:T(8,128)(2,1)S(1)} collective-permute-done((bf16[208,128]{1,0:T(8,128)(2,1)S(1)}, bf16[208,128]{1,0:T(8,128)(2,1)S(1)}, u32[]{:S(2)}, u32[]{:S(2)}) %collective-permute-start.1) | collective-permute-done | bytes 53280 | tf_op jit(solution)/shard_map/rims_y/ppermute | solution.py:341
  15.9 0.1 slabs.1
  16.0 3.2 %collective-permute-start.2 = (bf16[208,256]{1,0:T(8,128)(2,1)S(1)}, bf16[208,256]{1,0:T(8,128)(2,1)S(1)}, u32[]{:S(2)}, u32[]{:S(2)}) collective-permute-start(bf16[208,256]{1,0:T(8,128)(2,1)S(1)} %get-tuple-element.39), channel_id=1, source_target_pairs={{0,8},{8,16},{16,24},{24,32},{32,40},{40,48},{48,56},{64,72},{72,8... | collective-permute-start | bytes 319496 | tf_op jit(solution)/shard_map/rims_x/ppermute | solution.py:341
  19.2 1.3 %collective-permute-start.3 = (bf16[208,256]{1,0:T(8,128)(2,1)S(1)}, bf16[208,256]{1,0:T(8,128)(2,1)S(1)}, u32[]{:S(2)}, u32[]{:S(2)}) collective-permute-start(bf16[208,256]{1,0:T(8,128)(2,1)S(1)} %get-tuple-element.40), channel_id=1, source_target_pairs={{8,0},{16,8},{24,16},{32,24},{40,32},{48,40},{56,48},{72,64},{80,7... | collective-permute-start | bytes 319496 | tf_op jit(solution)/shard_map/rims_x/ppermute | solution.py:341
  20.5 1.3 %place.1 = (bf16[208,1920]{1,0:T(8,128)(2,1)S(1)}, bf16[256,1920]{1,0:T(8,128)(2,1)S(1)}) custom-call(bf16[208,128]{1,0:T(8,128)(2,1)S(1)} %get-tuple-element.35.first.q0, bf16[208,128]{1,0:T(8,128)(2,1)S(1)} %get-tuple-element.41.q1, bf16[208,128]{1,0:T(8,128)(2,1)S(1)} %get-tuple-element.42.q2, bf16[208,128]{1,0:T(8,128)(2,1)S(1)} %get-tuple-element.36.last.q3, ...), custom_call_target="tpu_custom_call" | custom-call | tf_op jit(solution)/shard_map/place/pallas_call | solution.py:378
  21.8 0.0 collective-permute-done.2.xm
  21.9 2.8 %collective-permute-done.3.xp = bf16[208,256]{1,0:T(8,128)(2,1)S(1)} collective-permute-done((bf16[208,256]{1,0:T(8,128)(2,1)S(1)}, bf16[208,256]{1,0:T(8,128)(2,1)S(1)}, u32[]{:S(2)}, u32[]{:S(2)}) %collective-permute-start.3) | collective-permute-done | bytes 106528 | tf_op jit(solution)/shard_map/rims_x/ppermute | solution.py:341
  24.6 5.5 %middle.1 = (f32[128,16,128]{2,1,0:T(8,128)S(1)}, bf16[208,1920]{1,0:T(8,128)(2,1)S(1)}, bf16[96,1536]{1,0:T(8,128)(2,1)S(1)}, bf16[96,1536]{1,0:T(8,128)(2,1)S(...) custom-call(s32[2]{0:T(128)S(1)} %pad_add_fusion.own, ...), custom_call_target="tpu_custom_call" | custom-call | tf_op jit(solution)/shard_map/middle/pallas_call | solution.py:387
  30.2 5.7 %collective-permute-start.4 = (f32[128,16,128]{2,1,0:T(8,128)S(1)}, f32[128,16,128]{2,1,0:T(8,128)S(1)}, u32[]{:S(2)}, u32[]{:S(2)}) collective-permute-start(f32[128,16,128]{2,1,0:T(8,128)S(1)} %get-tuple-element.51), channel_id=1, source_target_pairs={{0,1},{1,0},{2,3},{3,2},{4,5},{5,4},{6,7},{7,6},{8,9},{9,8},{10,11... | collective-permute-start | bytes 3145736 | tf_op jit(solution)/shard_map/pair/ppermute | solution.py:345
  35.9 2.0 %keep.1 = f32[128,16,128]{2,1,0:T(8,128)S(1)} custom-call(s32[2]{0:T(128)S(1)} %pad_add_fusion.own, bf16[2,96,1536]{2,1,0:T(8,128)(2,1)S(1)} %get-tuple-element.49.inner, bf16[2,864,1536]{2,1,0:T(8,128)(2,1)S(1)} %get-tuple-element.50.columns), custom_call_target="tpu_custom_call" | custom-call | tf_op jit(solution)/shard_map/keep/pallas_call | solution.py:397
  37.9 0.3 collective-permute-done.4
  38.2 0.1 add.11
  38.3 23.3 %all_to_all.15 = f32[128,16,128]{2,1,0:T(8,128)S(1)} all-to-all(f32[128,16,128]{2,1,0:T(8,128)S(1)} %add.11), channel_id=1, replica_groups=mesh['zh'=8,'zl'=2,'y'=4,'x'=4,'core'=2] {'zl','y','x'}, dimensions={0} | all-to-all | bytes 2097152 | tf_op jit(solution)/shard_map/sum/all_to_all | solution.py:402
  61.7 0.7 sum.1.after
  62.4 11.4 %all-to-all-start.1 = ((bf16[8,4,16,128]{3,2,1,0:T(8,128)(2,1)}), bf16[8,4,16,128]{3,2,1,0:T(8,128)(2,1)S(1)}, u32[]{:S(2)}, u32[]{:S(2)}) async-start(bf16[8,4,16,128]{3,2,1,0:T(8,128)(2,1)} %sum.1.after), calls=%async_computation.1 | async-start | bytes 262144 | tf_op jit(solution)/shard_map/sum/all_to_all | solution.py:406
  73.8 2.0 %late_weights.1 = (bf16[288,864]{1,0:T(8,128)(2,1)S(1)}, bf16[288,864]{1,0:T(8,128)(2,1)S(1)}) custom-call(bf16[8,4,16,128]{3,2,1,0:T(8,128)(2,1)} %sum.1.after, bf16[96,2592]{1,0:T(8,128)(2,1)} %first_in.3, bf16[96,2592]{1,0:T(8,128)(2,1)} %second_in.3), custom_call_target="tpu_custom_call" | custom-call | tf_op jit(solution)/shard_map/late_weights/pallas_call | solution.py:408
  75.9 3.8 %outputs.1 = (bf16[1,96,512]{2,1,0:T(8,128)(2,1)}, bf16[1,96,512]{2,1,0:T(8,128)(2,1)}, f32[8,128]{1,0:T(8,128)S(1)}) custom-call(bf16[8,4,16,128]{3,2,1,0:T(8,128)(2,1)} %sum.1.after, bf16[208,1920]{1,0:T(8,128)(2,1)S(1)} %get-tuple-element.52.padded, bf16[96,1536]{1,0:T(8,128)(2,1)S(1)} %get-tuple-element.53.hidden, ...), custom_call_target="tpu_custom_call" | custom-call | tf_op jit(solution)/shard_map/outputs/pallas_call | solution.py:412
  79.7 8.1 %all-to-all-done.1.refs_0_ = bf16[8,4,16,128]{3,2,1,0:T(8,128)(2,1)S(1)} async-done(((bf16[8,4,16,128]{3,2,1,0:T(8,128)(2,1)}), bf16[8,4,16,128]{3,2,1,0:T(8,128)(2,1)S(1)}, u32[]{:S(2)}, u32[]{:S(2)}) %all-to-all-start.1) | async-done | bytes 131104 | tf_op jit(solution)/shard_map/sum/all_to_all | solution.py:406
  87.8 0.1 shares.1
  87.8 14.5 %all_to_all.16 = bf16[32,4,16,128]{3,2,1,0:T(8,128)(2,1)S(1)} all-to-all(bf16[32,4,16,128]{3,2,1,0:T(8,128)(2,1)S(1)} %shares.1), channel_id=1, replica_groups=mesh['zh'=8,'zl'=2,'y'=4,'x'=4,'core'=2] {'zl','y','x'}, dimensions={0} | all-to-all | bytes 1048576 | tf_op jit(solution)/shard_map/shares/all_to_all | solution.py:422
  102.4 5.7 %collective-permute-start.5 = (bf16[128,16,128]{2,1,0:T(8,128)(2,1)S(1)}, bf16[128,16,128]{2,1,0:T(8,128)(2,1)S(1)}, u32[]{:S(2)}, u32[]{:S(2)}) collective-permute-start(bf16[128,16,128]{2,1,0:T(8,128)(2,1)S(1)} %bitcast.5), channel_id=1, source_target_pairs={{0,1},{1,0},{2,3},{3,2},{4,5},{5,4},{6,7},{7,6},{8,9},{9,8},{10,11... | collective-permute-start | bytes 1572872 | tf_op jit(solution)/shard_map/shares/ppermute | solution.py:345
  108.1 1.6 %mine.1 = (f32[96,2592]{1,0:T(8,128)}, f32[96,2592]{1,0:T(8,128)}) custom-call(s32[2]{0:T(128)S(1)} %pad_add_fusion.own, bf16[128,16,128]{2,1,0:T(8,128)(2,1)S(1)} %bitcast.6), custom_call_target="tpu_custom_call" | custom-call | tf_op jit(solution)/shard_map/mine/pallas_call | solution.py:426
  109.7 0.0 collective-permute-done.5.half
  109.7 1.6 %other.1 = (f32[96,2592]{1,0:T(8,128)}, f32[96,2592]{1,0:T(8,128)}) custom-call(s32[2]{0:T(128)S(1)} %pad_add_fusion.own, bf16[128,16,128]{2,1,0:T(8,128)(2,1)S(1)} %collective-permute-done.5.half, f32[96,2592]{1,0:T(8,128)} %get-tuple-element.60.first_in, f32[96,2592]{1,0:T(8,128)} %get-tuple-element.61.second_in), custom_call_target="tpu_custom_call", output_to_operand_aliasing={{0}: (2, {}), {1}: (3, {})} | custom-call | tf_op jit(solution)/shard_map/other/pallas_call | solution.py:428
  (2 shorter events, 0.0 us)
Async XLA Ops:
  0.6 0.7 copy-start
  2.5 10.2 %collective-permute-start = (bf16[208,128]{1,0:T(8,128)(2,1)S(1)}, bf16[208,128]{1,0:T(8,128)(2,1)S(1)}, u32[]{:S(2)}, u32[]{:S(2)}) collective-permute-start(bf16[208,128]{1,0:T(8,128)(2,1)S(1)} %get-tuple-element.37), channel_id=1, source_target_pairs={{0,64},{8,72},{16,80},{24,88},{32,96},{40,104},{48,112},{56,120},{... | collective-permute-start | bytes 159752 | tf_op jit(solution)/shard_map/rims_y/ppermute | solution.py:341
  8.2 7.6 %collective-permute-start.1 = (bf16[208,128]{1,0:T(8,128)(2,1)S(1)}, bf16[208,128]{1,0:T(8,128)(2,1)S(1)}, u32[]{:S(2)}, u32[]{:S(2)}) collective-permute-start(bf16[208,128]{1,0:T(8,128)(2,1)S(1)} %get-tuple-element.38), channel_id=1, source_target_pairs={{64,0},{72,8},{80,16},{88,24},{96,32},{104,40},{112,48},{120,56},{... | collective-permute-start | bytes 159752 | tf_op jit(solution)/shard_map/rims_y/ppermute | solution.py:341
  9.6 0.7 copy-start.1
  16.0 5.9 %collective-permute-start.2 = (bf16[208,256]{1,0:T(8,128)(2,1)S(1)}, bf16[208,256]{1,0:T(8,128)(2,1)S(1)}, u32[]{:S(2)}, u32[]{:S(2)}) collective-permute-start(bf16[208,256]{1,0:T(8,128)(2,1)S(1)} %get-tuple-element.39), channel_id=1, source_target_pairs={{0,8},{8,16},{16,24},{24,32},{32,40},{40,48},{48,56},{64,72},{72,8... | collective-permute-start | bytes 319496 | tf_op jit(solution)/shard_map/rims_x/ppermute | solution.py:341
  19.2 5.4 %collective-permute-start.3 = (bf16[208,256]{1,0:T(8,128)(2,1)S(1)}, bf16[208,256]{1,0:T(8,128)(2,1)S(1)}, u32[]{:S(2)}, u32[]{:S(2)}) collective-permute-start(bf16[208,256]{1,0:T(8,128)(2,1)S(1)} %get-tuple-element.40), channel_id=1, source_target_pairs={{8,0},{16,8},{24,16},{32,24},{40,32},{48,40},{56,48},{72,64},{80,7... | collective-permute-start | bytes 319496 | tf_op jit(solution)/shard_map/rims_x/ppermute | solution.py:341
  30.2 8.0 %collective-permute-start.4 = (f32[128,16,128]{2,1,0:T(8,128)S(1)}, f32[128,16,128]{2,1,0:T(8,128)S(1)}, u32[]{:S(2)}, u32[]{:S(2)}) collective-permute-start(f32[128,16,128]{2,1,0:T(8,128)S(1)} %get-tuple-element.51), channel_id=1, source_target_pairs={{0,1},{1,0},{2,3},{3,2},{4,5},{5,4},{6,7},{7,6},{8,9},{9,8},{10,11... | collective-permute-start | bytes 3145736 | tf_op jit(solution)/shard_map/pair/ppermute | solution.py:345
  62.4 25.3 %all-to-all-start.1 = ((bf16[8,4,16,128]{3,2,1,0:T(8,128)(2,1)}), bf16[8,4,16,128]{3,2,1,0:T(8,128)(2,1)S(1)}, u32[]{:S(2)}, u32[]{:S(2)}) async-start(bf16[8,4,16,128]{3,2,1,0:T(8,128)(2,1)} %sum.1.after), calls=%async_computation.1 | async-start | bytes 262144 | tf_op jit(solution)/shard_map/sum/all_to_all | solution.py:406
  102.4 7.3 %collective-permute-start.5 = (bf16[128,16,128]{2,1,0:T(8,128)(2,1)S(1)}, bf16[128,16,128]{2,1,0:T(8,128)(2,1)S(1)}, u32[]{:S(2)}, u32[]{:S(2)}) collective-permute-start(bf16[128,16,128]{2,1,0:T(8,128)(2,1)S(1)} %bitcast.5), channel_id=1, source_target_pairs={{0,1},{1,0},{2,3},{3,2},{4,5},{5,4},{6,7},{7,6},{8,9},{9,8},{10,11... | collective-permute-start | bytes 1572872 | tf_op jit(solution)/shard_map/shares/ppermute | solution.py:345

commit v6 on v5

--- a/solution.py
+++ b/solution.py
@@ -266,6 +266,28 @@
         kept = padded[first : first + C, start : start + INNER].astype(F32)
         wide = (kept + pre * mask).astype(BF16)
         out[0] = jnp.dot(wide, squeeze, preferred_element_type=F32).astype(BF16)
+
+
+def pair_kernel(keep, other, coded):
+    for number in range(32):
+        tiles = slice(number * 4, number * 4 + 4)
+        total = keep[tiles] + other[tiles]
+        most = jnp.maximum(jnp.max(jnp.abs(total), axis=1), 1e-30)
+        exponent = jnp.ceil(jnp.log2(most))
+        values = jnp.round(total * jnp.exp2(14.0 - exponent)[:, None, :])
+        coded[number, 0:4] = values.astype(jnp.int32).astype(jnp.int16)
+        rows = jnp.concatenate([exponent, jnp.zeros((12, 128), F32)], axis=0)
+        coded[number, 4] = rows.astype(jnp.int32).astype(jnp.int16)
+
+
+def decode_kernel(coded, copies):
+    total = jnp.zeros((4, 16, 128), F32)
+    for number in range(32):
+        exponent = coded[number, 4].astype(jnp.int32).astype(F32)[0:4]
+        values = coded[number, 0:4].astype(jnp.int32).astype(F32)
+        total = total + values * jnp.exp2(exponent - 14.0)[:, None, :]
+    for number in range(copies.shape[0]):
+        copies[number] = total.astype(BF16)
 
 
 def share_kernel(count, parts, *refs):
@@ -396,13 +418,13 @@
     with jax.named_scope("keep"):
         (keep,) = call(keep_kernel, [half], [SMEM] + [VMEM] * 2, [grads])(own, inner, columns)
     with jax.named_scope("pair"):
-        pair = keep + swap_halves(send)
+        (coded,) = call(pair_kernel, [((32, 5, 16, 128), jnp.int16)], [VMEM] * 2)(
+            keep, swap_halves(send)
+        )
     near, far = ("zl", "y", "x"), "zh"
     with jax.named_scope("sum"):
-        parts = lax.all_to_all(pair, near, 0, 0, tiled=True).reshape(32, 4, 16, 128)
-        (copies,) = call(
-            lambda *refs: share_kernel(32, *refs), [((8, 4, 16, 128), BF16)], [VMEM]
-        )(parts)
+        parts = lax.all_to_all(coded, near, 0, 0)
+        (copies,) = call(decode_kernel, [((8, 4, 16, 128), BF16)], [VMEM])(parts)
         parts = lax.all_to_all(copies, far, 0, 0)
     with jax.named_scope("late_weights"):
         two_f, one_b = call(

time: 112 us -> 108 us (0.964)
  blocking collectives: 37.9 us -> 33.4 us
    all_to_all x1, blocking collectives: 23.3 us -> 19.3 us  [body(): parts = lax.all_to_all(coded, near, 0, 0)]
where the time goes in v6:
time: 108 us; the launch traced here: 107 us
  starting transfers between devices  34.4 us (32%)
  blocking collectives  33.4 us (31%)
  Pallas kernels  22.9 us (21%)
  waiting for transfers between devices  14.4 us (13%)
  local copies, waits for them, and re-layouts  1.33 us (1%)
    all_to_all x1, blocking collectives, body(): parts = lax.all_to_all(coded, near, 0, 0)  19.3 us
    all_to_all x1, blocking collectives, body(): mine = lax.all_to_all(copies, near, 0, 0).reshape(128, 16, 128)  14.1 us
    ppermute x4, starting transfers between devices, from_owner(): return lax.ppermute(value, ('zh', 'zl', 'y'), pairs)  11.5 us
    ppermute x2, starting transfers between devices, swap_halves(): return lax.ppermute(value, 'core', [(0, 1), (1, 0)])  11.4 us
    all_to_all x1, starting transfers between devices, body(): parts = lax.all_to_all(copies, far, 0, 0)  11.4 us
    all_to_all x1, waiting for transfers between devices, body(): parts = lax.all_to_all(copies, far, 0, 0)  8.13 us
    ppermute x4, waiting for transfers between devices, from_owner(): return lax.ppermute(value, ('zh', 'zl', 'y'), pairs)  5.93 us
    pallas_call x1, Pallas kernels, body(): call(main_kernel, [half, ((ROWS, LANES), BF16), outer, outer, ((2, C, OUT...  5.54 us
  transfers between devices with their start and end apart: 7, of which 4 were waited for; matrix products, arithmetic and copies ran while one was open for 0% of the time, Pallas kernels for 12%

profile of v6, /device:TPU:1, one launch (start us, length us, event | category | flops | bytes accessed | tf_op | source)
XLA Modules:
  0.0 107.3 jit_solution(11486807474095982378)
XLA Ops:
  0.6 0.7 copy-done
  1.3 1.2 %pack.1 = (bf16[208,128]{1,0:T(8,128)(2,1)S(1)}, bf16[208,128]{1,0:T(8,128)(2,1)S(1)}, bf16[208,128]{1,0:T(8,128)(2,1)S(1)}, bf16[208,128]{1,0:T(8,128)(2,1)S(1)...) custom-call(bf16[1,96,512]{2,1,0:T(8,128)(2,1)} %feats_in.1, bf16[1,96,512]{2,1,0:T(8,128)(2,1)} %cot_in.1, ...), custom_call_target="tpu_custom_call" | custom-call | tf_op jit(solution)/shard_map/pack/pallas_call | solution.py:379
  2.5 5.7 %collective-permute-start = (bf16[208,128]{1,0:T(8,128)(2,1)S(1)}, bf16[208,128]{1,0:T(8,128)(2,1)S(1)}, u32[]{:S(2)}, u32[]{:S(2)}) collective-permute-start(bf16[208,128]{1,0:T(8,128)(2,1)S(1)} %get-tuple-element.37), channel_id=1, source_target_pairs={{0,64},{8,72},{16,80},{24,88},{32,96},{40,104},{48,112},{56,120},{... | collective-permute-start | bytes 159752 | tf_op jit(solution)/shard_map/rims_y/ppermute | solution.py:363
  8.2 1.3 %collective-permute-start.1 = (bf16[208,128]{1,0:T(8,128)(2,1)S(1)}, bf16[208,128]{1,0:T(8,128)(2,1)S(1)}, u32[]{:S(2)}, u32[]{:S(2)}) collective-permute-start(bf16[208,128]{1,0:T(8,128)(2,1)S(1)} %get-tuple-element.38), channel_id=1, source_target_pairs={{64,0},{72,8},{80,16},{88,24},{96,32},{104,40},{112,48},{120,56},{... | collective-permute-start | bytes 159752 | tf_op jit(solution)/shard_map/rims_y/ppermute | solution.py:363
  9.5 0.1 pad_add_fusion.own
  9.6 0.7 copy-done.1
  10.3 2.4 %prepare.1 = (bf16[288,864]{1,0:T(8,128)(2,1)S(1)}, bf16[288,864]{1,0:T(8,128)(2,1)S(1)}, s32[8,1920]{1,0:T(8,128)S(1)}, bf16[16,128]{1,0:T(8,128)(2,1)S(1)}, bf16[16,256]{1,0:T(8,128)(2,1)S(1)}) custom-call(s32[1,27]{1,0:T(1,128)S(1)} %copy-done.1, s32[2]{0:T(128)S(1)} %pad_add_fusion.own, bf16[96,2592]{1,0:T(8,128)(2,1)} %first_in.3, ...), custom_call_target="tpu_custom_call" | custom-call | tf_op jit(solution)/shard_map/prepare/pallas_call | solution.py:383
  12.7 0.0 collective-permute-done.ym
  12.7 3.1 %collective-permute-done.1.yp = bf16[208,128]{1,0:T(8,128)(2,1)S(1)} collective-permute-done((bf16[208,128]{1,0:T(8,128)(2,1)S(1)}, bf16[208,128]{1,0:T(8,128)(2,1)S(1)}, u32[]{:S(2)}, u32[]{:S(2)}) %collective-permute-start.1) | collective-permute-done | bytes 53280 | tf_op jit(solution)/shard_map/rims_y/ppermute | solution.py:363
  15.9 0.1 slabs.1
  16.0 3.2 %collective-permute-start.2 = (bf16[208,256]{1,0:T(8,128)(2,1)S(1)}, bf16[208,256]{1,0:T(8,128)(2,1)S(1)}, u32[]{:S(2)}, u32[]{:S(2)}) collective-permute-start(bf16[208,256]{1,0:T(8,128)(2,1)S(1)} %get-tuple-element.39), channel_id=1, source_target_pairs={{0,8},{8,16},{16,24},{24,32},{32,40},{40,48},{48,56},{64,72},{72,8... | collective-permute-start | bytes 319496 | tf_op jit(solution)/shard_map/rims_x/ppermute | solution.py:363
  19.2 1.3 %collective-permute-start.3 = (bf16[208,256]{1,0:T(8,128)(2,1)S(1)}, bf16[208,256]{1,0:T(8,128)(2,1)S(1)}, u32[]{:S(2)}, u32[]{:S(2)}) collective-permute-start(bf16[208,256]{1,0:T(8,128)(2,1)S(1)} %get-tuple-element.40), channel_id=1, source_target_pairs={{8,0},{16,8},{24,16},{32,24},{40,32},{48,40},{56,48},{72,64},{80,7... | collective-permute-start | bytes 319496 | tf_op jit(solution)/shard_map/rims_x/ppermute | solution.py:363
  20.5 1.3 %place.1 = (bf16[208,1920]{1,0:T(8,128)(2,1)S(1)}, bf16[256,1920]{1,0:T(8,128)(2,1)S(1)}) custom-call(bf16[208,128]{1,0:T(8,128)(2,1)S(1)} %get-tuple-element.35.first.q0, bf16[208,128]{1,0:T(8,128)(2,1)S(1)} %get-tuple-element.41.q1, bf16[208,128]{1,0:T(8,128)(2,1)S(1)} %get-tuple-element.42.q2, bf16[208,128]{1,0:T(8,128)(2,1)S(1)} %get-tuple-element.36.last.q3, ...), custom_call_target="tpu_custom_call" | custom-call | tf_op jit(solution)/shard_map/place/pallas_call | solution.py:400
  21.8 0.0 collective-permute-done.2.xm
  21.9 2.8 %collective-permute-done.3.xp = bf16[208,256]{1,0:T(8,128)(2,1)S(1)} collective-permute-done((bf16[208,256]{1,0:T(8,128)(2,1)S(1)}, bf16[208,256]{1,0:T(8,128)(2,1)S(1)}, u32[]{:S(2)}, u32[]{:S(2)}) %collective-permute-start.3) | collective-permute-done | bytes 106528 | tf_op jit(solution)/shard_map/rims_x/ppermute | solution.py:363
  24.6 5.5 %middle.1 = (f32[128,16,128]{2,1,0:T(8,128)S(1)}, bf16[208,1920]{1,0:T(8,128)(2,1)S(1)}, bf16[96,1536]{1,0:T(8,128)(2,1)S(1)}, bf16[96,1536]{1,0:T(8,128)(2,1)S(...) custom-call(s32[2]{0:T(128)S(1)} %pad_add_fusion.own, ...), custom_call_target="tpu_custom_call" | custom-call | tf_op jit(solution)/shard_map/middle/pallas_call | solution.py:409
  30.2 5.7 %collective-permute-start.4 = (f32[128,16,128]{2,1,0:T(8,128)S(1)}, f32[128,16,128]{2,1,0:T(8,128)S(1)}, u32[]{:S(2)}, u32[]{:S(2)}) collective-permute-start(f32[128,16,128]{2,1,0:T(8,128)S(1)} %get-tuple-element.51), channel_id=1, source_target_pairs={{0,1},{1,0},{2,3},{3,2},{4,5},{5,4},{6,7},{7,6},{8,9},{9,8},{10,11... | collective-permute-start | bytes 3145736 | tf_op jit(solution)/shard_map/pair/ppermute | solution.py:367
  35.9 2.0 %keep.1 = f32[128,16,128]{2,1,0:T(8,128)S(1)} custom-call(s32[2]{0:T(128)S(1)} %pad_add_fusion.own, bf16[2,96,1536]{2,1,0:T(8,128)(2,1)S(1)} %get-tuple-element.49.inner, bf16[2,864,1536]{2,1,0:T(8,128)(2,1)S(1)} %get-tuple-element.50.columns), custom_call_target="tpu_custom_call" | custom-call | tf_op jit(solution)/shard_map/keep/pallas_call | solution.py:419
  37.9 0.3 collective-permute-done.4.other
  38.2 0.4 pair.1
  38.6 19.3 %all_to_all.15.coded = s16[32,5,16,128]{3,2,1,0:T(8,128)(2,1)S(1)} all-to-all(s16[32,5,16,128]{3,2,1,0:T(8,128)(2,1)S(1)} %pair.1), channel_id=1, replica_groups=mesh['zh'=8,'zl'=2,'y'=4,'x'=4,'core'=2] {'zl','y','x'}, dimensions={0} | all-to-all | bytes 1310720 | tf_op jit(solution)/shard_map/sum/all_to_all | solution.py:426
  57.9 0.9 sum.1.after
  58.8 11.4 %all-to-all-start.1 = ((bf16[8,4,16,128]{3,2,1,0:T(8,128)(2,1)}), bf16[8,4,16,128]{3,2,1,0:T(8,128)(2,1)S(1)}, u32[]{:S(2)}, u32[]{:S(2)}) async-start(bf16[8,4,16,128]{3,2,1,0:T(8,128)(2,1)} %sum.1.after), calls=%async_computation.1 | async-start | bytes 262144 | tf_op jit(solution)/shard_map/sum/all_to_all | solution.py:428
  70.2 2.0 %late_weights.1 = (bf16[288,864]{1,0:T(8,128)(2,1)S(1)}, bf16[288,864]{1,0:T(8,128)(2,1)S(1)}) custom-call(bf16[8,4,16,128]{3,2,1,0:T(8,128)(2,1)} %sum.1.after, bf16[96,2592]{1,0:T(8,128)(2,1)} %first_in.3, bf16[96,2592]{1,0:T(8,128)(2,1)} %second_in.3), custom_call_target="tpu_custom_call" | custom-call | tf_op jit(solution)/shard_map/late_weights/pallas_call | solution.py:430
  72.3 3.8 %outputs.1 = (bf16[1,96,512]{2,1,0:T(8,128)(2,1)}, bf16[1,96,512]{2,1,0:T(8,128)(2,1)}, f32[8,128]{1,0:T(8,128)S(1)}) custom-call(bf16[8,4,16,128]{3,2,1,0:T(8,128)(2,1)} %sum.1.after, bf16[208,1920]{1,0:T(8,128)(2,1)S(1)} %get-tuple-element.52.padded, bf16[96,1536]{1,0:T(8,128)(2,1)S(1)} %get-tuple-element.53.hidden, ...), custom_call_target="tpu_custom_call" | custom-call | tf_op jit(solution)/shard_map/outputs/pallas_call | solution.py:434
  76.0 8.1 %all-to-all-done.1.refs_0_ = bf16[8,4,16,128]{3,2,1,0:T(8,128)(2,1)S(1)} async-done(((bf16[8,4,16,128]{3,2,1,0:T(8,128)(2,1)}), bf16[8,4,16,128]{3,2,1,0:T(8,128)(2,1)S(1)}, u32[]{:S(2)}, u32[]{:S(2)}) %all-to-all-start.1) | async-done | bytes 131104 | tf_op jit(solution)/shard_map/sum/all_to_all | solution.py:428
  84.2 0.1 shares.1
  84.2 14.1 %all_to_all.16 = bf16[32,4,16,128]{3,2,1,0:T(8,128)(2,1)S(1)} all-to-all(bf16[32,4,16,128]{3,2,1,0:T(8,128)(2,1)S(1)} %shares.1), channel_id=1, replica_groups=mesh['zh'=8,'zl'=2,'y'=4,'x'=4,'core'=2] {'zl','y','x'}, dimensions={0} | all-to-all | bytes 1048576 | tf_op jit(solution)/shard_map/shares/all_to_all | solution.py:444
  98.3 5.7 %collective-permute-start.5 = (bf16[128,16,128]{2,1,0:T(8,128)(2,1)S(1)}, bf16[128,16,128]{2,1,0:T(8,128)(2,1)S(1)}, u32[]{:S(2)}, u32[]{:S(2)}) collective-permute-start(bf16[128,16,128]{2,1,0:T(8,128)(2,1)S(1)} %bitcast.3), channel_id=1, source_target_pairs={{0,1},{1,0},{2,3},{3,2},{4,5},{5,4},{6,7},{7,6},{8,9},{9,8},{10,11... | collective-permute-start | bytes 1572872 | tf_op jit(solution)/shard_map/shares/ppermute | solution.py:367
  104.0 1.6 %mine.1 = (f32[96,2592]{1,0:T(8,128)}, f32[96,2592]{1,0:T(8,128)}) custom-call(s32[2]{0:T(128)S(1)} %pad_add_fusion.own, bf16[128,16,128]{2,1,0:T(8,128)(2,1)S(1)} %bitcast.4), custom_call_target="tpu_custom_call" | custom-call | tf_op jit(solution)/shard_map/mine/pallas_call | solution.py:448
  105.6 0.0 collective-permute-done.5.half
  105.6 1.6 %other.1 = (f32[96,2592]{1,0:T(8,128)}, f32[96,2592]{1,0:T(8,128)}) custom-call(s32[2]{0:T(128)S(1)} %pad_add_fusion.own, bf16[128,16,128]{2,1,0:T(8,128)(2,1)S(1)} %collective-permute-done.5.half, f32[96,2592]{1,0:T(8,128)} %get-tuple-element.60.first_in, f32[96,2592]{1,0:T(8,128)} %get-tuple-element.61.second_in), custom_call_target="tpu_custom_call", output_to_operand_aliasing={{0}: (2, {}), {1}: (3, {})} | custom-call | tf_op jit(solution)/shard_map/other/pallas_call | solution.py:450
  (2 shorter events, 0.0 us)
Async XLA Ops:
  0.6 0.7 copy-start
  2.5 10.2 %collective-permute-start = (bf16[208,128]{1,0:T(8,128)(2,1)S(1)}, bf16[208,128]{1,0:T(8,128)(2,1)S(1)}, u32[]{:S(2)}, u32[]{:S(2)}) collective-permute-start(bf16[208,128]{1,0:T(8,128)(2,1)S(1)} %get-tuple-element.37), channel_id=1, source_target_pairs={{0,64},{8,72},{16,80},{24,88},{32,96},{40,104},{48,112},{56,120},{... | collective-permute-start | bytes 159752 | tf_op jit(solution)/shard_map/rims_y/ppermute | solution.py:363
  8.2 7.6 %collective-permute-start.1 = (bf16[208,128]{1,0:T(8,128)(2,1)S(1)}, bf16[208,128]{1,0:T(8,128)(2,1)S(1)}, u32[]{:S(2)}, u32[]{:S(2)}) collective-permute-start(bf16[208,128]{1,0:T(8,128)(2,1)S(1)} %get-tuple-element.38), channel_id=1, source_target_pairs={{64,0},{72,8},{80,16},{88,24},{96,32},{104,40},{112,48},{120,56},{... | collective-permute-start | bytes 159752 | tf_op jit(solution)/shard_map/rims_y/ppermute | solution.py:363
  9.6 0.7 copy-start.1
  16.0 5.9 %collective-permute-start.2 = (bf16[208,256]{1,0:T(8,128)(2,1)S(1)}, bf16[208,256]{1,0:T(8,128)(2,1)S(1)}, u32[]{:S(2)}, u32[]{:S(2)}) collective-permute-start(bf16[208,256]{1,0:T(8,128)(2,1)S(1)} %get-tuple-element.39), channel_id=1, source_target_pairs={{0,8},{8,16},{16,24},{24,32},{32,40},{40,48},{48,56},{64,72},{72,8... | collective-permute-start | bytes 319496 | tf_op jit(solution)/shard_map/rims_x/ppermute | solution.py:363
  19.2 5.4 %collective-permute-start.3 = (bf16[208,256]{1,0:T(8,128)(2,1)S(1)}, bf16[208,256]{1,0:T(8,128)(2,1)S(1)}, u32[]{:S(2)}, u32[]{:S(2)}) collective-permute-start(bf16[208,256]{1,0:T(8,128)(2,1)S(1)} %get-tuple-element.40), channel_id=1, source_target_pairs={{8,0},{16,8},{24,16},{32,24},{40,32},{48,40},{56,48},{72,64},{80,7... | collective-permute-start | bytes 319496 | tf_op jit(solution)/shard_map/rims_x/ppermute | solution.py:363
  30.2 8.0 %collective-permute-start.4 = (f32[128,16,128]{2,1,0:T(8,128)S(1)}, f32[128,16,128]{2,1,0:T(8,128)S(1)}, u32[]{:S(2)}, u32[]{:S(2)}) collective-permute-start(f32[128,16,128]{2,1,0:T(8,128)S(1)} %get-tuple-element.51), channel_id=1, source_target_pairs={{0,1},{1,0},{2,3},{3,2},{4,5},{5,4},{6,7},{7,6},{8,9},{9,8},{10,11... | collective-permute-start | bytes 3145736 | tf_op jit(solution)/shard_map/pair/ppermute | solution.py:367
  58.8 25.4 %all-to-all-start.1 = ((bf16[8,4,16,128]{3,2,1,0:T(8,128)(2,1)}), bf16[8,4,16,128]{3,2,1,0:T(8,128)(2,1)S(1)}, u32[]{:S(2)}, u32[]{:S(2)}) async-start(bf16[8,4,16,128]{3,2,1,0:T(8,128)(2,1)} %sum.1.after), calls=%async_computation.1 | async-start | bytes 262144 | tf_op jit(solution)/shard_map/sum/all_to_all | solution.py:428
  98.3 7.3 %collective-permute-start.5 = (bf16[128,16,128]{2,1,0:T(8,128)(2,1)S(1)}, bf16[128,16,128]{2,1,0:T(8,128)(2,1)S(1)}, u32[]{:S(2)}, u32[]{:S(2)}) collective-permute-start(bf16[128,16,128]{2,1,0:T(8,128)(2,1)S(1)} %bitcast.3), channel_id=1, source_target_pairs={{0,1},{1,0},{2,3},{3,2},{4,5},{5,4},{6,7},{7,6},{8,9},{9,8},{10,11... | collective-permute-start | bytes 1572872 | tf_op jit(solution)/shard_map/shares/ppermute | solution.py:367

commit v7 on v6

--- a/solution.py
+++ b/solution.py
@@ -268,24 +268,35 @@
         out[0] = jnp.dot(wide, squeeze, preferred_element_type=F32).astype(BF16)
 
 
+def power_of_two(exponent):
+    power = jnp.ones(exponent.shape, F32)
+    for sign in (1.0, -1.0):
+        rest = jnp.maximum(exponent * sign, 0.0)
+        for bit in (64.0, 32.0, 16.0, 8.0, 4.0, 2.0, 1.0):
+            has = rest >= bit
+            power = jnp.where(has, power * 2.0 ** (sign * bit), power)
+            rest = jnp.where(has, rest - bit, rest)
+    return power
+
+
 def pair_kernel(keep, other, coded):
     for number in range(32):
         tiles = slice(number * 4, number * 4 + 4)
         total = keep[tiles] + other[tiles]
         most = jnp.maximum(jnp.max(jnp.abs(total), axis=1), 1e-30)
         exponent = jnp.ceil(jnp.log2(most))
-        values = jnp.round(total * jnp.exp2(14.0 - exponent)[:, None, :])
-        coded[number, 0:4] = values.astype(jnp.int32).astype(jnp.int16)
-        rows = jnp.concatenate([exponent, jnp.zeros((12, 128), F32)], axis=0)
-        coded[number, 4] = rows.astype(jnp.int32).astype(jnp.int16)
+        values = jnp.round(total * power_of_two(14.0 - exponent)[:, None, :])
+        coded[number, 0:64] = values.astype(jnp.int32).astype(jnp.int16).reshape(64, 128)
+        rows = jnp.concatenate([exponent, jnp.zeros((4, 128), F32)], axis=0)
+        coded[number, 64:72] = rows.astype(jnp.int32).astype(jnp.int16)
 
 
 def decode_kernel(coded, copies):
     total = jnp.zeros((4, 16, 128), F32)
     for number in range(32):
-        exponent = coded[number, 4].astype(jnp.int32).astype(F32)[0:4]
-        values = coded[number, 0:4].astype(jnp.int32).astype(F32)
-        total = total + values * jnp.exp2(exponent - 14.0)[:, None, :]
+        exponent = coded[number, 64:72].astype(jnp.int32).astype(F32)[0:4]
+        values = coded[number, 0:64].astype(jnp.int32).astype(F32).reshape(4, 16, 128)
+        total = total + values * power_of_two(exponent - 14.0)[:, None, :]
     for number in range(copies.shape[0]):
         copies[number] = total.astype(BF16)
 
@@ -418,7 +429,7 @@
     with jax.named_scope("keep"):
         (keep,) = call(keep_kernel, [half], [SMEM] + [VMEM] * 2, [grads])(own, inner, columns)
     with jax.named_scope("pair"):
-        (coded,) = call(pair_kernel, [((32, 5, 16, 128), jnp.int16)], [VMEM] * 2)(
+        (coded,) = call(pair_kernel, [((32, 72, 128), jnp.int16)], [VMEM] * 2)(
             keep, swap_halves(send)
         )
     near, far = ("zl", "y", "x"), "zh"

time: 108 us -> 109 us (level)
  Pallas kernels: 22.9 us -> 24.3 us
    pallas_call x1, Pallas kernels: 0.4 us -> 1.56 us  [body(): call(pair_kernel, [((32, 72, 128), jnp.int16)], [VMEM] * 2)]
where the time goes in v7:
time: 109 us; the launch traced here: 108 us
  starting transfers between devices  34.4 us (32%)
  blocking collectives  32.7 us (30%)
  Pallas kernels  24.3 us (22%)
  waiting for transfers between devices  14.3 us (13%)
  local copies, waits for them, and re-layouts  1.33 us (1%)
    all_to_all x1, blocking collectives, body(): parts = lax.all_to_all(coded, near, 0, 0)  19 us
    all_to_all x1, blocking collectives, body(): mine = lax.all_to_all(copies, near, 0, 0).reshape(128, 16, 128)  13.7 us
    ppermute x4, starting transfers between devices, from_owner(): return lax.ppermute(value, ('zh', 'zl', 'y'), pairs)  11.5 us
    ppermute x2, starting transfers between devices, swap_halves(): return lax.ppermute(value, 'core', [(0, 1), (1, 0)])  11.5 us
    all_to_all x1, starting transfers between devices, body(): parts = lax.all_to_all(copies, far, 0, 0)  11.4 us
    all_to_all x1, waiting for transfers between devices, body(): parts = lax.all_to_all(copies, far, 0, 0)  8.1 us
    ppermute x4, waiting for transfers between devices, from_owner(): return lax.ppermute(value, ('zh', 'zl', 'y'), pairs)  5.93 us
    pallas_call x1, Pallas kernels, body(): call(main_kernel, [half, ((ROWS, LANES), BF16), outer, outer, ((2, C, OUT...  5.54 us
  transfers between devices with their start and end apart: 7, of which 4 were waited for; matrix products, arithmetic and copies ran while one was open for 0% of the time, Pallas kernels for 12%

profile of v7, /device:TPU:1, one launch (start us, length us, event | category | flops | bytes accessed | tf_op | source)
XLA Modules:
  0.0 108.1 jit_solution(5578858160794605894)
XLA Ops:
  0.6 0.7 copy-done
  1.3 1.2 %pack.1 = (bf16[208,128]{1,0:T(8,128)(2,1)S(1)}, bf16[208,128]{1,0:T(8,128)(2,1)S(1)}, bf16[208,128]{1,0:T(8,128)(2,1)S(1)}, bf16[208,128]{1,0:T(8,128)(2,1)S(1)...) custom-call(bf16[1,96,512]{2,1,0:T(8,128)(2,1)} %feats_in.1, bf16[1,96,512]{2,1,0:T(8,128)(2,1)} %cot_in.1, ...), custom_call_target="tpu_custom_call" | custom-call | tf_op jit(solution)/shard_map/pack/pallas_call | solution.py:390
  2.5 5.7 %collective-permute-start = (bf16[208,128]{1,0:T(8,128)(2,1)S(1)}, bf16[208,128]{1,0:T(8,128)(2,1)S(1)}, u32[]{:S(2)}, u32[]{:S(2)}) collective-permute-start(bf16[208,128]{1,0:T(8,128)(2,1)S(1)} %get-tuple-element.37), channel_id=1, source_target_pairs={{0,64},{8,72},{16,80},{24,88},{32,96},{40,104},{48,112},{56,120},{... | collective-permute-start | bytes 159752 | tf_op jit(solution)/shard_map/rims_y/ppermute | solution.py:374
  8.2 1.3 %collective-permute-start.1 = (bf16[208,128]{1,0:T(8,128)(2,1)S(1)}, bf16[208,128]{1,0:T(8,128)(2,1)S(1)}, u32[]{:S(2)}, u32[]{:S(2)}) collective-permute-start(bf16[208,128]{1,0:T(8,128)(2,1)S(1)} %get-tuple-element.38), channel_id=1, source_target_pairs={{64,0},{72,8},{80,16},{88,24},{96,32},{104,40},{112,48},{120,56},{... | collective-permute-start | bytes 159752 | tf_op jit(solution)/shard_map/rims_y/ppermute | solution.py:374
  9.5 0.1 pad_add_fusion.own
  9.6 0.7 copy-done.1
  10.3 2.4 %prepare.1 = (bf16[288,864]{1,0:T(8,128)(2,1)S(1)}, bf16[288,864]{1,0:T(8,128)(2,1)S(1)}, s32[8,1920]{1,0:T(8,128)S(1)}, bf16[16,128]{1,0:T(8,128)(2,1)S(1)}, bf16[16,256]{1,0:T(8,128)(2,1)S(1)}) custom-call(s32[1,27]{1,0:T(1,128)S(1)} %copy-done.1, s32[2]{0:T(128)S(1)} %pad_add_fusion.own, bf16[96,2592]{1,0:T(8,128)(2,1)} %first_in.3, ...), custom_call_target="tpu_custom_call" | custom-call | tf_op jit(solution)/shard_map/prepare/pallas_call | solution.py:394
  12.7 0.0 collective-permute-done.ym
  12.7 3.1 %collective-permute-done.1.yp = bf16[208,128]{1,0:T(8,128)(2,1)S(1)} collective-permute-done((bf16[208,128]{1,0:T(8,128)(2,1)S(1)}, bf16[208,128]{1,0:T(8,128)(2,1)S(1)}, u32[]{:S(2)}, u32[]{:S(2)}) %collective-permute-start.1) | collective-permute-done | bytes 53280 | tf_op jit(solution)/shard_map/rims_y/ppermute | solution.py:374
  15.9 0.1 slabs.1
  16.0 3.2 %collective-permute-start.2 = (bf16[208,256]{1,0:T(8,128)(2,1)S(1)}, bf16[208,256]{1,0:T(8,128)(2,1)S(1)}, u32[]{:S(2)}, u32[]{:S(2)}) collective-permute-start(bf16[208,256]{1,0:T(8,128)(2,1)S(1)} %get-tuple-element.39), channel_id=1, source_target_pairs={{0,8},{8,16},{16,24},{24,32},{32,40},{40,48},{48,56},{64,72},{72,8... | collective-permute-start | bytes 319496 | tf_op jit(solution)/shard_map/rims_x/ppermute | solution.py:374
  19.2 1.3 %collective-permute-start.3 = (bf16[208,256]{1,0:T(8,128)(2,1)S(1)}, bf16[208,256]{1,0:T(8,128)(2,1)S(1)}, u32[]{:S(2)}, u32[]{:S(2)}) collective-permute-start(bf16[208,256]{1,0:T(8,128)(2,1)S(1)} %get-tuple-element.40), channel_id=1, source_target_pairs={{8,0},{16,8},{24,16},{32,24},{40,32},{48,40},{56,48},{72,64},{80,7... | collective-permute-start | bytes 319496 | tf_op jit(solution)/shard_map/rims_x/ppermute | solution.py:374
  20.5 1.3 %place.1 = (bf16[208,1920]{1,0:T(8,128)(2,1)S(1)}, bf16[256,1920]{1,0:T(8,128)(2,1)S(1)}) custom-call(bf16[208,128]{1,0:T(8,128)(2,1)S(1)} %get-tuple-element.35.first.q0, bf16[208,128]{1,0:T(8,128)(2,1)S(1)} %get-tuple-element.41.q1, bf16[208,128]{1,0:T(8,128)(2,1)S(1)} %get-tuple-element.42.q2, bf16[208,128]{1,0:T(8,128)(2,1)S(1)} %get-tuple-element.36.last.q3, ...), custom_call_target="tpu_custom_call" | custom-call | tf_op jit(solution)/shard_map/place/pallas_call | solution.py:411
  21.8 0.0 collective-permute-done.2.xm
  21.9 2.8 %collective-permute-done.3.xp = bf16[208,256]{1,0:T(8,128)(2,1)S(1)} collective-permute-done((bf16[208,256]{1,0:T(8,128)(2,1)S(1)}, bf16[208,256]{1,0:T(8,128)(2,1)S(1)}, u32[]{:S(2)}, u32[]{:S(2)}) %collective-permute-start.3) | collective-permute-done | bytes 106528 | tf_op jit(solution)/shard_map/rims_x/ppermute | solution.py:374
  24.6 5.5 %middle.1 = (f32[128,16,128]{2,1,0:T(8,128)S(1)}, bf16[208,1920]{1,0:T(8,128)(2,1)S(1)}, bf16[96,1536]{1,0:T(8,128)(2,1)S(1)}, bf16[96,1536]{1,0:T(8,128)(2,1)S(...) custom-call(s32[2]{0:T(128)S(1)} %pad_add_fusion.own, ...), custom_call_target="tpu_custom_call" | custom-call | tf_op jit(solution)/shard_map/middle/pallas_call | solution.py:420
  30.2 5.7 %collective-permute-start.4 = (f32[128,16,128]{2,1,0:T(8,128)S(1)}, f32[128,16,128]{2,1,0:T(8,128)S(1)}, u32[]{:S(2)}, u32[]{:S(2)}) collective-permute-start(f32[128,16,128]{2,1,0:T(8,128)S(1)} %get-tuple-element.51), channel_id=1, source_target_pairs={{0,1},{1,0},{2,3},{3,2},{4,5},{5,4},{6,7},{7,6},{8,9},{9,8},{10,11... | collective-permute-start | bytes 3145736 | tf_op jit(solution)/shard_map/pair/ppermute | solution.py:378
  35.9 2.0 %keep.1 = f32[128,16,128]{2,1,0:T(8,128)S(1)} custom-call(s32[2]{0:T(128)S(1)} %pad_add_fusion.own, bf16[2,96,1536]{2,1,0:T(8,128)(2,1)S(1)} %get-tuple-element.49.inner, bf16[2,864,1536]{2,1,0:T(8,128)(2,1)S(1)} %get-tuple-element.50.columns), custom_call_target="tpu_custom_call" | custom-call | tf_op jit(solution)/shard_map/keep/pallas_call | solution.py:430
  37.9 0.3 collective-permute-done.4.other
  38.2 1.6 %pair.1 = s16[32,72,128]{2,1,0:T(8,128)(2,1)S(1)} custom-call(f32[128,16,128]{2,1,0:T(8,128)S(1)} %keep.1, f32[128,16,128]{2,1,0:T(8,128)S(1)} %collective-permute-done.4.other), custom_call_target="tpu_custom_call" | custom-call | tf_op jit(solution)/shard_map/pair/pallas_call | solution.py:432
  39.8 19.0 %all_to_all.15.coded = s16[32,72,128]{2,1,0:T(8,128)(2,1)S(1)} all-to-all(s16[32,72,128]{2,1,0:T(8,128)(2,1)S(1)} %pair.1), channel_id=1, replica_groups=mesh['zh'=8,'zl'=2,'y'=4,'x'=4,'core'=2] {'zl','y','x'}, dimensions={0} | all-to-all | bytes 1179648 | tf_op jit(solution)/shard_map/sum/all_to_all | solution.py:437
  58.8 1.1 %sum.1.after = bf16[8,4,16,128]{3,2,1,0:T(8,128)(2,1)} custom-call(s16[32,72,128]{2,1,0:T(8,128)(2,1)S(1)} %all_to_all.15.coded), custom_call_target="tpu_custom_call" | custom-call | tf_op jit(solution)/shard_map/sum/pallas_call | solution.py:438
  59.9 11.4 %all-to-all-start.1 = ((bf16[8,4,16,128]{3,2,1,0:T(8,128)(2,1)}), bf16[8,4,16,128]{3,2,1,0:T(8,128)(2,1)S(1)}, u32[]{:S(2)}, u32[]{:S(2)}) async-start(bf16[8,4,16,128]{3,2,1,0:T(8,128)(2,1)} %sum.1.after), calls=%async_computation.1 | async-start | bytes 262144 | tf_op jit(solution)/shard_map/sum/all_to_all | solution.py:439
  71.3 2.0 %late_weights.1 = (bf16[288,864]{1,0:T(8,128)(2,1)S(1)}, bf16[288,864]{1,0:T(8,128)(2,1)S(1)}) custom-call(bf16[8,4,16,128]{3,2,1,0:T(8,128)(2,1)} %sum.1.after, bf16[96,2592]{1,0:T(8,128)(2,1)} %first_in.3, bf16[96,2592]{1,0:T(8,128)(2,1)} %second_in.3), custom_call_target="tpu_custom_call" | custom-call | tf_op jit(solution)/shard_map/late_weights/pallas_call | solution.py:441
  73.4 3.8 %outputs.1 = (bf16[1,96,512]{2,1,0:T(8,128)(2,1)}, bf16[1,96,512]{2,1,0:T(8,128)(2,1)}, f32[8,128]{1,0:T(8,128)S(1)}) custom-call(bf16[8,4,16,128]{3,2,1,0:T(8,128)(2,1)} %sum.1.after, bf16[208,1920]{1,0:T(8,128)(2,1)S(1)} %get-tuple-element.52.padded, bf16[96,1536]{1,0:T(8,128)(2,1)S(1)} %get-tuple-element.53.hidden, ...), custom_call_target="tpu_custom_call" | custom-call | tf_op jit(solution)/shard_map/outputs/pallas_call | solution.py:445
  77.1 8.1 %all-to-all-done.1.refs_0_ = bf16[8,4,16,128]{3,2,1,0:T(8,128)(2,1)S(1)} async-done(((bf16[8,4,16,128]{3,2,1,0:T(8,128)(2,1)}), bf16[8,4,16,128]{3,2,1,0:T(8,128)(2,1)S(1)}, u32[]{:S(2)}, u32[]{:S(2)}) %all-to-all-start.1) | async-done | bytes 131104 | tf_op jit(solution)/shard_map/sum/all_to_all | solution.py:439
  85.2 0.1 shares.1
  85.3 13.7 %all_to_all.16 = bf16[32,4,16,128]{3,2,1,0:T(8,128)(2,1)S(1)} all-to-all(bf16[32,4,16,128]{3,2,1,0:T(8,128)(2,1)S(1)} %shares.1), channel_id=1, replica_groups=mesh['zh'=8,'zl'=2,'y'=4,'x'=4,'core'=2] {'zl','y','x'}, dimensions={0} | all-to-all | bytes 1048576 | tf_op jit(solution)/shard_map/shares/all_to_all | solution.py:455
  99.0 5.7 %collective-permute-start.5 = (bf16[128,16,128]{2,1,0:T(8,128)(2,1)S(1)}, bf16[128,16,128]{2,1,0:T(8,128)(2,1)S(1)}, u32[]{:S(2)}, u32[]{:S(2)}) collective-permute-start(bf16[128,16,128]{2,1,0:T(8,128)(2,1)S(1)} %bitcast.3), channel_id=1, source_target_pairs={{0,1},{1,0},{2,3},{3,2},{4,5},{5,4},{6,7},{7,6},{8,9},{9,8},{10,11... | collective-permute-start | bytes 1572872 | tf_op jit(solution)/shard_map/shares/ppermute | solution.py:378
  104.7 1.6 %mine.1 = (f32[96,2592]{1,0:T(8,128)}, f32[96,2592]{1,0:T(8,128)}) custom-call(s32[2]{0:T(128)S(1)} %pad_add_fusion.own, bf16[128,16,128]{2,1,0:T(8,128)(2,1)S(1)} %bitcast.4), custom_call_target="tpu_custom_call" | custom-call | tf_op jit(solution)/shard_map/mine/pallas_call | solution.py:459
  106.3 0.0 collective-permute-done.5.half
  106.3 1.6 %other.1 = (f32[96,2592]{1,0:T(8,128)}, f32[96,2592]{1,0:T(8,128)}) custom-call(s32[2]{0:T(128)S(1)} %pad_add_fusion.own, bf16[128,16,128]{2,1,0:T(8,128)(2,1)S(1)} %collective-permute-done.5.half, f32[96,2592]{1,0:T(8,128)} %get-tuple-element.60.first_in, f32[96,2592]{1,0:T(8,128)} %get-tuple-element.61.second_in), custom_call_target="tpu_custom_call", output_to_operand_aliasing={{0}: (2, {}), {1}: (3, {})} | custom-call | tf_op jit(solution)/shard_map/other/pallas_call | solution.py:461
  (2 shorter events, 0.0 us)
Async XLA Ops:
  0.6 0.7 copy-start
  2.5 10.2 %collective-permute-start = (bf16[208,128]{1,0:T(8,128)(2,1)S(1)}, bf16[208,128]{1,0:T(8,128)(2,1)S(1)}, u32[]{:S(2)}, u32[]{:S(2)}) collective-permute-start(bf16[208,128]{1,0:T(8,128)(2,1)S(1)} %get-tuple-element.37), channel_id=1, source_target_pairs={{0,64},{8,72},{16,80},{24,88},{32,96},{40,104},{48,112},{56,120},{... | collective-permute-start | bytes 159752 | tf_op jit(solution)/shard_map/rims_y/ppermute | solution.py:374
  8.2 7.6 %collective-permute-start.1 = (bf16[208,128]{1,0:T(8,128)(2,1)S(1)}, bf16[208,128]{1,0:T(8,128)(2,1)S(1)}, u32[]{:S(2)}, u32[]{:S(2)}) collective-permute-start(bf16[208,128]{1,0:T(8,128)(2,1)S(1)} %get-tuple-element.38), channel_id=1, source_target_pairs={{64,0},{72,8},{80,16},{88,24},{96,32},{104,40},{112,48},{120,56},{... | collective-permute-start | bytes 159752 | tf_op jit(solution)/shard_map/rims_y/ppermute | solution.py:374
  9.6 0.7 copy-start.1
  16.0 5.9 %collective-permute-start.2 = (bf16[208,256]{1,0:T(8,128)(2,1)S(1)}, bf16[208,256]{1,0:T(8,128)(2,1)S(1)}, u32[]{:S(2)}, u32[]{:S(2)}) collective-permute-start(bf16[208,256]{1,0:T(8,128)(2,1)S(1)} %get-tuple-element.39), channel_id=1, source_target_pairs={{0,8},{8,16},{16,24},{24,32},{32,40},{40,48},{48,56},{64,72},{72,8... | collective-permute-start | bytes 319496 | tf_op jit(solution)/shard_map/rims_x/ppermute | solution.py:374
  19.2 5.4 %collective-permute-start.3 = (bf16[208,256]{1,0:T(8,128)(2,1)S(1)}, bf16[208,256]{1,0:T(8,128)(2,1)S(1)}, u32[]{:S(2)}, u32[]{:S(2)}) collective-permute-start(bf16[208,256]{1,0:T(8,128)(2,1)S(1)} %get-tuple-element.40), channel_id=1, source_target_pairs={{8,0},{16,8},{24,16},{32,24},{40,32},{48,40},{56,48},{72,64},{80,7... | collective-permute-start | bytes 319496 | tf_op jit(solution)/shard_map/rims_x/ppermute | solution.py:374
  30.2 8.0 %collective-permute-start.4 = (f32[128,16,128]{2,1,0:T(8,128)S(1)}, f32[128,16,128]{2,1,0:T(8,128)S(1)}, u32[]{:S(2)}, u32[]{:S(2)}) collective-permute-start(f32[128,16,128]{2,1,0:T(8,128)S(1)} %get-tuple-element.51), channel_id=1, source_target_pairs={{0,1},{1,0},{2,3},{3,2},{4,5},{5,4},{6,7},{7,6},{8,9},{9,8},{10,11... | collective-permute-start | bytes 3145736 | tf_op jit(solution)/shard_map/pair/ppermute | solution.py:378
  59.9 25.3 %all-to-all-start.1 = ((bf16[8,4,16,128]{3,2,1,0:T(8,128)(2,1)}), bf16[8,4,16,128]{3,2,1,0:T(8,128)(2,1)S(1)}, u32[]{:S(2)}, u32[]{:S(2)}) async-start(bf16[8,4,16,128]{3,2,1,0:T(8,128)(2,1)} %sum.1.after), calls=%async_computation.1 | async-start | bytes 262144 | tf_op jit(solution)/shard_map/sum/all_to_all | solution.py:439
  99.0 7.3 %collective-permute-start.5 = (bf16[128,16,128]{2,1,0:T(8,128)(2,1)S(1)}, bf16[128,16,128]{2,1,0:T(8,128)(2,1)S(1)}, u32[]{:S(2)}, u32[]{:S(2)}) collective-permute-start(bf16[128,16,128]{2,1,0:T(8,128)(2,1)S(1)} %bitcast.3), channel_id=1, source_target_pairs={{0,1},{1,0},{2,3},{3,2},{4,5},{5,4},{6,7},{7,6},{8,9},{9,8},{10,11... | collective-permute-start | bytes 1572872 | tf_op jit(solution)/shard_map/shares/ppermute | solution.py:378

commit v8 on v6

--- a/solution.py
+++ b/solution.py
@@ -161,11 +161,15 @@
     return found
 
 
-def prepare_kernel(
-    adj, own, first_in, second_in, first_forward, second_turned, places, low, side,
-    first, second, sems,
-):
+def early_weight_kernel(after, first_in, second_in, first_forward, second_turned, first, second, sems):
     copies = start_weights(first_in, second_in, first, second, sems)
+    copies[0].wait()
+    forward_weight(first, first_forward)
+    copies[1].wait()
+    turned_weight(second, second_turned)
+
+
+def site_kernel(adj, own, places, low, side):
     relative = relative_owners(adj, own)
     from_left = among(relative, [-1 - GRID, -1, -1 + GRID])
     side[...] = jnp.full(side.shape, jnp.where(from_left, 1.0, 0.0), F32).astype(BF16)
@@ -190,10 +194,6 @@
             there = (768 if sy < 0 else 800) + nx * 16 + ny * 8 + z
         place = jnp.where(which == sx + GRID * sy, there, place)
     places[...] = jnp.broadcast_to(place, places.shape)
-    copies[0].wait()
-    forward_weight(first, first_forward)
-    copies[1].wait()
-    turned_weight(second, second_turned)
 
 
 def either(flag, one, other):
@@ -275,16 +275,16 @@
         most = jnp.maximum(jnp.max(jnp.abs(total), axis=1), 1e-30)
         exponent = jnp.ceil(jnp.log2(most))
         values = jnp.round(total * jnp.exp2(14.0 - exponent)[:, None, :])
-        coded[number, 0:4] = values.astype(jnp.int32).astype(jnp.int16)
-        rows = jnp.concatenate([exponent, jnp.zeros((12, 128), F32)], axis=0)
-        coded[number, 4] = rows.astype(jnp.int32).astype(jnp.int16)
+        coded[number, 0:64] = values.astype(jnp.int32).astype(jnp.int16).reshape(64, 128)
+        rows = jnp.concatenate([exponent, jnp.zeros((4, 128), F32)], axis=0)
+        coded[number, 64:72] = rows.astype(jnp.int32).astype(jnp.int16)
 
 
 def decode_kernel(coded, copies):
     total = jnp.zeros((4, 16, 128), F32)
     for number in range(32):
-        exponent = coded[number, 4].astype(jnp.int32).astype(F32)[0:4]
-        values = coded[number, 0:4].astype(jnp.int32).astype(F32)
+        exponent = coded[number, 64:72].astype(jnp.int32).astype(F32)[0:4]
+        values = coded[number, 0:64].astype(jnp.int32).astype(F32).reshape(4, 16, 128)
         total = total + values * jnp.exp2(exponent - 14.0)[:, None, :]
     for number in range(copies.shape[0]):
         copies[number] = total.astype(BF16)
@@ -339,7 +339,7 @@
 ANY = pl.BlockSpec(memory_space=pl.ANY)
 DMA = pltpu.SemaphoreType.DMA
 MIB = 1024 * 1024
-PACK, PREPARE, LATE = int(53.58 * MIB), int(52.4 * MIB), int(52.5 * MIB)
+PACK, EARLY, LATE = int(53.58 * MIB), int(52.6 * MIB), int(52.5 * MIB)
 
 
 def call(kernel, outs, specs, scratch=(), place=VMEM, limit=40 * MIB, **options):
@@ -379,15 +379,12 @@
         down, up, *quarters = call(
             pack_kernel, [rim] * 6, [HBM] * 3, [vmem((ROWS, 512), BF16)] + inputs, limit=PACK
         )(feats, cotangent, occupancy)
-    with jax.named_scope("prepare"):
-        one_f, two_b, places, low, side = call(
-            prepare_kernel,
-            [turned] * 2
-            + [((8, LANES), jnp.int32), ((16, 128), BF16), ((16, 256), BF16)],
-            [SMEM] * 2 + [HBM] * 2,
-            weights,
-            limit=PREPARE,
-        )(adjacency, own, w_first, w_second)
+    with jax.named_scope("sites"):
+        places, low, side = call(
+            site_kernel,
+            [((8, LANES), jnp.int32), ((16, 128), BF16), ((16, 256), BF16)],
+            [SMEM] * 2,
+        )(adjacency, own)
     with jax.named_scope("rims_y"):
         ym, yp = from_owner(down, 0, -1), from_owner(up, 0, 1)
     with jax.named_scope("slabs"):
@@ -396,6 +393,10 @@
         )
     with jax.named_scope("rims_x"):
         xm, xp = from_owner(left, -1, 0), from_owner(right, 1, 0)
+    with jax.named_scope("early_weights"):
+        one_f, two_b = call(
+            early_weight_kernel, [turned] * 2, [VMEM] + [HBM] * 2, weights, limit=EARLY
+        )(left, w_first, w_second)
     with jax.named_scope("place"):
         base, hot_x = call(
             place_kernel,
@@ -418,7 +419,7 @@
     with jax.named_scope("keep"):
         (keep,) = call(keep_kernel, [half], [SMEM] + [VMEM] * 2, [grads])(own, inner, columns)
     with jax.named_scope("pair"):
-        (coded,) = call(pair_kernel, [((32, 5, 16, 128), jnp.int16)], [VMEM] * 2)(
+        (coded,) = call(pair_kernel, [((32, 72, 128), jnp.int16)], [VMEM] * 2)(
             keep, swap_halves(send)
         )
     near, far = ("zl", "y", "x"), "zh"

time: 108 us -> 108 us (level)
  waiting for transfers between devices: 14.4 us -> 13 us
    ppermute x4, waiting for transfers between devices: 5.93 us -> 4.59 us  [from_owner(): return lax.ppermute(value, ('zh', 'zl', 'y'), pairs)]
    pallas_call x2 -> x3, Pallas kernels: 2.84 us -> 3.28 us  [the longest x1 1.9 us: body(): call(early_weight_kernel, [turned] * 2, [VMEM] + [HBM] * 2, weights, limi...]
  transfers between devices with their start and end apart: 7 -> 7, of which waited for: 4 -> 3; matrix products, arithmetic and copies ran while one was open for 0% -> 0% of each run, Pallas kernels for 12% -> 13%
where the time goes in v8:
time: 108 us; the launch traced here: 107 us
  starting transfers between devices  34.7 us (32%)
  blocking collectives  34.1 us (32%)
  Pallas kernels  23.3 us (22%)
  waiting for transfers between devices  13 us (12%)
  local copies, waits for them, and re-layouts  1.33 us (1%)
    all_to_all x1, blocking collectives, body(): parts = lax.all_to_all(coded, near, 0, 0)  20.4 us
    all_to_all x1, blocking collectives, body(): mine = lax.all_to_all(copies, near, 0, 0).reshape(128, 16, 128)  13.7 us
    ppermute x4, starting transfers between devices, from_owner(): return lax.ppermute(value, ('zh', 'zl', 'y'), pairs)  12.3 us
    all_to_all x1, starting transfers between devices, body(): parts = lax.all_to_all(copies, far, 0, 0)  11.8 us
    ppermute x2, starting transfers between devices, swap_halves(): return lax.ppermute(value, 'core', [(0, 1), (1, 0)])  10.6 us
    all_to_all x1, waiting for transfers between devices, body(): parts = lax.all_to_all(copies, far, 0, 0)  8.09 us
    pallas_call x1, Pallas kernels, body(): call(main_kernel, [half, ((ROWS, LANES), BF16), outer, outer, ((2, C, OUT...  5.57 us
    ppermute x4, waiting for transfers between devices, from_owner(): return lax.ppermute(value, ('zh', 'zl', 'y'), pairs)  4.59 us
  transfers between devices with their start and end apart: 7, of which 3 were waited for; matrix products, arithmetic and copies ran while one was open for 0% of the time, Pallas kernels for 13%

profile of v8, /device:TPU:1, one launch (start us, length us, event | category | flops | bytes accessed | tf_op | source)
XLA Modules:
  0.0 107.5 jit_solution(5111737771235079771)
XLA Ops:
  0.6 0.7 copy-done
  1.3 1.2 %pack.1 = (bf16[208,128]{1,0:T(8,128)(2,1)S(1)}, bf16[208,128]{1,0:T(8,128)(2,1)S(1)}, bf16[208,128]{1,0:T(8,128)(2,1)S(1)}, bf16[208,128]{1,0:T(8,128)(2,1)S(1)...) custom-call(bf16[1,96,512]{2,1,0:T(8,128)(2,1)} %feats_in.1, bf16[1,96,512]{2,1,0:T(8,128)(2,1)} %cot_in.1, ...), custom_call_target="tpu_custom_call" | custom-call | tf_op jit(solution)/shard_map/pack/pallas_call | solution.py:379
  2.5 5.7 %collective-permute-start = (bf16[208,128]{1,0:T(8,128)(2,1)S(1)}, bf16[208,128]{1,0:T(8,128)(2,1)S(1)}, u32[]{:S(2)}, u32[]{:S(2)}) collective-permute-start(bf16[208,128]{1,0:T(8,128)(2,1)S(1)} %get-tuple-element.37), channel_id=1, source_target_pairs={{0,64},{8,72},{16,80},{24,88},{32,96},{40,104},{48,112},{56,120},{... | collective-permute-start | bytes 159752 | tf_op jit(solution)/shard_map/rims_y/ppermute | solution.py:363
  8.2 1.3 %collective-permute-start.1 = (bf16[208,128]{1,0:T(8,128)(2,1)S(1)}, bf16[208,128]{1,0:T(8,128)(2,1)S(1)}, u32[]{:S(2)}, u32[]{:S(2)}) collective-permute-start(bf16[208,128]{1,0:T(8,128)(2,1)S(1)} %get-tuple-element.38), channel_id=1, source_target_pairs={{64,0},{72,8},{80,16},{88,24},{96,32},{104,40},{112,48},{120,56},{... | collective-permute-start | bytes 159752 | tf_op jit(solution)/shard_map/rims_y/ppermute | solution.py:363
  9.5 0.1 pad_add_fusion.own
  9.6 0.7 copy-done.1
  10.3 1.0 sites.1
  11.3 0.0 collective-permute-done.ym
  11.3 4.6 %collective-permute-done.1.yp = bf16[208,128]{1,0:T(8,128)(2,1)S(1)} collective-permute-done((bf16[208,128]{1,0:T(8,128)(2,1)S(1)}, bf16[208,128]{1,0:T(8,128)(2,1)S(1)}, u32[]{:S(2)}, u32[]{:S(2)}) %collective-permute-start.1) | collective-permute-done | bytes 53280 | tf_op jit(solution)/shard_map/rims_y/ppermute | solution.py:363
  15.9 0.1 slabs.1
  16.0 1.3 %collective-permute-start.3 = (bf16[208,256]{1,0:T(8,128)(2,1)S(1)}, bf16[208,256]{1,0:T(8,128)(2,1)S(1)}, u32[]{:S(2)}, u32[]{:S(2)}) collective-permute-start(bf16[208,256]{1,0:T(8,128)(2,1)S(1)} %get-tuple-element.40), channel_id=1, source_target_pairs={{8,0},{16,8},{24,16},{32,24},{40,32},{48,40},{56,48},{72,64},{80,7... | collective-permute-start | bytes 319496 | tf_op jit(solution)/shard_map/rims_x/ppermute | solution.py:363
  17.3 4.0 %collective-permute-start.2 = (bf16[208,256]{1,0:T(8,128)(2,1)S(1)}, bf16[208,256]{1,0:T(8,128)(2,1)S(1)}, u32[]{:S(2)}, u32[]{:S(2)}) collective-permute-start(bf16[208,256]{1,0:T(8,128)(2,1)S(1)} %get-tuple-element.39.after), channel_id=1, source_target_pairs={{0,8},{8,16},{16,24},{24,32},{32,40},{40,48},{48,56},{64,72},{72,8... | collective-permute-start | bytes 319496 | tf_op jit(solution)/shard_map/rims_x/ppermute | solution.py:363
  21.3 1.9 %early_weights.1 = (bf16[288,864]{1,0:T(8,128)(2,1)S(1)}, bf16[288,864]{1,0:T(8,128)(2,1)S(1)}) custom-call(bf16[208,256]{1,0:T(8,128)(2,1)S(1)} %get-tuple-element.39.after, bf16[96,2592]{1,0:T(8,128)(2,1)} %first_in.3, bf16[96,2592]{1,0:T(8,128)(2,1)} %second_in.3), custom_call_target="tpu_custom_call" | custom-call | tf_op jit(solution)/shard_map/early_weights/pallas_call | solution.py:397
  23.2 1.3 %place.1 = (bf16[208,1920]{1,0:T(8,128)(2,1)S(1)}, bf16[256,1920]{1,0:T(8,128)(2,1)S(1)}) custom-call(bf16[208,128]{1,0:T(8,128)(2,1)S(1)} %get-tuple-element.35.first.q0, bf16[208,128]{1,0:T(8,128)(2,1)S(1)} %get-tuple-element.41.q1, bf16[208,128]{1,0:T(8,128)(2,1)S(1)} %get-tuple-element.42.q2, bf16[208,128]{1,0:T(8,128)(2,1)S(1)} %get-tuple-element.36.last.q3, ...), custom_call_target="tpu_custom_call" | custom-call | tf_op jit(solution)/shard_map/place/pallas_call | solution.py:401
  24.5 0.0 collective-permute-done.3.xp
  24.5 5.6 %middle.1 = (f32[128,16,128]{2,1,0:T(8,128)S(1)}, bf16[208,1920]{1,0:T(8,128)(2,1)S(1)}, bf16[96,1536]{1,0:T(8,128)(2,1)S(1)}, bf16[96,1536]{1,0:T(8,128)(2,1)S(...) custom-call(s32[2]{0:T(128)S(1)} %pad_add_fusion.own, ...), custom_call_target="tpu_custom_call" | custom-call | tf_op jit(solution)/shard_map/middle/pallas_call | solution.py:410
  30.1 4.9 %collective-permute-start.4 = (f32[128,16,128]{2,1,0:T(8,128)S(1)}, f32[128,16,128]{2,1,0:T(8,128)S(1)}, u32[]{:S(2)}, u32[]{:S(2)}) collective-permute-start(f32[128,16,128]{2,1,0:T(8,128)S(1)} %get-tuple-element.51), channel_id=1, source_target_pairs={{0,1},{1,0},{2,3},{3,2},{4,5},{5,4},{6,7},{7,6},{8,9},{9,8},{10,11... | collective-permute-start | bytes 3145736 | tf_op jit(solution)/shard_map/pair/ppermute | solution.py:367
  35.0 2.0 %keep.1 = f32[128,16,128]{2,1,0:T(8,128)S(1)} custom-call(s32[2]{0:T(128)S(1)} %pad_add_fusion.own, bf16[2,96,1536]{2,1,0:T(8,128)(2,1)S(1)} %get-tuple-element.49.inner, bf16[2,864,1536]{2,1,0:T(8,128)(2,1)S(1)} %get-tuple-element.50.columns), custom_call_target="tpu_custom_call" | custom-call | tf_op jit(solution)/shard_map/keep/pallas_call | solution.py:420
  37.0 0.3 collective-permute-done.4.other
  37.3 0.4 pair.1
  37.7 20.4 %all_to_all.15.coded = s16[32,72,128]{2,1,0:T(8,128)(2,1)S(1)} all-to-all(s16[32,72,128]{2,1,0:T(8,128)(2,1)S(1)} %pair.1), channel_id=1, replica_groups=mesh['zh'=8,'zl'=2,'y'=4,'x'=4,'core'=2] {'zl','y','x'}, dimensions={0} | all-to-all | bytes 1179648 | tf_op jit(solution)/shard_map/sum/all_to_all | solution.py:427
  58.1 0.9 sum.1.after
  58.9 11.8 %all-to-all-start.1 = ((bf16[8,4,16,128]{3,2,1,0:T(8,128)(2,1)}), bf16[8,4,16,128]{3,2,1,0:T(8,128)(2,1)S(1)}, u32[]{:S(2)}, u32[]{:S(2)}) async-start(bf16[8,4,16,128]{3,2,1,0:T(8,128)(2,1)} %sum.1.after), calls=%async_computation.1 | async-start | bytes 262144 | tf_op jit(solution)/shard_map/sum/all_to_all | solution.py:429
  70.7 2.0 %late_weights.1 = (bf16[288,864]{1,0:T(8,128)(2,1)S(1)}, bf16[288,864]{1,0:T(8,128)(2,1)S(1)}) custom-call(bf16[8,4,16,128]{3,2,1,0:T(8,128)(2,1)} %sum.1.after, bf16[96,2592]{1,0:T(8,128)(2,1)} %first_in.3, bf16[96,2592]{1,0:T(8,128)(2,1)} %second_in.3), custom_call_target="tpu_custom_call" | custom-call | tf_op jit(solution)/shard_map/late_weights/pallas_call | solution.py:431
  72.7 3.8 %outputs.1 = (bf16[1,96,512]{2,1,0:T(8,128)(2,1)}, bf16[1,96,512]{2,1,0:T(8,128)(2,1)}, f32[8,128]{1,0:T(8,128)S(1)}) custom-call(bf16[8,4,16,128]{3,2,1,0:T(8,128)(2,1)} %sum.1.after, bf16[208,1920]{1,0:T(8,128)(2,1)S(1)} %get-tuple-element.52.padded, bf16[96,1536]{1,0:T(8,128)(2,1)S(1)} %get-tuple-element.53.hidden, ...), custom_call_target="tpu_custom_call" | custom-call | tf_op jit(solution)/shard_map/outputs/pallas_call | solution.py:435
  76.5 8.1 %all-to-all-done.1.refs_0_ = bf16[8,4,16,128]{3,2,1,0:T(8,128)(2,1)S(1)} async-done(((bf16[8,4,16,128]{3,2,1,0:T(8,128)(2,1)}), bf16[8,4,16,128]{3,2,1,0:T(8,128)(2,1)S(1)}, u32[]{:S(2)}, u32[]{:S(2)}) %all-to-all-start.1) | async-done | bytes 131104 | tf_op jit(solution)/shard_map/sum/all_to_all | solution.py:429
  84.6 0.1 shares.1
  84.7 13.7 %all_to_all.16 = bf16[32,4,16,128]{3,2,1,0:T(8,128)(2,1)S(1)} all-to-all(bf16[32,4,16,128]{3,2,1,0:T(8,128)(2,1)S(1)} %shares.1), channel_id=1, replica_groups=mesh['zh'=8,'zl'=2,'y'=4,'x'=4,'core'=2] {'zl','y','x'}, dimensions={0} | all-to-all | bytes 1048576 | tf_op jit(solution)/shard_map/shares/all_to_all | solution.py:445
  98.4 5.7 %collective-permute-start.5 = (bf16[128,16,128]{2,1,0:T(8,128)(2,1)S(1)}, bf16[128,16,128]{2,1,0:T(8,128)(2,1)S(1)}, u32[]{:S(2)}, u32[]{:S(2)}) collective-permute-start(bf16[128,16,128]{2,1,0:T(8,128)(2,1)S(1)} %bitcast.3), channel_id=1, source_target_pairs={{0,1},{1,0},{2,3},{3,2},{4,5},{5,4},{6,7},{7,6},{8,9},{9,8},{10,11... | collective-permute-start | bytes 1572872 | tf_op jit(solution)/shard_map/shares/ppermute | solution.py:367
  104.1 1.6 %mine.1 = (f32[96,2592]{1,0:T(8,128)}, f32[96,2592]{1,0:T(8,128)}) custom-call(s32[2]{0:T(128)S(1)} %pad_add_fusion.own, bf16[128,16,128]{2,1,0:T(8,128)(2,1)S(1)} %bitcast.4), custom_call_target="tpu_custom_call" | custom-call | tf_op jit(solution)/shard_map/mine/pallas_call | solution.py:449
  105.7 0.0 collective-permute-done.5.half
  105.7 1.6 %other.1 = (f32[96,2592]{1,0:T(8,128)}, f32[96,2592]{1,0:T(8,128)}) custom-call(s32[2]{0:T(128)S(1)} %pad_add_fusion.own, bf16[128,16,128]{2,1,0:T(8,128)(2,1)S(1)} %collective-permute-done.5.half, f32[96,2592]{1,0:T(8,128)} %get-tuple-element.60.first_in, f32[96,2592]{1,0:T(8,128)} %get-tuple-element.61.second_in), custom_call_target="tpu_custom_call", output_to_operand_aliasing={{0}: (2, {}), {1}: (3, {})} | custom-call | tf_op jit(solution)/shard_map/other/pallas_call | solution.py:451
  (3 shorter events, 0.0 us)
Async XLA Ops:
  0.6 0.7 copy-start
  2.5 8.8 %collective-permute-start = (bf16[208,128]{1,0:T(8,128)(2,1)S(1)}, bf16[208,128]{1,0:T(8,128)(2,1)S(1)}, u32[]{:S(2)}, u32[]{:S(2)}) collective-permute-start(bf16[208,128]{1,0:T(8,128)(2,1)S(1)} %get-tuple-element.37), channel_id=1, source_target_pairs={{0,64},{8,72},{16,80},{24,88},{32,96},{40,104},{48,112},{56,120},{... | collective-permute-start | bytes 159752 | tf_op jit(solution)/shard_map/rims_y/ppermute | solution.py:363
  8.2 7.6 %collective-permute-start.1 = (bf16[208,128]{1,0:T(8,128)(2,1)S(1)}, bf16[208,128]{1,0:T(8,128)(2,1)S(1)}, u32[]{:S(2)}, u32[]{:S(2)}) collective-permute-start(bf16[208,128]{1,0:T(8,128)(2,1)S(1)} %get-tuple-element.38), channel_id=1, source_target_pairs={{64,0},{72,8},{80,16},{88,24},{96,32},{104,40},{112,48},{120,56},{... | collective-permute-start | bytes 159752 | tf_op jit(solution)/shard_map/rims_y/ppermute | solution.py:363
  9.6 0.7 copy-start.1
  16.0 8.5 %collective-permute-start.3 = (bf16[208,256]{1,0:T(8,128)(2,1)S(1)}, bf16[208,256]{1,0:T(8,128)(2,1)S(1)}, u32[]{:S(2)}, u32[]{:S(2)}) collective-permute-start(bf16[208,256]{1,0:T(8,128)(2,1)S(1)} %get-tuple-element.40), channel_id=1, source_target_pairs={{8,0},{16,8},{24,16},{32,24},{40,32},{48,40},{56,48},{72,64},{80,7... | collective-permute-start | bytes 319496 | tf_op jit(solution)/shard_map/rims_x/ppermute | solution.py:363
  17.3 7.3 %collective-permute-start.2 = (bf16[208,256]{1,0:T(8,128)(2,1)S(1)}, bf16[208,256]{1,0:T(8,128)(2,1)S(1)}, u32[]{:S(2)}, u32[]{:S(2)}) collective-permute-start(bf16[208,256]{1,0:T(8,128)(2,1)S(1)} %get-tuple-element.39.after), channel_id=1, source_target_pairs={{0,8},{8,16},{16,24},{24,32},{32,40},{40,48},{48,56},{64,72},{72,8... | collective-permute-start | bytes 319496 | tf_op jit(solution)/shard_map/rims_x/ppermute | solution.py:363
  30.1 7.1 %collective-permute-start.4 = (f32[128,16,128]{2,1,0:T(8,128)S(1)}, f32[128,16,128]{2,1,0:T(8,128)S(1)}, u32[]{:S(2)}, u32[]{:S(2)}) collective-permute-start(f32[128,16,128]{2,1,0:T(8,128)S(1)} %get-tuple-element.51), channel_id=1, source_target_pairs={{0,1},{1,0},{2,3},{3,2},{4,5},{5,4},{6,7},{7,6},{8,9},{9,8},{10,11... | collective-permute-start | bytes 3145736 | tf_op jit(solution)/shard_map/pair/ppermute | solution.py:367
  58.9 25.7 %all-to-all-start.1 = ((bf16[8,4,16,128]{3,2,1,0:T(8,128)(2,1)}), bf16[8,4,16,128]{3,2,1,0:T(8,128)(2,1)S(1)}, u32[]{:S(2)}, u32[]{:S(2)}) async-start(bf16[8,4,16,128]{3,2,1,0:T(8,128)(2,1)} %sum.1.after), calls=%async_computation.1 | async-start | bytes 262144 | tf_op jit(solution)/shard_map/sum/all_to_all | solution.py:429
  98.4 7.3 %collective-permute-start.5 = (bf16[128,16,128]{2,1,0:T(8,128)(2,1)S(1)}, bf16[128,16,128]{2,1,0:T(8,128)(2,1)S(1)}, u32[]{:S(2)}, u32[]{:S(2)}) collective-permute-start(bf16[128,16,128]{2,1,0:T(8,128)(2,1)S(1)} %bitcast.3), channel_id=1, source_target_pairs={{0,1},{1,0},{2,3},{3,2},{4,5},{5,4},{6,7},{7,6},{8,9},{9,8},{10,11... | collective-permute-start | bytes 1572872 | tf_op jit(solution)/shard_map/shares/ppermute | solution.py:367

commit v9 on v8

--- a/solution.py
+++ b/solution.py
@@ -15,6 +15,7 @@
 LANES = 1920
 OUTER = 1536
 INNER = 1152
+SPAN = 384
 BASE = PAD * PAD + PAD
 TILES_L = 21
 DIRECTIONS = [(-1, -1), (0, -1), (1, -1), (-1, 0), (1, 0), (-1, 1), (0, 1), (1, 1)]
@@ -200,7 +201,10 @@
     return one * flag + other * (1.0 - flag.astype(F32)).astype(BF16)
 
 
-def place_kernel(q0, q1, q2, q3, ym, yp, places, low, base, hot_x, sources):
+def place_kernel(
+    q0, q1, q2, q3, ym, yp, places, low, w_one, w_two,
+    base, hot_x, col_m, pre, back, sources, col_g,
+):
     for number, quarter in enumerate((q0, q1, q2, q3)):
         sources[:, number * 128 : (number + 1) * 128] = quarter[...]
     sources[:, 512:640] = either(low[0:1, :], ym[...], yp[...])
@@ -212,26 +216,36 @@
         base[:, cut] = jnp.dot(
             sources[...], hot[0:640], preferred_element_type=F32
         ).astype(BF16)
+    shifted_columns(base[0:C, :], col_m, OUTER)
+    pre[...] = three_taps(w_one, col_m, OUTER)
+    shifted_columns(base[C : 2 * C, :], col_g, OUTER)
+    back[...] = three_taps(w_two, col_g, OUTER)
 
 
 def main_kernel(
-    own, xm, xp, base, hot_x, side, w_one, w_two,
+    own, xm, xp, base, hot_x, side, w_one, w_two, col_base, pre_base, back_base,
     send, padded, hidden, grad_one, inner, columns,
-    col_g, grads,
+    near, col_w, wide_pre, wide_back, grads,
 ):
+    from_left = jnp.max(side[...].astype(F32)) > 0.5
+    start = pl.multiple_of(jnp.where(from_left, 0, OUTER - SPAN), 128)
+    lanes, window = pl.ds(start, 2 * SPAN), pl.ds(start, SPAN)
     slab = either(side[0:1, :], xm[...], xp[...])
-    width = 384
-    for part in range(LANES // width):
-        cut = slice(part * width, (part + 1) * width)
-        near = jnp.dot(slab, hot_x[:, cut], preferred_element_type=F32)
-        padded[:, cut] = (base[:, cut].astype(F32) + near).astype(BF16)
-    shifted_columns(padded[0:C, :], columns.at[0], OUTER)
-    shifted_columns(padded[C : 2 * C, :], col_g, OUTER)
+    near[...] = jnp.dot(slab, hot_x[:, lanes], preferred_element_type=F32).astype(BF16)
+    padded[...] = base[...]
+    padded[:, lanes] = base[:, lanes] + near[...]
+    columns[0] = col_base[...]
+    wide_pre[...] = pre_base[...]
+    wide_back[...] = back_base[...]
+    shifted_columns(near[0:C, :], col_w, SPAN)
+    columns[0, :, window] = col_base[:, window] + col_w[...]
+    wide_pre[:, window] = pre_base[:, window] + three_taps(w_one, col_w, SPAN)
+    shifted_columns(near[C : 2 * C, :], col_w, SPAN)
+    wide_back[:, window] = back_base[:, window] + three_taps(w_two, col_w, SPAN)
     mask = padded[2 * C : 2 * C + 1, BASE + 1 : BASE + 1 + OUTER].astype(F32)
-    pre = three_taps(w_one, columns.at[0], OUTER)
+    pre, back = wide_pre[...], wide_back[...]
     sig = jax.nn.sigmoid(pre)
     hidden[...] = (pre * sig * mask).astype(BF16)
-    back = three_taps(w_two, col_g, OUTER)
     grad = (back * mask * sig * (1.0 + pre * (1.0 - sig))).astype(BF16)
     grad_one[...] = grad
     shifted_columns(hidden[...], columns.at[1], INNER)
@@ -275,16 +289,16 @@
         most = jnp.maximum(jnp.max(jnp.abs(total), axis=1), 1e-30)
         exponent = jnp.ceil(jnp.log2(most))
         values = jnp.round(total * jnp.exp2(14.0 - exponent)[:, None, :])
-        coded[number, 0:64] = values.astype(jnp.int32).astype(jnp.int16).reshape(64, 128)
-        rows = jnp.concatenate([exponent, jnp.zeros((4, 128), F32)], axis=0)
-        coded[number, 64:72] = rows.astype(jnp.int32).astype(jnp.int16)
+        coded[number, 0:4] = values.astype(jnp.int32).astype(jnp.int16)
+        rows = jnp.concatenate([exponent, jnp.zeros((12, 128), F32)], axis=0)
+        coded[number, 4] = rows.astype(jnp.int32).astype(jnp.int16)
 
 
 def decode_kernel(coded, copies):
     total = jnp.zeros((4, 16, 128), F32)
     for number in range(32):
-        exponent = coded[number, 64:72].astype(jnp.int32).astype(F32)[0:4]
-        values = coded[number, 0:64].astype(jnp.int32).astype(F32).reshape(4, 16, 128)
+        exponent = coded[number, 4].astype(jnp.int32).astype(F32)[0:4]
+        values = coded[number, 0:4].astype(jnp.int32).astype(F32)
         total = total + values * jnp.exp2(exponent - 14.0)[:, None, :]
     for number in range(copies.shape[0]):
         copies[number] = total.astype(BF16)
@@ -398,14 +412,14 @@
             early_weight_kernel, [turned] * 2, [VMEM] + [HBM] * 2, weights, limit=EARLY
         )(left, w_first, w_second)
     with jax.named_scope("place"):
-        base, hot_x = call(
+        outer, field = ((C, OUTER), BF16), ((C, OUTER), F32)
+        base, hot_x, col_base, pre_base, back_base = call(
             place_kernel,
-            [((ROWS, LANES), BF16), ((256, LANES), BF16)],
-            [VMEM] * 8,
-            [vmem((ROWS, 640), BF16)],
-        )(*quarters, ym, yp, places, low)
+            [((ROWS, LANES), BF16), ((256, LANES), BF16), ((9 * C, OUTER), BF16), field, field],
+            [VMEM] * 10,
+            [vmem((ROWS, 640), BF16), vmem((9 * C, OUTER), BF16)],
+        )(*quarters, ym, yp, places, low, one_f, two_b)
     half, grads = ((128, 16, 128), F32), vmem((C, TILES_L * 128), F32)
-    outer = ((C, OUTER), BF16)
     with jax.named_scope("middle"):
         send, padded, hidden, grad_one, inner, columns = call(
             main_kernel,
@@ -413,13 +427,20 @@
                 half, ((ROWS, LANES), BF16), outer, outer,
                 ((2, C, OUTER), BF16), ((2, 9 * C, OUTER), BF16),
             ],
-            [SMEM] + [VMEM] * 7,
-            [vmem((9 * C, OUTER), BF16), grads],
-        )(own, xm, xp, base, hot_x, side, one_f, two_b)
+            [SMEM] + [VMEM] * 10,
+            [
+                vmem((ROWS, 2 * SPAN), BF16), vmem((9 * C, SPAN), BF16),
+                vmem((C, OUTER), F32), vmem((C, OUTER), F32), grads,
+            ],
+            limit=24 * MIB,
+        )(
+            own, xm, xp, base, hot_x, side, one_f, two_b,
+            col_base, pre_base, back_base,
+        )
     with jax.named_scope("keep"):
         (keep,) = call(keep_kernel, [half], [SMEM] + [VMEM] * 2, [grads])(own, inner, columns)
     with jax.named_scope("pair"):
-        (coded,) = call(pair_kernel, [((32, 72, 128), jnp.int16)], [VMEM] * 2)(
+        (coded,) = call(pair_kernel, [((32, 5, 16, 128), jnp.int16)], [VMEM] * 2)(
             keep, swap_halves(send)
         )
     near, far = ("zl", "y", "x"), "zh"

time: 108 us -> 109 us (level)
  Pallas kernels: 23.3 us -> 24.6 us
    pallas_call x2, Pallas kernels: 1.73 us -> 4.04 us  [the longest x1 3.64 us: body(): call(place_kernel, [((ROWS, LANES), BF16), ((256, LANES), BF16), ((9 * C,...]
  transfers between devices with their start and end apart: 7 -> 7, of which waited for: 3 -> 3; matrix products, arithmetic and copies ran while one was open for 0% -> 0% of each run, Pallas kernels for 13% -> 15%
where the time goes in v9:
time: 109 us
  starting transfers between devices  34.6 us (32%)
  blocking collectives  33.9 us (31%)
  Pallas kernels  24.6 us (23%)
  waiting for transfers between devices  13 us (12%)
  local copies, waits for them, and re-layouts  1.33 us (1%)
    all_to_all x1, blocking collectives, body(): parts = lax.all_to_all(coded, near, 0, 0)  19.9 us
    all_to_all x1, blocking collectives, body(): mine = lax.all_to_all(copies, near, 0, 0).reshape(128, 16, 128)  14.1 us
    ppermute x4, starting transfers between devices, from_owner(): return lax.ppermute(value, ('zh', 'zl', 'y'), pairs)  12.3 us
    all_to_all x1, starting transfers between devices, body(): parts = lax.all_to_all(copies, far, 0, 0)  11.8 us
    ppermute x2, starting transfers between devices, swap_halves(): return lax.ppermute(value, 'core', [(0, 1), (1, 0)])  10.6 us
    all_to_all x1, waiting for transfers between devices, body(): parts = lax.all_to_all(copies, far, 0, 0)  8.13 us
    ppermute x4, waiting for transfers between devices, from_owner(): return lax.ppermute(value, ('zh', 'zl', 'y'), pairs)  4.59 us
    pallas_call x1, Pallas kernels, body(): call(main_kernel, [half, ((ROWS, LANES), BF16), outer, outer, ((2, C, OUT...  4.5 us
  transfers between devices with their start and end apart: 7, of which 3 were waited for; matrix products, arithmetic and copies ran while one was open for 0% of the time, Pallas kernels for 15%

profile of v9, /device:TPU:1, one launch (start us, length us, event | category | flops | bytes accessed | tf_op | source)
XLA Modules:
  0.0 108.6 jit_solution(1510870656310965380)
XLA Ops:
  0.6 0.7 copy-done
  1.3 1.2 %pack.1 = (bf16[208,128]{1,0:T(8,128)(2,1)S(1)}, bf16[208,128]{1,0:T(8,128)(2,1)S(1)}, bf16[208,128]{1,0:T(8,128)(2,1)S(1)}, bf16[208,128]{1,0:T(8,128)(2,1)S(1)...) custom-call(bf16[1,96,512]{2,1,0:T(8,128)(2,1)} %feats_in.1, bf16[1,96,512]{2,1,0:T(8,128)(2,1)} %cot_in.1, ...), custom_call_target="tpu_custom_call" | custom-call | tf_op jit(solution)/shard_map/pack/pallas_call | solution.py:393
  2.5 5.7 %collective-permute-start = (bf16[208,128]{1,0:T(8,128)(2,1)S(1)}, bf16[208,128]{1,0:T(8,128)(2,1)S(1)}, u32[]{:S(2)}, u32[]{:S(2)}) collective-permute-start(bf16[208,128]{1,0:T(8,128)(2,1)S(1)} %get-tuple-element.40), channel_id=1, source_target_pairs={{0,64},{8,72},{16,80},{24,88},{32,96},{40,104},{48,112},{56,120},{... | collective-permute-start | bytes 159752 | tf_op jit(solution)/shard_map/rims_y/ppermute | solution.py:377
  8.2 1.3 %collective-permute-start.1 = (bf16[208,128]{1,0:T(8,128)(2,1)S(1)}, bf16[208,128]{1,0:T(8,128)(2,1)S(1)}, u32[]{:S(2)}, u32[]{:S(2)}) collective-permute-start(bf16[208,128]{1,0:T(8,128)(2,1)S(1)} %get-tuple-element.41), channel_id=1, source_target_pairs={{64,0},{72,8},{80,16},{88,24},{96,32},{104,40},{112,48},{120,56},{... | collective-permute-start | bytes 159752 | tf_op jit(solution)/shard_map/rims_y/ppermute | solution.py:377
  9.5 0.1 pad_add_fusion.own
  9.6 0.7 copy-done.1
  10.3 1.0 sites.1
  11.3 0.0 collective-permute-done.ym
  11.3 4.6 %collective-permute-done.1.yp = bf16[208,128]{1,0:T(8,128)(2,1)S(1)} collective-permute-done((bf16[208,128]{1,0:T(8,128)(2,1)S(1)}, bf16[208,128]{1,0:T(8,128)(2,1)S(1)}, u32[]{:S(2)}, u32[]{:S(2)}) %collective-permute-start.1) | collective-permute-done | bytes 53280 | tf_op jit(solution)/shard_map/rims_y/ppermute | solution.py:377
  15.9 0.1 slabs.1
  16.0 1.3 %collective-permute-start.3 = (bf16[208,256]{1,0:T(8,128)(2,1)S(1)}, bf16[208,256]{1,0:T(8,128)(2,1)S(1)}, u32[]{:S(2)}, u32[]{:S(2)}) collective-permute-start(bf16[208,256]{1,0:T(8,128)(2,1)S(1)} %get-tuple-element.43), channel_id=1, source_target_pairs={{8,0},{16,8},{24,16},{32,24},{40,32},{48,40},{56,48},{72,64},{80,7... | collective-permute-start | bytes 319496 | tf_op jit(solution)/shard_map/rims_x/ppermute | solution.py:377
  17.3 4.0 %collective-permute-start.2 = (bf16[208,256]{1,0:T(8,128)(2,1)S(1)}, bf16[208,256]{1,0:T(8,128)(2,1)S(1)}, u32[]{:S(2)}, u32[]{:S(2)}) collective-permute-start(bf16[208,256]{1,0:T(8,128)(2,1)S(1)} %get-tuple-element.42.after), channel_id=1, source_target_pairs={{0,8},{8,16},{16,24},{24,32},{32,40},{40,48},{48,56},{64,72},{72,8... | collective-permute-start | bytes 319496 | tf_op jit(solution)/shard_map/rims_x/ppermute | solution.py:377
  21.3 1.9 %early_weights.1 = (bf16[288,864]{1,0:T(8,128)(2,1)S(1)}, bf16[288,864]{1,0:T(8,128)(2,1)S(1)}) custom-call(bf16[208,256]{1,0:T(8,128)(2,1)S(1)} %get-tuple-element.42.after, bf16[96,2592]{1,0:T(8,128)(2,1)} %first_in.3, bf16[96,2592]{1,0:T(8,128)(2,1)} %second_in.3), custom_call_target="tpu_custom_call" | custom-call | tf_op jit(solution)/shard_map/early_weights/pallas_call | solution.py:411
  23.2 3.6 %place.1 = (bf16[208,1920]{1,0:T(8,128)(2,1)S(1)}, bf16[256,1920]{1,0:T(8,128)(2,1)S(1)}, bf16[864,1536]{1,0:T(8,128)(2,1)S(1)}, f32[96,1536]{1,0:T(8,128)S(1)}, f32[96,1536]{1,0:T(8,128)S(1)}) custom-call(bf16[208,128]{1,0:T(8,128)(2,1)S(1)} %get-tuple-element.38.first.q0, bf16[208,128]{1,0:T(8,128)(2,1)S(1)} %get-tuple-element.44.q1, ...), custom_call_target="tpu_custom_call" | custom-call | tf_op jit(solution)/shard_map/place/pallas_call | solution.py:416
  26.8 0.0 collective-permute-done.3.xp
  26.9 0.0 collective-permute-done.2.xm
  26.9 4.5 %middle.1 = (f32[128,16,128]{2,1,0:T(8,128)S(1)}, bf16[208,1920]{1,0:T(8,128)(2,1)S(1)}, bf16[96,1536]{1,0:T(8,128)(2,1)S(1)}, bf16[96,1536]{1,0:T(8,128)(2,1)S(...) custom-call(s32[2]{0:T(128)S(1)} %pad_add_fusion.own, ...), custom_call_target="tpu_custom_call" | custom-call | tf_op jit(solution)/shard_map/middle/pallas_call | solution.py:424
  31.4 4.9 %collective-permute-start.4 = (f32[128,16,128]{2,1,0:T(8,128)S(1)}, f32[128,16,128]{2,1,0:T(8,128)S(1)}, u32[]{:S(2)}, u32[]{:S(2)}) collective-permute-start(f32[128,16,128]{2,1,0:T(8,128)S(1)} %get-tuple-element.57), channel_id=1, source_target_pairs={{0,1},{1,0},{2,3},{3,2},{4,5},{5,4},{6,7},{7,6},{8,9},{9,8},{10,11... | collective-permute-start | bytes 3145736 | tf_op jit(solution)/shard_map/pair/ppermute | solution.py:381
  36.2 2.0 %keep.1 = f32[128,16,128]{2,1,0:T(8,128)S(1)} custom-call(s32[2]{0:T(128)S(1)} %pad_add_fusion.own, bf16[2,96,1536]{2,1,0:T(8,128)(2,1)S(1)} %get-tuple-element.55.inner, bf16[2,864,1536]{2,1,0:T(8,128)(2,1)S(1)} %get-tuple-element.56.columns), custom_call_target="tpu_custom_call" | custom-call | tf_op jit(solution)/shard_map/keep/pallas_call | solution.py:441
  38.2 0.3 collective-permute-done.4.other
  38.5 0.4 pair.1
  38.9 19.9 %all_to_all.15.coded = s16[32,5,16,128]{3,2,1,0:T(8,128)(2,1)S(1)} all-to-all(s16[32,5,16,128]{3,2,1,0:T(8,128)(2,1)S(1)} %pair.1), channel_id=1, replica_groups=mesh['zh'=8,'zl'=2,'y'=4,'x'=4,'core'=2] {'zl','y','x'}, dimensions={0} | all-to-all | bytes 1310720 | tf_op jit(solution)/shard_map/sum/all_to_all | solution.py:448
  58.8 0.9 sum.1.after
  59.6 11.8 %all-to-all-start.1 = ((bf16[8,4,16,128]{3,2,1,0:T(8,128)(2,1)}), bf16[8,4,16,128]{3,2,1,0:T(8,128)(2,1)S(1)}, u32[]{:S(2)}, u32[]{:S(2)}) async-start(bf16[8,4,16,128]{3,2,1,0:T(8,128)(2,1)} %sum.1.after), calls=%async_computation.1 | async-start | bytes 262144 | tf_op jit(solution)/shard_map/sum/all_to_all | solution.py:450
  71.4 2.0 %late_weights.1 = (bf16[288,864]{1,0:T(8,128)(2,1)S(1)}, bf16[288,864]{1,0:T(8,128)(2,1)S(1)}) custom-call(bf16[8,4,16,128]{3,2,1,0:T(8,128)(2,1)} %sum.1.after, bf16[96,2592]{1,0:T(8,128)(2,1)} %first_in.3, bf16[96,2592]{1,0:T(8,128)(2,1)} %second_in.3), custom_call_target="tpu_custom_call" | custom-call | tf_op jit(solution)/shard_map/late_weights/pallas_call | solution.py:452
  73.5 3.8 %outputs.1 = (bf16[1,96,512]{2,1,0:T(8,128)(2,1)}, bf16[1,96,512]{2,1,0:T(8,128)(2,1)}, f32[8,128]{1,0:T(8,128)S(1)}) custom-call(bf16[8,4,16,128]{3,2,1,0:T(8,128)(2,1)} %sum.1.after, bf16[208,1920]{1,0:T(8,128)(2,1)S(1)} %get-tuple-element.58.padded, bf16[96,1536]{1,0:T(8,128)(2,1)S(1)} %get-tuple-element.59.hidden, ...), custom_call_target="tpu_custom_call" | custom-call | tf_op jit(solution)/shard_map/outputs/pallas_call | solution.py:456
  77.3 8.1 %all-to-all-done.1.refs_0_ = bf16[8,4,16,128]{3,2,1,0:T(8,128)(2,1)S(1)} async-done(((bf16[8,4,16,128]{3,2,1,0:T(8,128)(2,1)}), bf16[8,4,16,128]{3,2,1,0:T(8,128)(2,1)S(1)}, u32[]{:S(2)}, u32[]{:S(2)}) %all-to-all-start.1) | async-done | bytes 131104 | tf_op jit(solution)/shard_map/sum/all_to_all | solution.py:450
  85.4 0.1 shares.1
  85.5 14.1 %all_to_all.16 = bf16[32,4,16,128]{3,2,1,0:T(8,128)(2,1)S(1)} all-to-all(bf16[32,4,16,128]{3,2,1,0:T(8,128)(2,1)S(1)} %shares.1), channel_id=1, replica_groups=mesh['zh'=8,'zl'=2,'y'=4,'x'=4,'core'=2] {'zl','y','x'}, dimensions={0} | all-to-all | bytes 1048576 | tf_op jit(solution)/shard_map/shares/all_to_all | solution.py:466
  99.5 5.7 %collective-permute-start.5 = (bf16[128,16,128]{2,1,0:T(8,128)(2,1)S(1)}, bf16[128,16,128]{2,1,0:T(8,128)(2,1)S(1)}, u32[]{:S(2)}, u32[]{:S(2)}) collective-permute-start(bf16[128,16,128]{2,1,0:T(8,128)(2,1)S(1)} %bitcast.3), channel_id=1, source_target_pairs={{0,1},{1,0},{2,3},{3,2},{4,5},{5,4},{6,7},{7,6},{8,9},{9,8},{10,11... | collective-permute-start | bytes 1572872 | tf_op jit(solution)/shard_map/shares/ppermute | solution.py:381
  105.2 1.6 %mine.1 = (f32[96,2592]{1,0:T(8,128)}, f32[96,2592]{1,0:T(8,128)}) custom-call(s32[2]{0:T(128)S(1)} %pad_add_fusion.own, bf16[128,16,128]{2,1,0:T(8,128)(2,1)S(1)} %bitcast.4), custom_call_target="tpu_custom_call" | custom-call | tf_op jit(solution)/shard_map/mine/pallas_call | solution.py:470
  106.8 1.6 %other.1 = (f32[96,2592]{1,0:T(8,128)}, f32[96,2592]{1,0:T(8,128)}) custom-call(s32[2]{0:T(128)S(1)} %pad_add_fusion.own, bf16[128,16,128]{2,1,0:T(8,128)(2,1)S(1)} %collective-permute-done.5.half, f32[96,2592]{1,0:T(8,128)} %get-tuple-element.66.first_in, f32[96,2592]{1,0:T(8,128)} %get-tuple-element.67.second_in), custom_call_target="tpu_custom_call", output_to_operand_aliasing={{0}: (2, {}), {1}: (3, {})} | custom-call | tf_op jit(solution)/shard_map/other/pallas_call | solution.py:472
  (3 shorter events, 0.0 us)
Async XLA Ops:
  0.6 0.7 copy-start
  2.5 8.8 %collective-permute-start = (bf16[208,128]{1,0:T(8,128)(2,1)S(1)}, bf16[208,128]{1,0:T(8,128)(2,1)S(1)}, u32[]{:S(2)}, u32[]{:S(2)}) collective-permute-start(bf16[208,128]{1,0:T(8,128)(2,1)S(1)} %get-tuple-element.40), channel_id=1, source_target_pairs={{0,64},{8,72},{16,80},{24,88},{32,96},{40,104},{48,112},{56,120},{... | collective-permute-start | bytes 159752 | tf_op jit(solution)/shard_map/rims_y/ppermute | solution.py:377
  8.2 7.6 %collective-permute-start.1 = (bf16[208,128]{1,0:T(8,128)(2,1)S(1)}, bf16[208,128]{1,0:T(8,128)(2,1)S(1)}, u32[]{:S(2)}, u32[]{:S(2)}) collective-permute-start(bf16[208,128]{1,0:T(8,128)(2,1)S(1)} %get-tuple-element.41), channel_id=1, source_target_pairs={{64,0},{72,8},{80,16},{88,24},{96,32},{104,40},{112,48},{120,56},{... | collective-permute-start | bytes 159752 | tf_op jit(solution)/shard_map/rims_y/ppermute | solution.py:377
  9.6 0.7 copy-start.1
  16.0 10.9 %collective-permute-start.3 = (bf16[208,256]{1,0:T(8,128)(2,1)S(1)}, bf16[208,256]{1,0:T(8,128)(2,1)S(1)}, u32[]{:S(2)}, u32[]{:S(2)}) collective-permute-start(bf16[208,256]{1,0:T(8,128)(2,1)S(1)} %get-tuple-element.43), channel_id=1, source_target_pairs={{8,0},{16,8},{24,16},{32,24},{40,32},{48,40},{56,48},{72,64},{80,7... | collective-permute-start | bytes 319496 | tf_op jit(solution)/shard_map/rims_x/ppermute | solution.py:377
  17.3 9.6 %collective-permute-start.2 = (bf16[208,256]{1,0:T(8,128)(2,1)S(1)}, bf16[208,256]{1,0:T(8,128)(2,1)S(1)}, u32[]{:S(2)}, u32[]{:S(2)}) collective-permute-start(bf16[208,256]{1,0:T(8,128)(2,1)S(1)} %get-tuple-element.42.after), channel_id=1, source_target_pairs={{0,8},{8,16},{16,24},{24,32},{32,40},{40,48},{48,56},{64,72},{72,8... | collective-permute-start | bytes 319496 | tf_op jit(solution)/shard_map/rims_x/ppermute | solution.py:377
  31.4 7.1 %collective-permute-start.4 = (f32[128,16,128]{2,1,0:T(8,128)S(1)}, f32[128,16,128]{2,1,0:T(8,128)S(1)}, u32[]{:S(2)}, u32[]{:S(2)}) collective-permute-start(f32[128,16,128]{2,1,0:T(8,128)S(1)} %get-tuple-element.57), channel_id=1, source_target_pairs={{0,1},{1,0},{2,3},{3,2},{4,5},{5,4},{6,7},{7,6},{8,9},{9,8},{10,11... | collective-permute-start | bytes 3145736 | tf_op jit(solution)/shard_map/pair/ppermute | solution.py:381
  59.6 25.7 %all-to-all-start.1 = ((bf16[8,4,16,128]{3,2,1,0:T(8,128)(2,1)}), bf16[8,4,16,128]{3,2,1,0:T(8,128)(2,1)S(1)}, u32[]{:S(2)}, u32[]{:S(2)}) async-start(bf16[8,4,16,128]{3,2,1,0:T(8,128)(2,1)} %sum.1.after), calls=%async_computation.1 | async-start | bytes 262144 | tf_op jit(solution)/shard_map/sum/all_to_all | solution.py:450
  99.5 7.3 %collective-permute-start.5 = (bf16[128,16,128]{2,1,0:T(8,128)(2,1)S(1)}, bf16[128,16,128]{2,1,0:T(8,128)(2,1)S(1)}, u32[]{:S(2)}, u32[]{:S(2)}) collective-permute-start(bf16[128,16,128]{2,1,0:T(8,128)(2,1)S(1)} %bitcast.3), channel_id=1, source_target_pairs={{0,1},{1,0},{2,3},{3,2},{4,5},{5,4},{6,7},{7,6},{8,9},{9,8},{10,11... | collective-permute-start | bytes 1572872 | tf_op jit(solution)/shard_map/shares/ppermute | solution.py:381

commit v10 on v6

--- a/solution.py
+++ b/solution.py
@@ -421,7 +421,7 @@
         (coded,) = call(pair_kernel, [((32, 5, 16, 128), jnp.int16)], [VMEM] * 2)(
             keep, swap_halves(send)
         )
-    near, far = ("zl", "y", "x"), "zh"
+    near, far = ("x", "y", "zl"), "zh"
     with jax.named_scope("sum"):
         parts = lax.all_to_all(coded, near, 0, 0)
         (copies,) = call(decode_kernel, [((8, 4, 16, 128), BF16)], [VMEM])(parts)

time: 108 us -> 109 us (level)
  waiting for transfers between devices: 14.4 us -> 13.2 us
    all_to_all x1, blocking collectives: 19.3 us -> 21 us  [body(): parts = lax.all_to_all(coded, near, 0, 0)]
    all_to_all x1, waiting for transfers between devices: 8.13 us -> 7.01 us  [body(): parts = lax.all_to_all(copies, far, 0, 0)]
where the time goes in v10:
time: 109 us; the launch traced here: 108 us
  starting transfers between devices  35.3 us (32%)
  blocking collectives  34.4 us (32%)
  Pallas kernels  22.9 us (21%)
  waiting for transfers between devices  13.2 us (12%)
  local copies, waits for them, and re-layouts  1.33 us (1%)
    all_to_all x1, blocking collectives, body(): parts = lax.all_to_all(coded, near, 0, 0)  21 us
    all_to_all x1, blocking collectives, body(): mine = lax.all_to_all(copies, near, 0, 0).reshape(128, 16, 128)  13.5 us
    ppermute x2, starting transfers between devices, swap_halves(): return lax.ppermute(value, 'core', [(0, 1), (1, 0)])  12.4 us
    ppermute x4, starting transfers between devices, from_owner(): return lax.ppermute(value, ('zh', 'zl', 'y'), pairs)  11.5 us
    all_to_all x1, starting transfers between devices, body(): parts = lax.all_to_all(copies, far, 0, 0)  11.4 us
    all_to_all x1, waiting for transfers between devices, body(): parts = lax.all_to_all(copies, far, 0, 0)  7.01 us
    ppermute x4, waiting for transfers between devices, from_owner(): return lax.ppermute(value, ('zh', 'zl', 'y'), pairs)  5.93 us
    pallas_call x1, Pallas kernels, body(): call(main_kernel, [half, ((ROWS, LANES), BF16), outer, outer, ((2, C, OUT...  5.54 us
  transfers between devices with their start and end apart: 7, of which 4 were waited for; matrix products, arithmetic and copies ran while one was open for 0% of the time, Pallas kernels for 12%

profile of v10, /device:TPU:1, one launch (start us, length us, event | category | flops | bytes accessed | tf_op | source)
XLA Modules:
  0.0 108.2 jit_solution(15432214328316865531)
XLA Ops:
  0.6 0.7 copy-done
  1.3 1.2 %pack.1 = (bf16[208,128]{1,0:T(8,128)(2,1)S(1)}, bf16[208,128]{1,0:T(8,128)(2,1)S(1)}, bf16[208,128]{1,0:T(8,128)(2,1)S(1)}, bf16[208,128]{1,0:T(8,128)(2,1)S(1)...) custom-call(bf16[1,96,512]{2,1,0:T(8,128)(2,1)} %feats_in.1, bf16[1,96,512]{2,1,0:T(8,128)(2,1)} %cot_in.1, ...), custom_call_target="tpu_custom_call" | custom-call | tf_op jit(solution)/shard_map/pack/pallas_call | solution.py:379
  2.5 5.7 %collective-permute-start = (bf16[208,128]{1,0:T(8,128)(2,1)S(1)}, bf16[208,128]{1,0:T(8,128)(2,1)S(1)}, u32[]{:S(2)}, u32[]{:S(2)}) collective-permute-start(bf16[208,128]{1,0:T(8,128)(2,1)S(1)} %get-tuple-element.37), channel_id=1, source_target_pairs={{0,64},{8,72},{16,80},{24,88},{32,96},{40,104},{48,112},{56,120},{... | collective-permute-start | bytes 159752 | tf_op jit(solution)/shard_map/rims_y/ppermute | solution.py:363
  8.2 1.3 %collective-permute-start.1 = (bf16[208,128]{1,0:T(8,128)(2,1)S(1)}, bf16[208,128]{1,0:T(8,128)(2,1)S(1)}, u32[]{:S(2)}, u32[]{:S(2)}) collective-permute-start(bf16[208,128]{1,0:T(8,128)(2,1)S(1)} %get-tuple-element.38), channel_id=1, source_target_pairs={{64,0},{72,8},{80,16},{88,24},{96,32},{104,40},{112,48},{120,56},{... | collective-permute-start | bytes 159752 | tf_op jit(solution)/shard_map/rims_y/ppermute | solution.py:363
  9.5 0.1 pad_add_fusion.own
  9.6 0.7 copy-done.1
  10.3 2.4 %prepare.1 = (bf16[288,864]{1,0:T(8,128)(2,1)S(1)}, bf16[288,864]{1,0:T(8,128)(2,1)S(1)}, s32[8,1920]{1,0:T(8,128)S(1)}, bf16[16,128]{1,0:T(8,128)(2,1)S(1)}, bf16[16,256]{1,0:T(8,128)(2,1)S(1)}) custom-call(s32[1,27]{1,0:T(1,128)S(1)} %copy-done.1, s32[2]{0:T(128)S(1)} %pad_add_fusion.own, bf16[96,2592]{1,0:T(8,128)(2,1)} %first_in.3, ...), custom_call_target="tpu_custom_call" | custom-call | tf_op jit(solution)/shard_map/prepare/pallas_call | solution.py:383
  12.7 0.0 collective-permute-done.ym
  12.7 3.1 %collective-permute-done.1.yp = bf16[208,128]{1,0:T(8,128)(2,1)S(1)} collective-permute-done((bf16[208,128]{1,0:T(8,128)(2,1)S(1)}, bf16[208,128]{1,0:T(8,128)(2,1)S(1)}, u32[]{:S(2)}, u32[]{:S(2)}) %collective-permute-start.1) | collective-permute-done | bytes 53280 | tf_op jit(solution)/shard_map/rims_y/ppermute | solution.py:363
  15.9 0.1 slabs.1
  16.0 3.2 %collective-permute-start.2 = (bf16[208,256]{1,0:T(8,128)(2,1)S(1)}, bf16[208,256]{1,0:T(8,128)(2,1)S(1)}, u32[]{:S(2)}, u32[]{:S(2)}) collective-permute-start(bf16[208,256]{1,0:T(8,128)(2,1)S(1)} %get-tuple-element.39), channel_id=1, source_target_pairs={{0,8},{8,16},{16,24},{24,32},{32,40},{40,48},{48,56},{64,72},{72,8... | collective-permute-start | bytes 319496 | tf_op jit(solution)/shard_map/rims_x/ppermute | solution.py:363
  19.2 1.3 %collective-permute-start.3 = (bf16[208,256]{1,0:T(8,128)(2,1)S(1)}, bf16[208,256]{1,0:T(8,128)(2,1)S(1)}, u32[]{:S(2)}, u32[]{:S(2)}) collective-permute-start(bf16[208,256]{1,0:T(8,128)(2,1)S(1)} %get-tuple-element.40), channel_id=1, source_target_pairs={{8,0},{16,8},{24,16},{32,24},{40,32},{48,40},{56,48},{72,64},{80,7... | collective-permute-start | bytes 319496 | tf_op jit(solution)/shard_map/rims_x/ppermute | solution.py:363
  20.5 1.3 %place.1 = (bf16[208,1920]{1,0:T(8,128)(2,1)S(1)}, bf16[256,1920]{1,0:T(8,128)(2,1)S(1)}) custom-call(bf16[208,128]{1,0:T(8,128)(2,1)S(1)} %get-tuple-element.35.first.q0, bf16[208,128]{1,0:T(8,128)(2,1)S(1)} %get-tuple-element.41.q1, bf16[208,128]{1,0:T(8,128)(2,1)S(1)} %get-tuple-element.42.q2, bf16[208,128]{1,0:T(8,128)(2,1)S(1)} %get-tuple-element.36.last.q3, ...), custom_call_target="tpu_custom_call" | custom-call | tf_op jit(solution)/shard_map/place/pallas_call | solution.py:400
  21.8 0.0 collective-permute-done.2.xm
  21.9 2.8 %collective-permute-done.3.xp = bf16[208,256]{1,0:T(8,128)(2,1)S(1)} collective-permute-done((bf16[208,256]{1,0:T(8,128)(2,1)S(1)}, bf16[208,256]{1,0:T(8,128)(2,1)S(1)}, u32[]{:S(2)}, u32[]{:S(2)}) %collective-permute-start.3) | collective-permute-done | bytes 106528 | tf_op jit(solution)/shard_map/rims_x/ppermute | solution.py:363
  24.6 5.5 %middle.1 = (f32[128,16,128]{2,1,0:T(8,128)S(1)}, bf16[208,1920]{1,0:T(8,128)(2,1)S(1)}, bf16[96,1536]{1,0:T(8,128)(2,1)S(1)}, bf16[96,1536]{1,0:T(8,128)(2,1)S(...) custom-call(s32[2]{0:T(128)S(1)} %pad_add_fusion.own, ...), custom_call_target="tpu_custom_call" | custom-call | tf_op jit(solution)/shard_map/middle/pallas_call | solution.py:409
  30.2 5.7 %collective-permute-start.4 = (f32[128,16,128]{2,1,0:T(8,128)S(1)}, f32[128,16,128]{2,1,0:T(8,128)S(1)}, u32[]{:S(2)}, u32[]{:S(2)}) collective-permute-start(f32[128,16,128]{2,1,0:T(8,128)S(1)} %get-tuple-element.51), channel_id=1, source_target_pairs={{0,1},{1,0},{2,3},{3,2},{4,5},{5,4},{6,7},{7,6},{8,9},{9,8},{10,11... | collective-permute-start | bytes 3145736 | tf_op jit(solution)/shard_map/pair/ppermute | solution.py:367
  35.9 2.0 %keep.1 = f32[128,16,128]{2,1,0:T(8,128)S(1)} custom-call(s32[2]{0:T(128)S(1)} %pad_add_fusion.own, bf16[2,96,1536]{2,1,0:T(8,128)(2,1)S(1)} %get-tuple-element.49.inner, bf16[2,864,1536]{2,1,0:T(8,128)(2,1)S(1)} %get-tuple-element.50.columns), custom_call_target="tpu_custom_call" | custom-call | tf_op jit(solution)/shard_map/keep/pallas_call | solution.py:419
  37.9 0.3 collective-permute-done.4.other
  38.2 0.4 pair.1
  38.6 21.0 %all_to_all.15.coded = s16[32,5,16,128]{3,2,1,0:T(8,128)(2,1)S(1)} all-to-all(s16[32,5,16,128]{3,2,1,0:T(8,128)(2,1)S(1)} %pair.1), channel_id=1, replica_groups=mesh['zh'=8,'zl'=2,'y'=4,'x'=4,'core'=2] {'x','y','zl'}, dimensions={0} | all-to-all | bytes 1310720 | tf_op jit(solution)/shard_map/sum/all_to_all | solution.py:426
  59.6 0.9 sum.1.after
  60.4 11.4 %all-to-all-start.1 = ((bf16[8,4,16,128]{3,2,1,0:T(8,128)(2,1)}), bf16[8,4,16,128]{3,2,1,0:T(8,128)(2,1)S(1)}, u32[]{:S(2)}, u32[]{:S(2)}) async-start(bf16[8,4,16,128]{3,2,1,0:T(8,128)(2,1)} %sum.1.after), calls=%async_computation.1 | async-start | bytes 262144 | tf_op jit(solution)/shard_map/sum/all_to_all | solution.py:428
  71.8 2.0 %late_weights.1 = (bf16[288,864]{1,0:T(8,128)(2,1)S(1)}, bf16[288,864]{1,0:T(8,128)(2,1)S(1)}) custom-call(bf16[8,4,16,128]{3,2,1,0:T(8,128)(2,1)} %sum.1.after, bf16[96,2592]{1,0:T(8,128)(2,1)} %first_in.3, bf16[96,2592]{1,0:T(8,128)(2,1)} %second_in.3), custom_call_target="tpu_custom_call" | custom-call | tf_op jit(solution)/shard_map/late_weights/pallas_call | solution.py:430
  73.9 3.8 %outputs.1 = (bf16[1,96,512]{2,1,0:T(8,128)(2,1)}, bf16[1,96,512]{2,1,0:T(8,128)(2,1)}, f32[8,128]{1,0:T(8,128)S(1)}) custom-call(bf16[8,4,16,128]{3,2,1,0:T(8,128)(2,1)} %sum.1.after, bf16[208,1920]{1,0:T(8,128)(2,1)S(1)} %get-tuple-element.52.padded, bf16[96,1536]{1,0:T(8,128)(2,1)S(1)} %get-tuple-element.53.hidden, ...), custom_call_target="tpu_custom_call" | custom-call | tf_op jit(solution)/shard_map/outputs/pallas_call | solution.py:434
  77.7 7.0 %all-to-all-done.1.refs_0_ = bf16[8,4,16,128]{3,2,1,0:T(8,128)(2,1)S(1)} async-done(((bf16[8,4,16,128]{3,2,1,0:T(8,128)(2,1)}), bf16[8,4,16,128]{3,2,1,0:T(8,128)(2,1)S(1)}, u32[]{:S(2)}, u32[]{:S(2)}) %all-to-all-start.1) | async-done | bytes 131104 | tf_op jit(solution)/shard_map/sum/all_to_all | solution.py:428
  84.7 0.1 shares.1
  84.7 13.5 %all_to_all.16 = bf16[32,4,16,128]{3,2,1,0:T(8,128)(2,1)S(1)} all-to-all(bf16[32,4,16,128]{3,2,1,0:T(8,128)(2,1)S(1)} %shares.1), channel_id=1, replica_groups=mesh['zh'=8,'zl'=2,'y'=4,'x'=4,'core'=2] {'x','y','zl'}, dimensions={0} | all-to-all | bytes 1048576 | tf_op jit(solution)/shard_map/shares/all_to_all | solution.py:444
  98.2 6.6 %collective-permute-start.5 = (bf16[128,16,128]{2,1,0:T(8,128)(2,1)S(1)}, bf16[128,16,128]{2,1,0:T(8,128)(2,1)S(1)}, u32[]{:S(2)}, u32[]{:S(2)}) collective-permute-start(bf16[128,16,128]{2,1,0:T(8,128)(2,1)S(1)} %bitcast.3), channel_id=1, source_target_pairs={{0,1},{1,0},{2,3},{3,2},{4,5},{5,4},{6,7},{7,6},{8,9},{9,8},{10,11... | collective-permute-start | bytes 1572872 | tf_op jit(solution)/shard_map/shares/ppermute | solution.py:367
  104.8 1.6 %mine.1 = (f32[96,2592]{1,0:T(8,128)}, f32[96,2592]{1,0:T(8,128)}) custom-call(s32[2]{0:T(128)S(1)} %pad_add_fusion.own, bf16[128,16,128]{2,1,0:T(8,128)(2,1)S(1)} %bitcast.4), custom_call_target="tpu_custom_call" | custom-call | tf_op jit(solution)/shard_map/mine/pallas_call | solution.py:448
  106.4 0.0 collective-permute-done.5.half
  106.4 1.6 %other.1 = (f32[96,2592]{1,0:T(8,128)}, f32[96,2592]{1,0:T(8,128)}) custom-call(s32[2]{0:T(128)S(1)} %pad_add_fusion.own, bf16[128,16,128]{2,1,0:T(8,128)(2,1)S(1)} %collective-permute-done.5.half, f32[96,2592]{1,0:T(8,128)} %get-tuple-element.60.first_in, f32[96,2592]{1,0:T(8,128)} %get-tuple-element.61.second_in), custom_call_target="tpu_custom_call", output_to_operand_aliasing={{0}: (2, {}), {1}: (3, {})} | custom-call | tf_op jit(solution)/shard_map/other/pallas_call | solution.py:450
  (2 shorter events, 0.0 us)
Async XLA Ops:
  0.6 0.7 copy-start
  2.5 10.2 %collective-permute-start = (bf16[208,128]{1,0:T(8,128)(2,1)S(1)}, bf16[208,128]{1,0:T(8,128)(2,1)S(1)}, u32[]{:S(2)}, u32[]{:S(2)}) collective-permute-start(bf16[208,128]{1,0:T(8,128)(2,1)S(1)} %get-tuple-element.37), channel_id=1, source_target_pairs={{0,64},{8,72},{16,80},{24,88},{32,96},{40,104},{48,112},{56,120},{... | collective-permute-start | bytes 159752 | tf_op jit(solution)/shard_map/rims_y/ppermute | solution.py:363
  8.2 7.6 %collective-permute-start.1 = (bf16[208,128]{1,0:T(8,128)(2,1)S(1)}, bf16[208,128]{1,0:T(8,128)(2,1)S(1)}, u32[]{:S(2)}, u32[]{:S(2)}) collective-permute-start(bf16[208,128]{1,0:T(8,128)(2,1)S(1)} %get-tuple-element.38), channel_id=1, source_target_pairs={{64,0},{72,8},{80,16},{88,24},{96,32},{104,40},{112,48},{120,56},{... | collective-permute-start | bytes 159752 | tf_op jit(solution)/shard_map/rims_y/ppermute | solution.py:363
  9.6 0.7 copy-start.1
  16.0 5.9 %collective-permute-start.2 = (bf16[208,256]{1,0:T(8,128)(2,1)S(1)}, bf16[208,256]{1,0:T(8,128)(2,1)S(1)}, u32[]{:S(2)}, u32[]{:S(2)}) collective-permute-start(bf16[208,256]{1,0:T(8,128)(2,1)S(1)} %get-tuple-element.39), channel_id=1, source_target_pairs={{0,8},{8,16},{16,24},{24,32},{32,40},{40,48},{48,56},{64,72},{72,8... | collective-permute-start | bytes 319496 | tf_op jit(solution)/shard_map/rims_x/ppermute | solution.py:363
  19.2 5.4 %collective-permute-start.3 = (bf16[208,256]{1,0:T(8,128)(2,1)S(1)}, bf16[208,256]{1,0:T(8,128)(2,1)S(1)}, u32[]{:S(2)}, u32[]{:S(2)}) collective-permute-start(bf16[208,256]{1,0:T(8,128)(2,1)S(1)} %get-tuple-element.40), channel_id=1, source_target_pairs={{8,0},{16,8},{24,16},{32,24},{40,32},{48,40},{56,48},{72,64},{80,7... | collective-permute-start | bytes 319496 | tf_op jit(solution)/shard_map/rims_x/ppermute | solution.py:363
  30.2 8.0 %collective-permute-start.4 = (f32[128,16,128]{2,1,0:T(8,128)S(1)}, f32[128,16,128]{2,1,0:T(8,128)S(1)}, u32[]{:S(2)}, u32[]{:S(2)}) collective-permute-start(f32[128,16,128]{2,1,0:T(8,128)S(1)} %get-tuple-element.51), channel_id=1, source_target_pairs={{0,1},{1,0},{2,3},{3,2},{4,5},{5,4},{6,7},{7,6},{8,9},{9,8},{10,11... | collective-permute-start | bytes 3145736 | tf_op jit(solution)/shard_map/pair/ppermute | solution.py:367
  60.4 24.2 %all-to-all-start.1 = ((bf16[8,4,16,128]{3,2,1,0:T(8,128)(2,1)}), bf16[8,4,16,128]{3,2,1,0:T(8,128)(2,1)S(1)}, u32[]{:S(2)}, u32[]{:S(2)}) async-start(bf16[8,4,16,128]{3,2,1,0:T(8,128)(2,1)} %sum.1.after), calls=%async_computation.1 | async-start | bytes 262144 | tf_op jit(solution)/shard_map/sum/all_to_all | solution.py:428
  98.2 8.2 %collective-permute-start.5 = (bf16[128,16,128]{2,1,0:T(8,128)(2,1)S(1)}, bf16[128,16,128]{2,1,0:T(8,128)(2,1)S(1)}, u32[]{:S(2)}, u32[]{:S(2)}) collective-permute-start(bf16[128,16,128]{2,1,0:T(8,128)(2,1)S(1)} %bitcast.3), channel_id=1, source_target_pairs={{0,1},{1,0},{2,3},{3,2},{4,5},{5,4},{6,7},{7,6},{8,9},{9,8},{10,11... | collective-permute-start | bytes 1572872 | tf_op jit(solution)/shard_map/shares/ppermute | solution.py:367
